TPU v7x, 256 devices: a whole 4x4x8 slice. The times are simulated.
256 devices in a mesh: frame: 64 (over x, z, core), head: 4 (over y).
Axes of the slice: x: 4, y: 4, z: 8, core: 2. Of those that a mesh axis runs over, the one named last changes fastest.
Arguments:
- queries: bfloat16 [16384, 1536], P(('frame', 'head')), may hold values from -40 to 40
- keys: bfloat16 [16384, 1536], P(('frame', 'head')), may hold values from -20 to 20
- values: bfloat16 [16384, 1536], P(('frame', 'head')), may hold values from -6 to 6
- band_width: int32 [64, 64], P('frame'), may hold values from 2 to 256, as said below
Outputs:
- attended: bfloat16 [16384, 1536], P(('frame', 'head'))
Inputs may be any that keep to these rules, and one draw needn't show every extreme that they name: band_width[f, g] equals 256 where g == f; otherwise it lies between half of and all of 256 >> k, where k is the bit length of |f - g|.
All inputs are finite; a program needn't handle non-finite values.
Results may differ from a plain program's by a relative error of at most 0.0049.
Values may be sent and summed in bfloat16 or wider, within the bound.
No kernel may reach another device: no remote copies, remote signals or barrier semaphores. Data moves between devices by JAX's collectives and lax.ppermute only.
A program may use at most 64 MiB of HBM per device.

v0:
```python
import jax
import jax.numpy as jnp
from jax import lax
from jax.sharding import PartitionSpec as P

HEAD_DIM = 128
BLK = 128


def shifted(block, axis, distance):
    devices = range(lax.axis_size(axis))
    route = [(i - distance, i) for i in devices if i - distance in devices]
    return lax.ppermute(block, axis, route)


def distance_list(frame_count):
    distances = [1, 2, 3]
    distance = 4
    while distance < frame_count:
        distances.append(distance)
        distance = distance * 2
    return distances


def window_of(distance, tokens, block):
    if distance == 0:
        return (tokens, 0)
    reach_width = tokens >> distance.bit_length()
    half_block = block // 2
    margin = -(-reach_width // half_block) * half_block
    return (min(tokens, block + 2 * margin), margin)


def shards(queries, keys, values, band_width):
    query_loc, key_loc, value_loc = (
        lax.all_to_all(queries, "head", split_axis=1, concat_axis=0, tiled=True),
        lax.all_to_all(keys, "head", split_axis=1, concat_axis=0, tiled=True),
        lax.all_to_all(values, "head", split_axis=1, concat_axis=0, tiled=True),
    )
    tokens_frame = query_loc.shape[0]
    heads_here = query_loc.shape[1] // HEAD_DIM
    frame_count = lax.axis_size("frame")
    current = lax.axis_index("frame")
    distances = distance_list(frame_count)
    sources = [(0, (key_loc, value_loc))]
    for distance in distances:
        earlier = shifted((key_loc, value_loc), "frame", distance)
        later = shifted((key_loc, value_loc), "frame", -distance)
        sources = sources + [(-distance, earlier), (distance, later)]
    band_row = band_width[0]
    position = jnp.arange(tokens_frame, dtype=jnp.int32)
    query_heads = query_loc.reshape(tokens_frame, heads_here, HEAD_DIM)
    prepared = []
    for offset, pair in sources:
        target = current + offset
        inside = (target >= 0) & (target < frame_count)
        clipped = jnp.clip(target, 0, frame_count - 1)
        band_here = lax.dynamic_index_in_dim(band_row, clipped, 0, keepdims=False)
        window_len, margin = window_of(abs(offset), tokens_frame, BLK)
        key_heads = pair[0].reshape(tokens_frame, heads_here, HEAD_DIM)
        value_heads = pair[1].reshape(tokens_frame, heads_here, HEAD_DIM)
        prepared.append((key_heads, value_heads, inside, band_here, window_len, margin))
    score_scale = HEAD_DIM ** (-0.5)
    outputs = []
    for block_start in range(0, tokens_frame, BLK):
        key_parts = []
        value_parts = []
        mask_parts = []
        for key_heads, value_heads, inside, band_here, window_len, margin in prepared:
            start = min(max(block_start - margin, 0), tokens_frame - window_len)
            key_parts.append(key_heads)
            value_parts.append(value_heads)
            spacing = jnp.abs(
                position[block_start : block_start + BLK, None]
                - position[None, start : start + window_len]
            )
            mask_parts.append(inside & (spacing <= band_here))
        key_all = jnp.concatenate(key_parts, axis=0)
        value_all = jnp.concatenate(value_parts, axis=0)
        mask_all = jnp.concatenate(mask_parts, axis=1)
        scores = (
            jnp.einsum(
                "qhd,khd->hqk",
                query_heads[block_start : block_start + BLK],
                key_all,
                preferred_element_type=jnp.float32,
            )
            * score_scale
        )
        scores = jnp.where(mask_all[None], scores, -jnp.inf)
        largest = jnp.max(scores, axis=-1, keepdims=True)
        exponent = jnp.exp(scores - largest)
        weights = (exponent / jnp.sum(exponent, axis=-1, keepdims=True)).astype(jnp.bfloat16)
        result = jnp.einsum("hqk,khd->qhd", weights, value_all, preferred_element_type=jnp.float32)
        outputs.append(result.astype(jnp.bfloat16).reshape(BLK, heads_here * HEAD_DIM))
    combined = jnp.concatenate(outputs, axis=0)
    return lax.all_to_all(combined, "head", split_axis=0, concat_axis=1, tiled=True)


def solution(mesh):
    placed = (
        P(("frame", "head"), None),
        P(("frame", "head"), None),
        P(("frame", "head"), None),
        P("frame", None),
    )
    return jax.shard_map(
        shards, mesh=mesh, in_specs=placed, out_specs=P(("frame", "head"), None), check_vma=False
    )
```

profile of v0, /device:TPU:36, one launch (start us, length us, event | category | flops | bytes accessed | tf_op | source)
XLA Modules:
  0.0 244.5 jit_solution(16049134115112876589)
XLA Ops:
  1.6 4.5 %all-to-all-start = ((bf16[64,4,384]{2,0,1:T(8,128)(2,1)}), bf16[64,4,384]{2,0,1:T(8,128)(2,1)S(1)}, u32[]{:S(2)}, u32[]{:S(2)}) async-start(bf16[64,4,384]{2,0,1:T(8,128)(2,1)} %bitcast.105), calls=%async_computation | async-start | bytes 393216 | tf_op jit(solution)/shard_map/all_to_all | solution.py:38
  29.0 4.8 %all-to-all-start.1 = ((bf16[64,4,384]{2,0,1:T(8,128)(2,1)}), bf16[64,4,384]{2,0,1:T(8,128)(2,1)S(1)}, u32[]{:S(2)}, u32[]{:S(2)}) async-start(bf16[64,4,384]{2,0,1:T(8,128)(2,1)} %bitcast.104), calls=%async_computation.1 | async-start | bytes 393216 | tf_op jit(solution)/shard_map/all_to_all | solution.py:37
  36.5 3.6 %collective-permute-start.1 = (bf16[256,384]{1,0:T(8,128)(2,1)S(1)}, bf16[256,384]{1,0:T(8,128)(2,1)S(1)}, u32[]{:S(2)}, u32[]{:S(2)}) collective-permute-start(bf16[256,384]{1,0:T(8,128)(2,1)S(1)} %bitcast.107), channel_id=1, source_target_pairs={{4,0},{8,4},{12,8},{16,12},{20,16},{24,20},{28,24},{32,28},{36,32}... | collective-permute-start | bytes 589832 | tf_op jit(solution)/shard_map/ppermute | solution.py:13
  40.1 3.8 %collective-permute-start.2 = (bf16[256,384]{1,0:T(8,128)(2,1)S(1)}, bf16[256,384]{1,0:T(8,128)(2,1)S(1)}, u32[]{:S(2)}, u32[]{:S(2)}) collective-permute-start(bf16[256,384]{1,0:T(8,128)(2,1)S(1)} %bitcast.108), channel_id=1, source_target_pairs={{0,8},{4,12},{8,16},{12,20},{16,24},{20,28},{24,32},{28,36},{32,40... | collective-permute-start | bytes 589832 | tf_op jit(solution)/shard_map/ppermute | solution.py:13
  43.9 4.8 %all-to-all-start.2 = ((bf16[64,4,384]{2,0,1:T(8,128)(2,1)}), bf16[64,4,384]{2,0,1:T(8,128)(2,1)S(1)}, u32[]{:S(2)}, u32[]{:S(2)}) async-start(bf16[64,4,384]{2,0,1:T(8,128)(2,1)} %bitcast.103), calls=%async_computation.2 | async-start | bytes 393216 | tf_op jit(solution)/shard_map/all_to_all | solution.py:36
  50.7 3.6 %collective-permute-start.15 = (bf16[256,384]{1,0:T(8,128)(2,1)S(1)}, bf16[256,384]{1,0:T(8,128)(2,1)S(1)}, u32[]{:S(2)}, u32[]{:S(2)}) collective-permute-start(bf16[256,384]{1,0:T(8,128)(2,1)S(1)} %bitcast.122), channel_id=1, source_target_pairs={{4,0},{8,4},{12,8},{16,12},{20,16},{24,20},{28,24},{32,28},{36,32}... | collective-permute-start | bytes 589832 | tf_op jit(solution)/shard_map/ppermute | solution.py:13
  54.3 3.8 %collective-permute-start.16 = (bf16[256,384]{1,0:T(8,128)(2,1)S(1)}, bf16[256,384]{1,0:T(8,128)(2,1)S(1)}, u32[]{:S(2)}, u32[]{:S(2)}) collective-permute-start(bf16[256,384]{1,0:T(8,128)(2,1)S(1)} %bitcast.123), channel_id=1, source_target_pairs={{0,8},{4,12},{8,16},{12,20},{16,24},{20,28},{24,32},{28,36},{32,40... | collective-permute-start | bytes 589832 | tf_op jit(solution)/shard_map/ppermute | solution.py:13
  59.7 2.7 %collective-permute-start.17 = (bf16[256,384]{1,0:T(8,128)(2,1)S(1)}, bf16[256,384]{1,0:T(8,128)(2,1)S(1)}, u32[]{:S(2)}, u32[]{:S(2)}) collective-permute-start(bf16[256,384]{1,0:T(8,128)(2,1)S(1)} %bitcast.124), channel_id=1, source_target_pairs={{8,0},{12,4},{16,8},{20,12},{24,16},{28,20},{32,24},{36,28},{40,32... | collective-permute-start | bytes 589832 | tf_op jit(solution)/shard_map/ppermute | solution.py:13
  62.4 4.9 %collective-permute-start.18 = (bf16[256,384]{1,0:T(8,128)(2,1)S(1)}, bf16[256,384]{1,0:T(8,128)(2,1)S(1)}, u32[]{:S(2)}, u32[]{:S(2)}) collective-permute-start(bf16[256,384]{1,0:T(8,128)(2,1)S(1)} %bitcast.125), channel_id=1, source_target_pairs={{0,12},{4,16},{8,20},{12,24},{16,28},{20,32},{24,36},{28,40},{32,4... | collective-permute-start | bytes 589832 | tf_op jit(solution)/shard_map/ppermute | solution.py:13
  67.3 3.7 %collective-permute-start.19 = (bf16[256,384]{1,0:T(8,128)(2,1)S(1)}, bf16[256,384]{1,0:T(8,128)(2,1)S(1)}, u32[]{:S(2)}, u32[]{:S(2)}) collective-permute-start(bf16[256,384]{1,0:T(8,128)(2,1)S(1)} %bitcast.126), channel_id=1, source_target_pairs={{12,0},{16,4},{20,8},{24,12},{28,16},{32,20},{36,24},{40,28},{44,3... | collective-permute-start | bytes 589832 | tf_op jit(solution)/shard_map/ppermute | solution.py:13
  71.0 4.8 %collective-permute-start.20 = (bf16[256,384]{1,0:T(8,128)(2,1)S(1)}, bf16[256,384]{1,0:T(8,128)(2,1)S(1)}, u32[]{:S(2)}, u32[]{:S(2)}) collective-permute-start(bf16[256,384]{1,0:T(8,128)(2,1)S(1)} %bitcast.127), channel_id=1, source_target_pairs={{0,16},{4,20},{8,24},{12,28},{16,32},{20,36},{24,40},{28,44},{32,4... | collective-permute-start | bytes 589832 | tf_op jit(solution)/shard_map/ppermute | solution.py:13
  75.8 4.1 %collective-permute-start.21 = (bf16[256,384]{1,0:T(8,128)(2,1)S(1)}, bf16[256,384]{1,0:T(8,128)(2,1)S(1)}, u32[]{:S(2)}, u32[]{:S(2)}) collective-permute-start(bf16[256,384]{1,0:T(8,128)(2,1)S(1)} %bitcast.128), channel_id=1, source_target_pairs={{16,0},{20,4},{24,8},{28,12},{32,16},{36,20},{40,24},{44,28},{48,3... | collective-permute-start | bytes 589832 | tf_op jit(solution)/shard_map/ppermute | solution.py:13
  81.4 5.2 %collective-permute-start.22 = (bf16[256,384]{1,0:T(8,128)(2,1)S(1)}, bf16[256,384]{1,0:T(8,128)(2,1)S(1)}, u32[]{:S(2)}, u32[]{:S(2)}) collective-permute-start(bf16[256,384]{1,0:T(8,128)(2,1)S(1)} %bitcast.130), channel_id=1, source_target_pairs={{0,32},{4,36},{8,40},{12,44},{16,48},{20,52},{24,56},{28,60},{32,6... | collective-permute-start | bytes 589832 | tf_op jit(solution)/shard_map/ppermute | solution.py:13
  86.6 5.5 %collective-permute-start.23 = (bf16[256,384]{1,0:T(8,128)(2,1)S(1)}, bf16[256,384]{1,0:T(8,128)(2,1)S(1)}, u32[]{:S(2)}, u32[]{:S(2)}) collective-permute-start(bf16[256,384]{1,0:T(8,128)(2,1)S(1)} %bitcast.131), channel_id=1, source_target_pairs={{32,0},{36,4},{40,8},{44,12},{48,16},{52,20},{56,24},{60,28},{64,3... | collective-permute-start | bytes 589832 | tf_op jit(solution)/shard_map/ppermute | solution.py:13
  92.1 3.4 %collective-permute-start.24 = (bf16[256,384]{1,0:T(8,128)(2,1)S(1)}, bf16[256,384]{1,0:T(8,128)(2,1)S(1)}, u32[]{:S(2)}, u32[]{:S(2)}) collective-permute-start(bf16[256,384]{1,0:T(8,128)(2,1)S(1)} %bitcast.132), channel_id=1, source_target_pairs={{0,64},{4,68},{8,72},{12,76},{16,80},{20,84},{24,88},{28,92},{32,9... | collective-permute-start | bytes 589832 | tf_op jit(solution)/shard_map/ppermute | solution.py:13
  95.5 2.4 collective-permute-start.25
  100.0 4.6 %collective-permute-done.22 = bf16[256,384]{1,0:T(8,128)(2,1)S(1)} collective-permute-done((bf16[256,384]{1,0:T(8,128)(2,1)S(1)}, bf16[256,384]{1,0:T(8,128)(2,1)S(1)}, u32[]{:S(2)}, u32[]{:S(2)}) %collective-permute-start.22) | collective-permute-done | bytes 196640 | tf_op jit(solution)/shard_map/ppermute | solution.py:13
  104.6 2.3 collective-permute-start.3
  110.3 6.7 %collective-permute-start.5 = (bf16[256,384]{1,0:T(8,128)(2,1)S(1)}, bf16[256,384]{1,0:T(8,128)(2,1)}, u32[]{:S(2)}, u32[]{:S(2)}) collective-permute-start(bf16[256,384]{1,0:T(8,128)(2,1)S(1)} %bitcast.111), channel_id=1, source_target_pairs={{12,0},{16,4},{20,8},{24,12},{28,16},{32,20},{36,24},{40,28},{44,3... | collective-permute-start | bytes 589832 | tf_op jit(solution)/shard_map/ppermute | solution.py:13
  117.0 6.1 %collective-permute-start.6 = (bf16[256,384]{1,0:T(8,128)(2,1)S(1)}, bf16[256,384]{1,0:T(8,128)(2,1)}, u32[]{:S(2)}, u32[]{:S(2)}) collective-permute-start(bf16[256,384]{1,0:T(8,128)(2,1)S(1)} %bitcast.112), channel_id=1, source_target_pairs={{0,16},{4,20},{8,24},{12,28},{16,32},{20,36},{24,40},{28,44},{32,4... | collective-permute-start | bytes 589832 | tf_op jit(solution)/shard_map/ppermute | solution.py:13
  123.8 7.4 %collective-permute-start.27 = (bf16[256,384]{1,0:T(8,128)(2,1)S(1)}, bf16[256,384]{1,0:T(8,128)(2,1)}, u32[]{:S(2)}, u32[]{:S(2)}) collective-permute-start(bf16[256,384]{1,0:T(8,128)(2,1)S(1)} %bitcast.135), channel_id=1, source_target_pairs={{128,0},{132,4},{136,8},{140,12},{144,16},{148,20},{152,24},{156,2... | collective-permute-start | bytes 589832 | tf_op jit(solution)/shard_map/ppermute | solution.py:13
  133.7 3.7 %collective-permute-start.7 = (bf16[256,384]{1,0:T(8,128)(2,1)S(1)}, bf16[256,384]{1,0:T(8,128)(2,1)}, u32[]{:S(2)}, u32[]{:S(2)}) collective-permute-start(bf16[256,384]{1,0:T(8,128)(2,1)S(1)} %bitcast.114), channel_id=1, source_target_pairs={{16,0},{20,4},{24,8},{28,12},{32,16},{36,20},{40,24},{44,28},{48,3... | collective-permute-start | bytes 589832 | tf_op jit(solution)/shard_map/ppermute | solution.py:13
  148.4 3.6 %collective-permute-start.8 = (bf16[256,384]{1,0:T(8,128)(2,1)S(1)}, bf16[256,384]{1,0:T(8,128)(2,1)}, u32[]{:S(2)}, u32[]{:S(2)}) collective-permute-start(bf16[256,384]{1,0:T(8,128)(2,1)S(1)} %bitcast.115), channel_id=1, source_target_pairs={{0,32},{4,36},{8,40},{12,44},{16,48},{20,52},{24,56},{28,60},{32,6... | collective-permute-start | bytes 589832 | tf_op jit(solution)/shard_map/ppermute | solution.py:13
  153.1 7.0 %collective-permute-start.9 = (bf16[256,384]{1,0:T(8,128)(2,1)S(1)}, bf16[256,384]{1,0:T(8,128)(2,1)}, u32[]{:S(2)}, u32[]{:S(2)}) collective-permute-start(bf16[256,384]{1,0:T(8,128)(2,1)S(1)} %bitcast.116), channel_id=1, source_target_pairs={{32,0},{36,4},{40,8},{44,12},{48,16},{52,20},{56,24},{60,28},{64,3... | collective-permute-start | bytes 589832 | tf_op jit(solution)/shard_map/ppermute | solution.py:13
  161.8 1.9 collective-permute-start.10
  165.5 3.9 %collective-permute-start.11 = (bf16[256,384]{1,0:T(8,128)(2,1)S(1)}, bf16[256,384]{1,0:T(8,128)(2,1)}, u32[]{:S(2)}, u32[]{:S(2)}) collective-permute-start(bf16[256,384]{1,0:T(8,128)(2,1)S(1)} %bitcast.118), channel_id=1, source_target_pairs={{64,0},{68,4},{72,8},{76,12},{80,16},{84,20},{88,24},{92,28},{96,3... | collective-permute-start | bytes 589832 | tf_op jit(solution)/shard_map/ppermute | solution.py:13
  177.3 7.4 %collective-permute-start.13 = (bf16[256,384]{1,0:T(8,128)(2,1)S(1)}, bf16[256,384]{1,0:T(8,128)(2,1)}, u32[]{:S(2)}, u32[]{:S(2)}) collective-permute-start(bf16[256,384]{1,0:T(8,128)(2,1)S(1)} %bitcast.120), channel_id=1, source_target_pairs={{128,0},{132,4},{136,8},{140,12},{144,16},{148,20},{152,24},{156,2... | collective-permute-start | bytes 589832 | tf_op jit(solution)/shard_map/ppermute | solution.py:13
  213.6 4.2 %fusion.135 = f32[3,128]{1,0:T(4,128)S(1)} fusion(bf16[3840,3,128]{2,0,1:T(8,128)(2,1)} %constant_dynamic-update-slice_fusion.15, pred[128,3840]{0,1:T(8,128)(4,1)} %copy-done.9, bf16[128,3,128]{2,1,0:T(4,128)(2,1)S(1)} %copy-done.6), kind=kOutput, calls=%fused_computation.176 | convolution fusion | flops 383389440 | bytes 3540480 | tf_op jit(solution)/shard_map/sub | solution.py:92
  217.8 5.6 %fusion.12 = bf16[3,128,128]{2,1,0:T(8,128)(2,1)S(1)} fusion(bf16[3840,3,128]{0,2,1:T(8,128)(2,1)} %constant_dynamic-update-slice_fusion, f32[3,128]{1,0:T(4,128)S(1)} %fusion.135, bf16[3840,3,128]{2,0,1:T(8,128)(2,1)} %constant_dynamic-update-slice_fusion.15, pred[128,3840]{0,1:T(8,128)(4,1)} %copy-done.9, bf16[128,3,128]{2,1,0:T(4,128)(2,1)S(1)} %copy-done.6), kind=kOutput, calls=%fused_computation.16 | convolution fusion | flops 762400896 | bytes 6587904 | tf_op jit(solution)/shard_map/hqk,khd->qhd/dot_general | solution.py:94
  223.6 4.3 %fusion.138 = f32[3,128]{1,0:T(4,128)S(1)} fusion(bf16[3840,3,128]{2,0,1:T(8,128)(2,1)} %constant_dynamic-update-slice_fusion.15, pred[128,3840]{0,1:T(8,128)(4,1)} %copy-done.8, bf16[128,3,128]{2,1,0:T(4,128)(2,1)S(1)} %copy-done.5), kind=kOutput, calls=%fused_computation.177 | convolution fusion | flops 383389440 | bytes 3540480 | tf_op jit(solution)/shard_map/sub | solution.py:92
  227.9 4.8 %fusion.13 = bf16[3,128,128]{2,1,0:T(8,128)(2,1)S(1)} fusion(bf16[3840,3,128]{0,2,1:T(8,128)(2,1)S(1)} %copy-done.7, f32[3,128]{1,0:T(4,128)S(1)} %fusion.138, bf16[3840,3,128]{2,0,1:T(8,128)(2,1)} %constant_dynamic-update-slice_fusion.15, pred[128,3840]{0,1:T(8,128)(4,1)} %copy-done.8, bf16[128,3,128]{2,1,0:T(4,128)(2,1)S(1)} %copy-done.5), kind=kOutput, calls=%fused_computation.17 | convolution fusion | flops 762400896 | bytes 6587904 | tf_op jit(solution)/shard_map/hqk,khd->qhd/dot_general | solution.py:94
  232.9 10.9 %all_to_all.73 = bf16[4,64,384]{2,1,0:T(8,128)(2,1)S(1)} all-to-all(bf16[4,64,384]{2,1,0:T(8,128)(2,1)S(1)} %bitcast.151), channel_id=1, replica_groups=mesh['frame'=64,'head'=4] {'head'}, dimensions={0} | all-to-all | bytes 393216 | tf_op jit(solution)/shard_map/all_to_all | solution.py:97
  (174 shorter events, 93.7 us)
Async XLA Ops:
  1.6 27.4 %all-to-all-start = ((bf16[64,4,384]{2,0,1:T(8,128)(2,1)}), bf16[64,4,384]{2,0,1:T(8,128)(2,1)S(1)}, u32[]{:S(2)}, u32[]{:S(2)}) async-start(bf16[64,4,384]{2,0,1:T(8,128)(2,1)} %bitcast.105), calls=%async_computation | async-start | bytes 393216 | tf_op jit(solution)/shard_map/all_to_all | solution.py:38
  29.0 14.9 %all-to-all-start.1 = ((bf16[64,4,384]{2,0,1:T(8,128)(2,1)}), bf16[64,4,384]{2,0,1:T(8,128)(2,1)S(1)}, u32[]{:S(2)}, u32[]{:S(2)}) async-start(bf16[64,4,384]{2,0,1:T(8,128)(2,1)} %bitcast.104), calls=%async_computation.1 | async-start | bytes 393216 | tf_op jit(solution)/shard_map/all_to_all | solution.py:37
  33.8 20.5 %collective-permute-start = (bf16[256,384]{1,0:T(8,128)(2,1)S(1)}, bf16[256,384]{1,0:T(8,128)(2,1)S(1)}, u32[]{:S(2)}, u32[]{:S(2)}) collective-permute-start(bf16[256,384]{1,0:T(8,128)(2,1)S(1)} %bitcast.106), channel_id=1, source_target_pairs={{0,4},{4,8},{8,12},{12,16},{16,20},{20,24},{24,28},{28,32},{32,36}... | collective-permute-start | bytes 589832 | tf_op jit(solution)/shard_map/ppermute | solution.py:13
  36.5 23.2 %collective-permute-start.1 = (bf16[256,384]{1,0:T(8,128)(2,1)S(1)}, bf16[256,384]{1,0:T(8,128)(2,1)S(1)}, u32[]{:S(2)}, u32[]{:S(2)}) collective-permute-start(bf16[256,384]{1,0:T(8,128)(2,1)S(1)} %bitcast.107), channel_id=1, source_target_pairs={{4,0},{8,4},{12,8},{16,12},{20,16},{24,20},{28,24},{32,28},{36,32}... | collective-permute-start | bytes 589832 | tf_op jit(solution)/shard_map/ppermute | solution.py:13
  40.1 22.3 %collective-permute-start.2 = (bf16[256,384]{1,0:T(8,128)(2,1)S(1)}, bf16[256,384]{1,0:T(8,128)(2,1)S(1)}, u32[]{:S(2)}, u32[]{:S(2)}) collective-permute-start(bf16[256,384]{1,0:T(8,128)(2,1)S(1)} %bitcast.108), channel_id=1, source_target_pairs={{0,8},{4,12},{8,16},{12,20},{16,24},{20,28},{24,32},{28,36},{32,40... | collective-permute-start | bytes 589832 | tf_op jit(solution)/shard_map/ppermute | solution.py:13
  43.9 87.3 %all-to-all-start.2 = ((bf16[64,4,384]{2,0,1:T(8,128)(2,1)}), bf16[64,4,384]{2,0,1:T(8,128)(2,1)S(1)}, u32[]{:S(2)}, u32[]{:S(2)}) async-start(bf16[64,4,384]{2,0,1:T(8,128)(2,1)} %bitcast.103), calls=%async_computation.2 | async-start | bytes 393216 | tf_op jit(solution)/shard_map/all_to_all | solution.py:36
  48.8 18.5 %collective-permute-start.14 = (bf16[256,384]{1,0:T(8,128)(2,1)S(1)}, bf16[256,384]{1,0:T(8,128)(2,1)S(1)}, u32[]{:S(2)}, u32[]{:S(2)}) collective-permute-start(bf16[256,384]{1,0:T(8,128)(2,1)S(1)} %bitcast.121), channel_id=1, source_target_pairs={{0,4},{4,8},{8,12},{12,16},{16,20},{20,24},{24,28},{28,32},{32,36}... | collective-permute-start | bytes 589832 | tf_op jit(solution)/shard_map/ppermute | solution.py:13
  50.7 20.3 %collective-permute-start.15 = (bf16[256,384]{1,0:T(8,128)(2,1)S(1)}, bf16[256,384]{1,0:T(8,128)(2,1)S(1)}, u32[]{:S(2)}, u32[]{:S(2)}) collective-permute-start(bf16[256,384]{1,0:T(8,128)(2,1)S(1)} %bitcast.122), channel_id=1, source_target_pairs={{4,0},{8,4},{12,8},{16,12},{20,16},{24,20},{28,24},{32,28},{36,32}... | collective-permute-start | bytes 589832 | tf_op jit(solution)/shard_map/ppermute | solution.py:13
  54.3 21.5 %collective-permute-start.16 = (bf16[256,384]{1,0:T(8,128)(2,1)S(1)}, bf16[256,384]{1,0:T(8,128)(2,1)S(1)}, u32[]{:S(2)}, u32[]{:S(2)}) collective-permute-start(bf16[256,384]{1,0:T(8,128)(2,1)S(1)} %bitcast.123), channel_id=1, source_target_pairs={{0,8},{4,12},{8,16},{12,20},{16,24},{20,28},{24,32},{28,36},{32,40... | collective-permute-start | bytes 589832 | tf_op jit(solution)/shard_map/ppermute | solution.py:13
  59.7 20.9 %copy-start.1 = (bf16[256,384]{1,0:T(8,128)(2,1)}, bf16[256,384]{1,0:T(8,128)(2,1)S(1)}, u32[]{:S(2)}) copy-start(bf16[256,384]{1,0:T(8,128)(2,1)S(1)} %collective-permute-done.1) | copy-start | bytes 589828
  59.7 21.7 %collective-permute-start.17 = (bf16[256,384]{1,0:T(8,128)(2,1)S(1)}, bf16[256,384]{1,0:T(8,128)(2,1)S(1)}, u32[]{:S(2)}, u32[]{:S(2)}) collective-permute-start(bf16[256,384]{1,0:T(8,128)(2,1)S(1)} %bitcast.124), channel_id=1, source_target_pairs={{8,0},{12,4},{16,8},{20,12},{24,16},{28,20},{32,24},{36,28},{40,32... | collective-permute-start | bytes 589832 | tf_op jit(solution)/shard_map/ppermute | solution.py:13
  62.4 24.2 %collective-permute-start.18 = (bf16[256,384]{1,0:T(8,128)(2,1)S(1)}, bf16[256,384]{1,0:T(8,128)(2,1)S(1)}, u32[]{:S(2)}, u32[]{:S(2)}) collective-permute-start(bf16[256,384]{1,0:T(8,128)(2,1)S(1)} %bitcast.125), channel_id=1, source_target_pairs={{0,12},{4,16},{8,20},{12,24},{16,28},{20,32},{24,36},{28,40},{32,4... | collective-permute-start | bytes 589832 | tf_op jit(solution)/shard_map/ppermute | solution.py:13
  67.3 24.8 %collective-permute-start.19 = (bf16[256,384]{1,0:T(8,128)(2,1)S(1)}, bf16[256,384]{1,0:T(8,128)(2,1)S(1)}, u32[]{:S(2)}, u32[]{:S(2)}) collective-permute-start(bf16[256,384]{1,0:T(8,128)(2,1)S(1)} %bitcast.126), channel_id=1, source_target_pairs={{12,0},{16,4},{20,8},{24,12},{28,16},{32,20},{36,24},{40,28},{44,3... | collective-permute-start | bytes 589832 | tf_op jit(solution)/shard_map/ppermute | solution.py:13
  71.0 24.5 %collective-permute-start.20 = (bf16[256,384]{1,0:T(8,128)(2,1)S(1)}, bf16[256,384]{1,0:T(8,128)(2,1)S(1)}, u32[]{:S(2)}, u32[]{:S(2)}) collective-permute-start(bf16[256,384]{1,0:T(8,128)(2,1)S(1)} %bitcast.127), channel_id=1, source_target_pairs={{0,16},{4,20},{8,24},{12,28},{16,32},{20,36},{24,40},{28,44},{32,4... | collective-permute-start | bytes 589832 | tf_op jit(solution)/shard_map/ppermute | solution.py:13
  75.8 22.1 %collective-permute-start.21 = (bf16[256,384]{1,0:T(8,128)(2,1)S(1)}, bf16[256,384]{1,0:T(8,128)(2,1)S(1)}, u32[]{:S(2)}, u32[]{:S(2)}) collective-permute-start(bf16[256,384]{1,0:T(8,128)(2,1)S(1)} %bitcast.128), channel_id=1, source_target_pairs={{16,0},{20,4},{24,8},{28,12},{32,16},{36,20},{40,24},{44,28},{48,3... | collective-permute-start | bytes 589832 | tf_op jit(solution)/shard_map/ppermute | solution.py:13
  81.4 23.2 %collective-permute-start.22 = (bf16[256,384]{1,0:T(8,128)(2,1)S(1)}, bf16[256,384]{1,0:T(8,128)(2,1)S(1)}, u32[]{:S(2)}, u32[]{:S(2)}) collective-permute-start(bf16[256,384]{1,0:T(8,128)(2,1)S(1)} %bitcast.130), channel_id=1, source_target_pairs={{0,32},{4,36},{8,40},{12,44},{16,48},{20,52},{24,56},{28,60},{32,6... | collective-permute-start | bytes 589832 | tf_op jit(solution)/shard_map/ppermute | solution.py:13
  86.6 21.8 %collective-permute-start.23 = (bf16[256,384]{1,0:T(8,128)(2,1)S(1)}, bf16[256,384]{1,0:T(8,128)(2,1)S(1)}, u32[]{:S(2)}, u32[]{:S(2)}) collective-permute-start(bf16[256,384]{1,0:T(8,128)(2,1)S(1)} %bitcast.131), channel_id=1, source_target_pairs={{32,0},{36,4},{40,8},{44,12},{48,16},{52,20},{56,24},{60,28},{64,3... | collective-permute-start | bytes 589832 | tf_op jit(solution)/shard_map/ppermute | solution.py:13
  92.1 18.2 %collective-permute-start.24 = (bf16[256,384]{1,0:T(8,128)(2,1)S(1)}, bf16[256,384]{1,0:T(8,128)(2,1)S(1)}, u32[]{:S(2)}, u32[]{:S(2)}) collective-permute-start(bf16[256,384]{1,0:T(8,128)(2,1)S(1)} %bitcast.132), channel_id=1, source_target_pairs={{0,64},{4,68},{8,72},{12,76},{16,80},{20,84},{24,88},{28,92},{32,9... | collective-permute-start | bytes 589832 | tf_op jit(solution)/shard_map/ppermute | solution.py:13
  95.5 21.5 %collective-permute-start.25 = (bf16[256,384]{1,0:T(8,128)(2,1)S(1)}, bf16[256,384]{1,0:T(8,128)(2,1)S(1)}, u32[]{:S(2)}, u32[]{:S(2)}) collective-permute-start(bf16[256,384]{1,0:T(8,128)(2,1)S(1)} %bitcast.133), channel_id=1, source_target_pairs={{64,0},{68,4},{72,8},{76,12},{80,16},{84,20},{88,24},{92,28},{96,3... | collective-permute-start | bytes 589832 | tf_op jit(solution)/shard_map/ppermute | solution.py:13
  98.0 25.2 %collective-permute-start.26 = (bf16[256,384]{1,0:T(8,128)(2,1)S(1)}, bf16[256,384]{1,0:T(8,128)(2,1)S(1)}, u32[]{:S(2)}, u32[]{:S(2)}) collective-permute-start(bf16[256,384]{1,0:T(8,128)(2,1)S(1)} %bitcast.134), channel_id=1, source_target_pairs={{0,128},{4,132},{8,136},{12,140},{16,144},{20,148},{24,152},{28,15... | collective-permute-start | bytes 589832 | tf_op jit(solution)/shard_map/ppermute | solution.py:13
  104.6 43.8 %collective-permute-start.3 = (bf16[256,384]{1,0:T(8,128)(2,1)S(1)}, bf16[256,384]{1,0:T(8,128)(2,1)}, u32[]{:S(2)}, u32[]{:S(2)}) collective-permute-start(bf16[256,384]{1,0:T(8,128)(2,1)S(1)} %bitcast.109), channel_id=1, source_target_pairs={{8,0},{12,4},{16,8},{20,12},{24,16},{28,20},{32,24},{36,28},{40,32... | collective-permute-start | bytes 589832 | tf_op jit(solution)/shard_map/ppermute | solution.py:13
  108.4 44.7 %collective-permute-start.4 = (bf16[256,384]{1,0:T(8,128)(2,1)S(1)}, bf16[256,384]{1,0:T(8,128)(2,1)}, u32[]{:S(2)}, u32[]{:S(2)}) collective-permute-start(bf16[256,384]{1,0:T(8,128)(2,1)S(1)} %bitcast.110), channel_id=1, source_target_pairs={{0,12},{4,16},{8,20},{12,24},{16,28},{20,32},{24,36},{28,40},{32,4... | collective-permute-start | bytes 589832 | tf_op jit(solution)/shard_map/ppermute | solution.py:13
  110.3 51.5 %collective-permute-start.5 = (bf16[256,384]{1,0:T(8,128)(2,1)S(1)}, bf16[256,384]{1,0:T(8,128)(2,1)}, u32[]{:S(2)}, u32[]{:S(2)}) collective-permute-start(bf16[256,384]{1,0:T(8,128)(2,1)S(1)} %bitcast.111), channel_id=1, source_target_pairs={{12,0},{16,4},{20,8},{24,12},{28,16},{32,20},{36,24},{40,28},{44,3... | collective-permute-start | bytes 589832 | tf_op jit(solution)/shard_map/ppermute | solution.py:13
  117.0 48.5 %collective-permute-start.6 = (bf16[256,384]{1,0:T(8,128)(2,1)S(1)}, bf16[256,384]{1,0:T(8,128)(2,1)}, u32[]{:S(2)}, u32[]{:S(2)}) collective-permute-start(bf16[256,384]{1,0:T(8,128)(2,1)S(1)} %bitcast.112), channel_id=1, source_target_pairs={{0,16},{4,20},{8,24},{12,28},{16,32},{20,36},{24,40},{28,44},{32,4... | collective-permute-start | bytes 589832 | tf_op jit(solution)/shard_map/ppermute | solution.py:13
  123.8 9.9 %collective-permute-start.27 = (bf16[256,384]{1,0:T(8,128)(2,1)S(1)}, bf16[256,384]{1,0:T(8,128)(2,1)}, u32[]{:S(2)}, u32[]{:S(2)}) collective-permute-start(bf16[256,384]{1,0:T(8,128)(2,1)S(1)} %bitcast.135), channel_id=1, source_target_pairs={{128,0},{132,4},{136,8},{140,12},{144,16},{148,20},{152,24},{156,2... | collective-permute-start | bytes 589832 | tf_op jit(solution)/shard_map/ppermute | solution.py:13
  133.7 39.2 %collective-permute-start.7 = (bf16[256,384]{1,0:T(8,128)(2,1)S(1)}, bf16[256,384]{1,0:T(8,128)(2,1)}, u32[]{:S(2)}, u32[]{:S(2)}) collective-permute-start(bf16[256,384]{1,0:T(8,128)(2,1)S(1)} %bitcast.114), channel_id=1, source_target_pairs={{16,0},{20,4},{24,8},{28,12},{32,16},{36,20},{40,24},{44,28},{48,3... | collective-permute-start | bytes 589832 | tf_op jit(solution)/shard_map/ppermute | solution.py:13
  148.4 29.0 %collective-permute-start.8 = (bf16[256,384]{1,0:T(8,128)(2,1)S(1)}, bf16[256,384]{1,0:T(8,128)(2,1)}, u32[]{:S(2)}, u32[]{:S(2)}) collective-permute-start(bf16[256,384]{1,0:T(8,128)(2,1)S(1)} %bitcast.115), channel_id=1, source_target_pairs={{0,32},{4,36},{8,40},{12,44},{16,48},{20,52},{24,56},{28,60},{32,6... | collective-permute-start | bytes 589832 | tf_op jit(solution)/shard_map/ppermute | solution.py:13
  153.1 35.1 %collective-permute-start.9 = (bf16[256,384]{1,0:T(8,128)(2,1)S(1)}, bf16[256,384]{1,0:T(8,128)(2,1)}, u32[]{:S(2)}, u32[]{:S(2)}) collective-permute-start(bf16[256,384]{1,0:T(8,128)(2,1)S(1)} %bitcast.116), channel_id=1, source_target_pairs={{32,0},{36,4},{40,8},{44,12},{48,16},{52,20},{56,24},{60,28},{64,3... | collective-permute-start | bytes 589832 | tf_op jit(solution)/shard_map/ppermute | solution.py:13
  161.8 30.8 %collective-permute-start.10 = (bf16[256,384]{1,0:T(8,128)(2,1)S(1)}, bf16[256,384]{1,0:T(8,128)(2,1)}, u32[]{:S(2)}, u32[]{:S(2)}) collective-permute-start(bf16[256,384]{1,0:T(8,128)(2,1)S(1)} %bitcast.117), channel_id=1, source_target_pairs={{0,64},{4,68},{8,72},{12,76},{16,80},{20,84},{24,88},{28,92},{32,9... | collective-permute-start | bytes 589832 | tf_op jit(solution)/shard_map/ppermute | solution.py:13
  165.5 30.3 %collective-permute-start.11 = (bf16[256,384]{1,0:T(8,128)(2,1)S(1)}, bf16[256,384]{1,0:T(8,128)(2,1)}, u32[]{:S(2)}, u32[]{:S(2)}) collective-permute-start(bf16[256,384]{1,0:T(8,128)(2,1)S(1)} %bitcast.118), channel_id=1, source_target_pairs={{64,0},{68,4},{72,8},{76,12},{80,16},{84,20},{88,24},{92,28},{96,3... | collective-permute-start | bytes 589832 | tf_op jit(solution)/shard_map/ppermute | solution.py:13
  172.9 26.4 %collective-permute-start.12 = (bf16[256,384]{1,0:T(8,128)(2,1)S(1)}, bf16[256,384]{1,0:T(8,128)(2,1)}, u32[]{:S(2)}, u32[]{:S(2)}) collective-permute-start(bf16[256,384]{1,0:T(8,128)(2,1)S(1)} %bitcast.119), channel_id=1, source_target_pairs={{0,128},{4,132},{8,136},{12,140},{16,144},{20,148},{24,152},{28,15... | collective-permute-start | bytes 589832 | tf_op jit(solution)/shard_map/ppermute | solution.py:13
  177.3 24.6 %collective-permute-start.13 = (bf16[256,384]{1,0:T(8,128)(2,1)S(1)}, bf16[256,384]{1,0:T(8,128)(2,1)}, u32[]{:S(2)}, u32[]{:S(2)}) collective-permute-start(bf16[256,384]{1,0:T(8,128)(2,1)S(1)} %bitcast.120), channel_id=1, source_target_pairs={{128,0},{132,4},{136,8},{140,12},{144,16},{148,20},{152,24},{156,2... | collective-permute-start | bytes 589832 | tf_op jit(solution)/shard_map/ppermute | solution.py:13
  (9 other events, 73.2 us)
where the time goes:
time: 246 us; the launch traced here: 244 us
  starting transfers between devices  124 us (50%)
  local copies, waits for them, and re-layouts  63.1 us (26%)
  other arithmetic  19.9 us (8%)
  matrix products  18.9 us (8%)
  blocking collectives  10.9 us (4%)
  waiting for transfers between devices  7.03 us (3%)
    ppermute x28, starting transfers between devices, shifted(): return lax.ppermute(block, axis, route)  110 us
    unnamed x48, local copies, waits for them, and re-layouts  27.1 us
    ppermute x28, local copies, waits for them, and re-layouts, shifted(): return lax.ppermute(block, axis, route)  22.9 us
    unnamed x27, other arithmetic  18.4 us
    all_to_all x1, blocking collectives, shards(): lax.all_to_all(combined, 'head', split_axis=0, concat_axis=1, tiled=True)  10.9 us
    dot_general x2, matrix products, shards(): jnp.einsum('hqk,khd->qhd', weights, value_all, preferred_element_type=jnp...  10.4 us
    sub x2, matrix products, shards(): exponent = jnp.exp(scores - largest)  8.51 us
    ppermute x28, waiting for transfers between devices, shifted(): return lax.ppermute(block, axis, route)  7.02 us
  transfers between devices with their start and end apart: 31, of which 3 were waited for; matrix products, arithmetic and copies ran while one was open for 27% of the time, Pallas kernels for 0%

commit v1 on v0

v1 whole, which is shorter than its diff:
```python
import functools
import math

import jax
import jax.numpy as jnp
from jax import lax
from jax.experimental import pallas as pl
from jax.experimental.pallas import tpu as pltpu
from jax.sharding import PartitionSpec as P

HEAD_DIM = 128
TOK = 256
QUARTER = 64
HEADS_HERE = 3
W = HEADS_HERE * HEAD_DIM
XS, ZS, CS, YS = 4, 8, 2, 4
FRAMES = XS * ZS * CS
SCALE = HEAD_DIM**-0.5 * math.log2(math.e)
VMEM = pl.BlockSpec(memory_space=pltpu.VMEM)
LIGHT = pl.CostEstimate(flops=1, bytes_accessed=1, transcendentals=0)
SMEM = pl.BlockSpec(memory_space=pltpu.SMEM)


def frame_of(x, z, core):
    return ((x % XS) * ZS + z % ZS) * CS + core


def route(source):
    return [
        (frame_of(*source(x, z, c)), frame_of(x, z, c))
        for x in range(XS)
        for z in range(ZS)
        for c in range(CS)
    ]


def from_z(step):
    return route(lambda x, z, c: (x, z + step, c))


def from_x(step):
    return route(lambda x, z, c: (x + step, z, c))


def from_chip(step):
    return [((f + step * CS) % FRAMES, f) for f in range(FRAMES)]


FROM_PARTNER = route(lambda x, z, c: (x, z, 1 - c))
FROM_X_FOR_8 = route(lambda x, z, c: (x - 1 if z < ZS // 2 else x + 1, z, c))


def move(block, pairs):
    return lax.ppermute(block, "frame", pairs)


def copy_all(pairs):
    for source, out in pairs:
        out[...] = source[...]


def copier(kernel, out_shape, name):
    return lambda *arrays: pl.pallas_call(
        kernel,
        out_shape=out_shape,
        in_specs=[VMEM] * len(arrays),
        out_specs=[VMEM] * len(out_shape),
        cost_estimate=LIGHT,
        name=name,
    )(*arrays)


def bf16(rows, columns):
    return jax.ShapeDtypeStruct((rows, columns), jnp.bfloat16)


def group_at(group):
    return pl.ds(pl.multiple_of(group * W, W), W)


def quarter_at(quarter):
    return pl.ds(pl.multiple_of(quarter * QUARTER, QUARTER), QUARTER)


def pack_kernel(k_ref, v_ref, q_ref, p0, p1, p2, p3, raw_ref):
    y = lax.axis_index("head")
    pairs = []
    for step, out in enumerate((p0, p1, p2, p3)):
        for i, ref in enumerate((k_ref, v_ref, q_ref)):
            pairs.append((ref.at[:, group_at((y + step) % YS)], out.at[:, i * W : (i + 1) * W]))
    for i, ref in enumerate((k_ref, v_ref)):
        pairs.append((ref, raw_ref.at[:, i * YS * W : (i + 1) * YS * W]))
    copy_all(pairs)


def pack(keys, values, queries):
    out_shape = [bf16(QUARTER, 3 * W)] * YS + [bf16(QUARTER, 2 * YS * W)]
    return copier(pack_kernel, out_shape, "pack")(keys, values, queries)


def unpack_kernel(raw_ref, out_ref):
    pairs = []
    for g in range(YS):
        for i in range(2):
            at = (i * YS + g) * W
            out = out_ref.at[g * QUARTER : (g + 1) * QUARTER, i * W : (i + 1) * W]
            pairs.append((raw_ref.at[:, at : at + W], out))
    copy_all(pairs)


def unpack(raw):
    return copier(unpack_kernel, [bf16(TOK, 2 * W)], "unpack")(raw)[0]


def join_kernel(p0, p1, p2, p3, kv_ref, q_ref):
    y = lax.axis_index("head")
    pairs = []
    for step, piece in enumerate((p0, p1, p2, p3)):
        rows = quarter_at((y + YS - step) % YS)
        pairs.append((piece.at[:, : 2 * W], kv_ref.at[rows, :]))
        pairs.append((piece.at[:, 2 * W :], q_ref.at[rows, :]))
    copy_all(pairs)


def join(pieces):
    return copier(join_kernel, [bf16(TOK, 2 * W), bf16(TOK, W)], "join")(*pieces)


def place_kernel(p0, p1, p2, p3, out_ref):
    y = lax.axis_index("head")
    pairs = [
        (piece, out_ref.at[:, group_at((y + YS - step) % YS)])
        for step, piece in enumerate((p0, p1, p2, p3))
    ]
    copy_all(pairs)


def place(pieces):
    return copier(place_kernel, [bf16(QUARTER, YS * W)], "place")(*pieces)[0]


def y_from(step):
    return [((y - step) % YS, y) for y in range(YS)]


def over_heads(pieces):
    return [pieces[0]] + [lax.ppermute(pieces[s], "head", y_from(s)) for s in range(1, YS)]


BLOCKS = {
    "own": (lambda f, x, z, c: f, None),
    "partner": (lambda f, x, z, c: f + 1 - 2 * c, 128),
    "next1": (lambda f, x, z, c: f + 2, 64),
    "prev1": (lambda f, x, z, c: f - 2, 64),
    "next1p": (lambda f, x, z, c: f + 3 - 2 * c, 128),
    "prev1p": (lambda f, x, z, c: f - 1 - 2 * c, 128),
    "next2": (lambda f, x, z, c: f + 4, 32),
    "prev2": (lambda f, x, z, c: f - 4, 32),
    "far2p": (lambda f, x, z, c: f - 3 + 6 * c, 64),
    "z4": (lambda f, x, z, c: jnp.where(z < 4, f + 8, f - 8), 32),
    "z4x": (lambda f, x, z, c: jnp.where(z < 4, f - 8, f + 8), 32),
    "xnext": (lambda f, x, z, c: f + 16, 32),
    "xprev": (lambda f, x, z, c: f - 16, 32),
    "x2": (lambda f, x, z, c: jnp.where(x < 2, f + 32, f - 32), 32),
}
ROWS = 128
HALF = 64
FAR_STARTS = (0, 32, 96, 128)


def dot_t(a, b):
    return lax.dot_general(a, b, (((1,), (1,)), ((), ())), preferred_element_type=jnp.float32)


def attend_kernel(names, kinds, first, last, band_ref, q_ref, *refs):
    core = lax.axis_index("frame") % CS
    blocks, at = [], 0
    for kind in kinds:
        blocks.append(refs[at : at + (1 if kind == "joint" else 2)])
        at += len(blocks[-1])
    refs = refs[at:]

    def block(i, rows, columns, value):
        kind, parts = kinds[i], blocks[i]
        if kind == "split":
            return parts[value][rows, columns]
        columns = slice(columns.start + value * W, columns.stop + value * W)
        here = parts[0][rows, columns]
        if kind == "choice":
            here = jnp.where(core == 0, here, parts[1][rows, columns])
        return here

    whole = slice(0, TOK)
    if not first:
        stats_in, acc_in = refs[:2]
        refs = refs[2:]
    f = lax.axis_index("frame")
    x, z = f // (ZS * CS), (f // CS) % ZS
    bands = []
    for name in names:
        frame_at, reach = BLOCKS[name]
        if reach is None:
            bands.append(None)
            continue
        g = frame_at(f, x, z, core)
        inside = (g >= 0) & (g < FRAMES)
        bands.append(jnp.where(inside, band_ref[0, jnp.clip(g, 0, FRAMES - 1)], -1))
    far = [i for i, n in enumerate(names) if BLOCKS[n][1] == 32]
    near = [i for i in range(len(names)) if i not in far]
    gaps = {}
    for part in range(TOK // ROWS):
        row0 = part * ROWS
        gap = lax.broadcasted_iota(jnp.int32, (ROWS, TOK), 0) - lax.broadcasted_iota(
            jnp.int32, (ROWS, TOK), 1
        )
        starts = FAR_STARTS[part * 2 : part * 2 + 2]
        far_gap = lax.broadcasted_iota(jnp.int32, (HALF, ROWS), 0) - lax.broadcasted_iota(
            jnp.int32, (HALF, ROWS), 1
        )
        gaps[part] = (
            jnp.abs(gap + row0),
            jnp.abs(
                jnp.concatenate([far_gap + (row0 + j * HALF - starts[j]) for j in range(2)], axis=0)
            ),
            starts,
        )

    units = [(part, h) for part in range(TOK // ROWS) for h in range(HEADS_HERE)]
    size = len(units) if len(names) <= 2 else HEADS_HERE
    for u0 in range(0, len(units), size):
        group = units[u0 : u0 + size]
        tiles, tops, fades, ps, totals, outs = {}, {}, {}, {}, {}, {}
        for u in group:
            part, h = u
            near_gap, far_gap, starts = gaps[part]
            rows = slice(part * ROWS, (part + 1) * ROWS)
            kc = slice(h * HEAD_DIM, (h + 1) * HEAD_DIM)
            q = q_ref[rows, kc]
            for i in near:
                s = dot_t(q, block(i, whole, kc, 0)) * SCALE
                if bands[i] is not None:
                    s = jnp.where(near_gap <= bands[i], s, -jnp.inf)
                tiles[u, i] = s
            for i in far:
                s = [
                    dot_t(
                        q[j * HALF : (j + 1) * HALF],
                        block(i, slice(starts[j], starts[j] + ROWS), kc, 0),
                    )
                    for j in range(2)
                ]
                s = jnp.concatenate(s, axis=0) * SCALE
                tiles[u, i] = jnp.where(far_gap <= bands[i], s, -jnp.inf)
        for u in group:
            parts = [
                tiles[u, i][:, c0 : c0 + 128]
                for i in range(len(names))
                for c0 in range(0, tiles[u, i].shape[1], 128)
            ]
            tops[u] = jnp.max(functools.reduce(jnp.maximum, parts), axis=1, keepdims=True)
        if not first:
            for u in group:
                part, h = u
                rows = slice(part * ROWS, (part + 1) * ROWS)
                top_in = stats_in[rows, h : h + 1]
                tops[u] = jnp.maximum(tops[u], top_in)
                fades[u] = jnp.exp2(top_in - tops[u])
        for u in group:
            parts = []
            for i in range(len(names)):
                p = jnp.exp2(tiles[u, i] - tops[u])
                parts += [p[:, c0 : c0 + 128] for c0 in range(0, p.shape[1], 128)]
                ps[u, i] = p.astype(jnp.bfloat16)
            totals[u] = jnp.sum(functools.reduce(jnp.add, parts), axis=1, keepdims=True)
        for u in group:
            part, h = u
            starts = gaps[part][2]
            kc = slice(h * HEAD_DIM, (h + 1) * HEAD_DIM)
            parts = []
            for i in range(len(names)):
                p = ps[u, i]
                if i in near:
                    o = jnp.dot(p, block(i, whole, kc, 1), preferred_element_type=jnp.float32)
                else:
                    o = [
                        jnp.dot(
                            p[j * HALF : (j + 1) * HALF],
                            block(i, slice(starts[j], starts[j] + ROWS), kc, 1),
                            preferred_element_type=jnp.float32,
                        )
                        for j in range(2)
                    ]
                    o = jnp.concatenate(o, axis=0)
                parts.append(o)
            outs[u] = functools.reduce(jnp.add, parts)
        for u in group:
            part, h = u
            rows = slice(part * ROWS, (part + 1) * ROWS)
            kc = slice(h * HEAD_DIM, (h + 1) * HEAD_DIM)
            total, out = totals[u], outs[u]
            if not first:
                total = total + stats_in[rows, 4 + h : 5 + h] * fades[u]
                out = out + acc_in[rows, kc] * fades[u]
            if last:
                refs[YS][rows, kc] = (out * (1.0 / total)).astype(jnp.bfloat16)
            else:
                refs[0][rows, h : h + 1] = tops[u]
                refs[0][rows, 4 + h : 5 + h] = total
                refs[1][rows, kc] = out
    if last:
        y = lax.axis_index("head")
        for step in range(YS):
            rows = pl.ds(pl.multiple_of(((y + step) % YS) * QUARTER, QUARTER), QUARTER)
            refs[step][...] = refs[YS][rows, :]


def attend(band, q, blocks, state, last):
    names = list(blocks)
    first = state is None
    kinds, arrays = [], []
    for block in blocks.values():
        kinds.append(block[0])
        arrays += block[1:]
    if last:
        out_shape = [jax.ShapeDtypeStruct((QUARTER, W), jnp.bfloat16)] * YS
    else:
        out_shape = [
            jax.ShapeDtypeStruct((TOK, 128), jnp.float32),
            jax.ShapeDtypeStruct((TOK, W), jnp.float32),
        ]
    return pl.pallas_call(
        functools.partial(attend_kernel, names, kinds, first, last),
        out_shape=out_shape,
        in_specs=[SMEM] + [VMEM] * (1 + len(arrays) + (0 if first else 2)),
        out_specs=[VMEM] * len(out_shape),
        scratch_shapes=[pltpu.VMEM((TOK, W), jnp.bfloat16)] if last else [],
        compiler_params=pltpu.CompilerParams(vmem_limit_bytes=32 * 1024 * 1024),
        cost_estimate=LIGHT,
        name="attend" + str(len(names)),
    )(band, q, *arrays, *(() if first else state))


def shards(queries, keys, values, band):
    barrier = lax.optimization_barrier
    *pieces, raw = pack(keys, values, queries)
    z4_raw = move(raw, from_z(4))
    own, q = join(over_heads(pieces))

    xnext, xprev = move(own, from_x(1)), move(own, from_x(-1))
    next1, prev1 = move(own, from_chip(1)), move(own, from_chip(-1))
    sent, z4_raw = barrier((own, z4_raw))
    partner = move(sent, FROM_PARTNER)
    z4_packed = unpack(z4_raw)
    z4 = lax.all_to_all(z4_packed, "head", split_axis=0, concat_axis=0, tiled=True)

    def step(state, last=False, **blocks):
        blocks = {k: b if isinstance(b, tuple) else ("joint", b) for k, b in blocks.items()}
        return attend(band, q, blocks, state, last)

    state = step(None, own=own, partner=partner, xnext=xnext, xprev=xprev)

    z = (lax.axis_index("frame") // CS) % ZS
    next2 = move(jnp.where(z < 2, xnext, own), from_z(2))
    prev2 = move(jnp.where(z >= ZS - 2, xprev, own), from_z(-2))
    z4x = move(z4, FROM_X_FOR_8)
    sent, sent1, sent2, *_ = barrier((own, next1, prev1, z4))
    x2 = move(sent, from_x(2))
    next1p, prev1p = move(sent1, FROM_PARTNER), move(sent2, FROM_PARTNER)
    state = step(state, next1=next1, prev1=prev1, next1p=next1p, prev1p=prev1p, z4=z4)

    next2, prev2, state = barrier((next2, prev2, state))
    next2p, prev2p = move(next2, FROM_PARTNER), move(prev2, FROM_PARTNER)
    state = step(state, x2=x2, z4x=z4x, next2=next2, prev2=prev2)
    outs = step(state, True, far2p=("choice", prev2p, next2p))
    return place(over_heads(outs))


def solution(mesh):
    placed = (
        P(("frame", "head"), None),
        P(("frame", "head"), None),
        P(("frame", "head"), None),
        P("frame", None),
    )
    return jax.shard_map(
        shards, mesh=mesh, in_specs=placed, out_specs=P(("frame", "head"), None), check_vma=False
    )
```

time: 246 us -> 84.4 us (0.34)
  the two profiles are of different devices: /device:TPU:36 before, /device:TPU:1 now
where the time goes in v1:
time: 84.4 us; the launch traced here: 83.9 us
  starting transfers between devices  36.2 us (43%)
  waiting for transfers between devices  27.8 us (33%)
  Pallas kernels  17 us (20%)
  local copies, waits for them, and re-layouts  2.68 us (3%)
    ppermute x14, starting transfers between devices, move(): return lax.ppermute(block, 'frame', pairs)  24.9 us
    ppermute x14, waiting for transfers between devices, move(): return lax.ppermute(block, 'frame', pairs)  17.2 us
    pallas_call x4, Pallas kernels, attend(): pl.pallas_call(functools.partial(attend_kernel, names, kinds, first, last...  9.48 us
    ppermute x6, waiting for transfers between devices, over_heads(): lax.ppermute(pieces[s], 'head', y_from(s))  8.1 us
    ppermute x6, starting transfers between devices, over_heads(): lax.ppermute(pieces[s], 'head', y_from(s))  7.66 us
    pallas_call x4, Pallas kernels, copier(): pl.pallas_call(kernel, out_shape=out_shape, in_specs=[VMEM] * len(arrays)...  7.49 us
    all_to_all x1, starting transfers between devices, shards(): lax.all_to_all(z4_packed, 'head', split_axis=0, concat_axis=0, tiled=True)  3.62 us
    unnamed x22, local copies, waits for them, and re-layouts  2.68 us
  transfers between devices with their start and end apart: 21, of which 11 were waited for; matrix products, arithmetic and copies ran while one was open for 0% of the time, Pallas kernels for 13%

profile of v1, /device:TPU:1, one launch (start us, length us, event | category | flops | bytes accessed | tf_op | source)
XLA Modules:
  0.0 83.9 jit_solution(6625232107896595239)
XLA Ops:
  0.0 2.1 %pack.1 = (bf16[64,1152]{1,0:T(8,128)(2,1)}, bf16[64,1152]{1,0:T(8,128)(2,1)}, bf16[64,1152]{1,0:T(8,128)(2,1)}, bf16[64,1152]{1,0:T(8,128)(2,1)}, bf16[64,3072]{1,0:T(8,128)(2,1)}) custom-call(bf16[64,1536]{1,0:T(8,128)(2,1)} %k_ref.1, bf16[64,1536]{1,0:T(8,128)(2,1)} %v_ref.1, bf16[64,1536]{1,0:T(8,128)(2,1)} %q_ref.1), custom_call_target="tpu_custom_call" | custom-call | flops 1 | bytes 1 | tf_op jit(solution)/shard_map/pack/pallas_call | solution.py:63
  2.1 7.7 %collective-permute-start.9 = (bf16[64,3072]{1,0:T(8,128)(2,1)}, bf16[64,3072]{1,0:T(8,128)(2,1)S(1)}, u32[]{:S(2)}, u32[]{:S(2)}) collective-permute-start(bf16[64,3072]{1,0:T(8,128)(2,1)} %get-tuple-element.37), channel_id=1, source_target_pairs={{32,0},{36,4},{40,8},{44,12},{48,16},{52,20},{56,24},{60,28},{0,32... | collective-permute-start | bytes 1179656 | tf_op jit(solution)/shard_map/ppermute | solution.py:54
  9.9 1.3 %collective-permute-start = (bf16[64,1152]{1,0:T(8,128)(2,1)}, bf16[64,1152]{1,0:T(8,128)(2,1)S(1)}, u32[]{:S(2)}, u32[]{:S(2)}) collective-permute-start(bf16[64,1152]{1,0:T(8,128)(2,1)} %get-tuple-element.32), channel_id=1, source_target_pairs={{3,0},{0,1},{1,2},{2,3},{7,4},{4,5},{5,6},{6,7},{11,8},{8,9},{9,10... | collective-permute-start | bytes 442376 | tf_op jit(solution)/shard_map/ppermute | solution.py:147
  11.2 2.6 %collective-permute-start.1 = (bf16[64,1152]{1,0:T(8,128)(2,1)}, bf16[64,1152]{1,0:T(8,128)(2,1)S(1)}, u32[]{:S(2)}, u32[]{:S(2)}) collective-permute-start(bf16[64,1152]{1,0:T(8,128)(2,1)} %get-tuple-element.33), channel_id=1, source_target_pairs={{2,0},{3,1},{0,2},{1,3},{6,4},{7,5},{4,6},{5,7},{10,8},{11,9},{8,1... | collective-permute-start | bytes 442376 | tf_op jit(solution)/shard_map/ppermute | solution.py:147
  13.8 1.1 %collective-permute-start.2 = (bf16[64,1152]{1,0:T(8,128)(2,1)}, bf16[64,1152]{1,0:T(8,128)(2,1)S(1)}, u32[]{:S(2)}, u32[]{:S(2)}) collective-permute-start(bf16[64,1152]{1,0:T(8,128)(2,1)} %get-tuple-element.34), channel_id=1, source_target_pairs={{1,0},{2,1},{3,2},{0,3},{5,4},{6,5},{7,6},{4,7},{9,8},{10,9},{11,1... | collective-permute-start | bytes 442376 | tf_op jit(solution)/shard_map/ppermute | solution.py:147
  14.9 1.0 %collective-permute-done.p1 = bf16[64,1152]{1,0:T(8,128)(2,1)S(1)} collective-permute-done((bf16[64,1152]{1,0:T(8,128)(2,1)}, bf16[64,1152]{1,0:T(8,128)(2,1)S(1)}, u32[]{:S(2)}, u32[]{:S(2)}) %collective-permute-start) | collective-permute-done | bytes 147488 | tf_op jit(solution)/shard_map/ppermute | solution.py:147
  15.8 4.3 %collective-permute-done.1.p2 = bf16[64,1152]{1,0:T(8,128)(2,1)S(1)} collective-permute-done((bf16[64,1152]{1,0:T(8,128)(2,1)}, bf16[64,1152]{1,0:T(8,128)(2,1)S(1)}, u32[]{:S(2)}, u32[]{:S(2)}) %collective-permute-start.1) | collective-permute-done | bytes 147488 | tf_op jit(solution)/shard_map/ppermute | solution.py:147
  20.8 2.0 %join.1 = (bf16[256,768]{1,0:T(8,128)(2,1)}, bf16[256,384]{1,0:T(8,128)(2,1)}) custom-call(bf16[64,1152]{1,0:T(8,128)(2,1)} %get-tuple-element.31.p0, bf16[64,1152]{1,0:T(8,128)(2,1)} %copy-done.5, bf16[64,1152]{1,0:T(8,128)(2,1)} %copy-done.6, bf16[64,1152]{1,0:T(8,128)(2,1)} %copy-done.7), custom_call_target="tpu_custom_call" | custom-call | flops 1 | bytes 1 | tf_op jit(solution)/shard_map/join/pallas_call | solution.py:63
  22.8 2.0 %collective-permute-start.7 = (bf16[256,768]{1,0:T(8,128)(2,1)}, bf16[256,768]{1,0:T(8,128)(2,1)S(1)}, u32[]{:S(2)}, u32[]{:S(2)}) collective-permute-start(bf16[256,768]{1,0:T(8,128)(2,1)} %get-tuple-element.48.refs_0_), channel_id=1, source_target_pairs={{8,0},{12,4},{16,8},{20,12},{24,16},{28,20},{32,24},{36,28},{40,32... | collective-permute-start | bytes 1179656 | tf_op jit(solution)/shard_map/ppermute | solution.py:54
  24.8 1.9 %collective-permute-start.3 = (bf16[256,768]{1,0:T(8,128)(2,1)}, bf16[256,768]{1,0:T(8,128)(2,1)S(1)}, u32[]{:S(2)}, u32[]{:S(2)}) collective-permute-start(bf16[256,768]{1,0:T(8,128)(2,1)} %get-tuple-element.48.refs_0_), channel_id=1, source_target_pairs={{64,0},{68,4},{72,8},{76,12},{80,16},{84,20},{88,24},{92,28},{96,3... | collective-permute-start | bytes 1179656 | tf_op jit(solution)/shard_map/ppermute | solution.py:54
  26.7 0.8 copy-done.4
  27.5 1.8 %unpack.1 = bf16[256,768]{1,0:T(8,128)(2,1)} custom-call(bf16[64,3072]{1,0:T(8,128)(2,1)} %copy-done.4), custom_call_target="tpu_custom_call" | custom-call | flops 1 | bytes 1 | tf_op jit(solution)/shard_map/unpack/pallas_call | solution.py:63
  29.3 3.6 %all-to-all-start = ((bf16[4,64,768]{2,1,0:T(8,128)(2,1)}), bf16[4,64,768]{2,1,0:T(8,128)(2,1)S(1)}, u32[]{:S(2)}, u32[]{:S(2)}) async-start(bf16[4,64,768]{2,1,0:T(8,128)(2,1)} %bitcast.4), calls=%async_computation | async-start | bytes 786432 | tf_op jit(solution)/shard_map/all_to_all | solution.py:354
  32.9 3.0 %collective-permute-start.12 = (bf16[256,768]{1,0:T(8,128)(2,1)S(1)}, bf16[256,768]{1,0:T(8,128)(2,1)S(1)}, u32[]{:S(2)}, u32[]{:S(2)}) collective-permute-start(bf16[256,768]{1,0:T(8,128)(2,1)S(1)} %copy-done.1), channel_id=1, source_target_pairs={{4,0},{0,4},{12,8},{8,12},{20,16},{16,20},{28,24},{24,28},{36,32},... | collective-permute-start | bytes 1179656 | tf_op jit(solution)/shard_map/ppermute | solution.py:54
  36.2 0.7 collective-permute-done.8.refs_1_
  36.9 2.5 %all-to-all-done = bf16[4,64,768]{2,1,0:T(8,128)(2,1)S(1)} async-done(((bf16[4,64,768]{2,1,0:T(8,128)(2,1)}), bf16[4,64,768]{2,1,0:T(8,128)(2,1)S(1)}, u32[]{:S(2)}, u32[]{:S(2)}) %all-to-all-start) | async-done | bytes 393248 | tf_op jit(solution)/shard_map/all_to_all | solution.py:354
  39.4 3.9 %collective-permute-start.10 = (bf16[256,768]{1,0:T(8,128)(2,1)S(1)}, bf16[256,768]{1,0:T(8,128)(2,1)S(1)}, u32[]{:S(2)}, u32[]{:S(2)}) collective-permute-start(bf16[256,768]{1,0:T(8,128)(2,1)S(1)} %collective-permute-done.7.refs_0_), channel_id=1, source_target_pairs={{4,0},{0,4},{12,8},{8,12},{20,16},{16,20},{28,24},{24,28},{36,32},... | collective-permute-start | bytes 1179656 | tf_op jit(solution)/shard_map/ppermute | solution.py:54
  43.3 4.1 %collective-permute-done.5.refs_3_ = bf16[256,768]{1,0:T(8,128)(2,1)S(1)} collective-permute-done((bf16[256,768]{1,0:T(8,128)(2,1)}, bf16[256,768]{1,0:T(8,128)(2,1)S(1)}, u32[]{:S(2)}, u32[]{:S(2)}) %collective-permute-start.5) | collective-permute-done | bytes 393248 | tf_op jit(solution)/shard_map/ppermute | solution.py:54
  47.5 1.3 %collective-permute-start.4 = (bf16[256,768]{1,0:T(8,128)(2,1)S(1)}, bf16[256,768]{1,0:T(8,128)(2,1)S(1)}, u32[]{:S(2)}, u32[]{:S(2)}) collective-permute-start(bf16[256,768]{1,0:T(8,128)(2,1)S(1)} %get-tuple-element.58), channel_id=1, source_target_pairs={{16,0},{20,4},{24,8},{28,12},{32,16},{36,20},{40,24},{44,28},{48,3... | collective-permute-start | bytes 1179656 | tf_op jit(solution)/shard_map/ppermute | solution.py:54
  48.8 1.2 %collective-permute-start.6 = (bf16[256,768]{1,0:T(8,128)(2,1)S(1)}, bf16[256,768]{1,0:T(8,128)(2,1)S(1)}, u32[]{:S(2)}, u32[]{:S(2)}) collective-permute-start(bf16[256,768]{1,0:T(8,128)(2,1)S(1)} %get-tuple-element.57), channel_id=1, source_target_pairs={{48,0},{52,4},{56,8},{60,12},{0,16},{4,20},{8,24},{12,28},{16,32},... | collective-permute-start | bytes 1179656 | tf_op jit(solution)/shard_map/ppermute | solution.py:54
  50.1 2.0 %attend4.2 = (f32[256,128]{1,0:T(8,128)S(1)}, f32[256,384]{1,0:T(8,128)S(1)}) custom-call(s32[1,64]{1,0:T(1,128)S(1)} %copy-done.3, bf16[256,384]{1,0:T(8,128)(2,1)S(1)} %copy-done, bf16[256,768]{1,0:T(8,128)(2,1)S(1)} %copy-done.1, bf16[256,768]{1,0:T(8,128)(2,1)S(1)} %collective-permute-done.12.refs_1_, ...), custom_call_target="tpu_custom_call" | custom-call | flops 1 | bytes 1 | tf_op jit(solution)/shard_map/attend4/pallas_call | solution.py:331
  52.1 2.7 %collective-permute-start.15 = (bf16[256,768]{1,0:T(8,128)(2,1)S(1)}, bf16[256,768]{1,0:T(8,128)(2,1)S(1)}, u32[]{:S(2)}, u32[]{:S(2)}) collective-permute-start(bf16[256,768]{1,0:T(8,128)(2,1)S(1)} %copy-done.1), channel_id=1, source_target_pairs={{128,0},{132,4},{136,8},{140,12},{144,16},{148,20},{152,24},{156,2... | collective-permute-start | bytes 1179656 | tf_op jit(solution)/shard_map/ppermute | solution.py:54
  54.8 2.8 %attend5.1 = (f32[256,128]{1,0:T(8,128)S(1)}, f32[256,384]{1,0:T(8,128)S(1)}) custom-call(s32[1,64]{1,0:T(1,128)S(1)} %copy-done.3, bf16[256,384]{1,0:T(8,128)(2,1)S(1)} %copy-done, bf16[256,768]{1,0:T(8,128)(2,1)S(1)} %collective-permute-done.7.refs_0_, bf16[256,768]{1,0:T(8,128)(2,1)S(1)} %collective-permute-done.8.refs_1_, ...), custom_call_target="tpu_custom_call" | custom-call | flops 1 | bytes 1 | tf_op jit(solution)/shard_map/attend5/pallas_call | solution.py:331
  57.6 7.7 %collective-permute-done.4.refs_2_ = bf16[256,768]{1,0:T(8,128)(2,1)S(1)} collective-permute-done((bf16[256,768]{1,0:T(8,128)(2,1)S(1)}, bf16[256,768]{1,0:T(8,128)(2,1)S(1)}, u32[]{:S(2)}, u32[]{:S(2)}) %collective-permute-start.4) | collective-permute-done | bytes 393248 | tf_op jit(solution)/shard_map/ppermute | solution.py:54
  65.3 4.4 %collective-permute-done.6.refs_3_ = bf16[256,768]{1,0:T(8,128)(2,1)S(1)} collective-permute-done((bf16[256,768]{1,0:T(8,128)(2,1)S(1)}, bf16[256,768]{1,0:T(8,128)(2,1)S(1)}, u32[]{:S(2)}, u32[]{:S(2)}) %collective-permute-start.6) | collective-permute-done | bytes 393248 | tf_op jit(solution)/shard_map/ppermute | solution.py:54
  69.7 1.1 %collective-permute-start.13 = (bf16[256,768]{1,0:T(8,128)(2,1)S(1)}, bf16[256,768]{1,0:T(8,128)(2,1)S(1)}, u32[]{:S(2)}, u32[]{:S(2)}) collective-permute-start(bf16[256,768]{1,0:T(8,128)(2,1)S(1)} %collective-permute-done.6.refs_3_), channel_id=1, source_target_pairs={{4,0},{0,4},{12,8},{8,12},{20,16},{16,20},{28,24},{24,28},{36,32},... | collective-permute-start | bytes 1179656 | tf_op jit(solution)/shard_map/ppermute | solution.py:54
  70.8 2.5 %attend4.3 = (f32[256,128]{1,0:T(8,128)S(1)}, f32[256,384]{1,0:T(8,128)S(1)}) custom-call(s32[1,64]{1,0:T(1,128)S(1)} %copy-done.3, bf16[256,384]{1,0:T(8,128)(2,1)S(1)} %copy-done, bf16[256,768]{1,0:T(8,128)(2,1)S(1)} %collective-permute-done.15.refs_0_, bf16[256,768]{1,0:T(8,128)(2,1)S(1)} %collective-permute-done.16.refs_1_, ...), custom_call_target="tpu_custom_call" | custom-call | flops 1 | bytes 1 | tf_op jit(solution)/shard_map/attend4/pallas_call | solution.py:331
  73.3 2.2 %attend1.1 = (bf16[64,384]{1,0:T(8,128)(2,1)S(1)}, bf16[64,384]{1,0:T(8,128)(2,1)S(1)}, bf16[64,384]{1,0:T(8,128)(2,1)S(1)}, bf16[64,384]{1,0:T(8,128)(2,1)S(1)}) custom-call(s32[1,64]{1,0:T(1,128)S(1)} %copy-done.3, bf16[256,384]{1,0:T(8,128)(2,1)S(1)} %copy-done, bf16[256,768]{1,0:T(8,128)(2,1)S(1)} %collective-permute-done.13.refs_0_, ...), custom_call_target="tpu_custom_call" | custom-call | flops 1 | bytes 1 | tf_op jit(solution)/shard_map/attend1/pallas_call | solution.py:331
  76.4 2.0 %collective-permute-start.18 = (bf16[64,384]{1,0:T(8,128)(2,1)S(1)}, bf16[64,384]{1,0:T(8,128)(2,1)S(1)}, u32[]{:S(2)}, u32[]{:S(2)}) collective-permute-start(bf16[64,384]{1,0:T(8,128)(2,1)S(1)} %get-tuple-element.55), channel_id=1, source_target_pairs={{2,0},{3,1},{0,2},{1,3},{6,4},{7,5},{4,6},{5,7},{10,8},{11,9},{8,1... | collective-permute-start | bytes 147464 | tf_op jit(solution)/shard_map/ppermute | solution.py:147
  78.8 1.5 %collective-permute-done.17.p1 = bf16[64,384]{1,0:T(8,128)(2,1)S(1)} collective-permute-done((bf16[64,384]{1,0:T(8,128)(2,1)S(1)}, bf16[64,384]{1,0:T(8,128)(2,1)S(1)}, u32[]{:S(2)}, u32[]{:S(2)}) %collective-permute-start.17) | collective-permute-done | bytes 49184 | tf_op jit(solution)/shard_map/ppermute | solution.py:147
  80.9 0.8 collective-permute-done.19.p3
  82.3 1.6 %place.1 = bf16[64,1536]{1,0:T(8,128)(2,1)} custom-call(bf16[64,384]{1,0:T(8,128)(2,1)} %copy-done.2, bf16[64,384]{1,0:T(8,128)(2,1)} %copy-done.8, bf16[64,384]{1,0:T(8,128)(2,1)} %copy-done.9, bf16[64,384]{1,0:T(8,128)(2,1)} %copy-done.10), custom_call_target="tpu_custom_call" | custom-call | flops 1 | bytes 1 | tf_op jit(solution)/shard_map/place/pallas_call | solution.py:63
  (41 shorter events, 3.7 us)
Async XLA Ops:
  2.1 24.6 %collective-permute-start.9 = (bf16[64,3072]{1,0:T(8,128)(2,1)}, bf16[64,3072]{1,0:T(8,128)(2,1)S(1)}, u32[]{:S(2)}, u32[]{:S(2)}) collective-permute-start(bf16[64,3072]{1,0:T(8,128)(2,1)} %get-tuple-element.37), channel_id=1, source_target_pairs={{32,0},{36,4},{40,8},{44,12},{48,16},{52,20},{56,24},{60,28},{0,32... | collective-permute-start | bytes 1179656 | tf_op jit(solution)/shard_map/ppermute | solution.py:54
  9.9 5.9 %collective-permute-start = (bf16[64,1152]{1,0:T(8,128)(2,1)}, bf16[64,1152]{1,0:T(8,128)(2,1)S(1)}, u32[]{:S(2)}, u32[]{:S(2)}) collective-permute-start(bf16[64,1152]{1,0:T(8,128)(2,1)} %get-tuple-element.32), channel_id=1, source_target_pairs={{3,0},{0,1},{1,2},{2,3},{7,4},{4,5},{5,6},{6,7},{11,8},{8,9},{9,10... | collective-permute-start | bytes 442376 | tf_op jit(solution)/shard_map/ppermute | solution.py:147
  11.2 8.9 %collective-permute-start.1 = (bf16[64,1152]{1,0:T(8,128)(2,1)}, bf16[64,1152]{1,0:T(8,128)(2,1)S(1)}, u32[]{:S(2)}, u32[]{:S(2)}) collective-permute-start(bf16[64,1152]{1,0:T(8,128)(2,1)} %get-tuple-element.33), channel_id=1, source_target_pairs={{2,0},{3,1},{0,2},{1,3},{6,4},{7,5},{4,6},{5,7},{10,8},{11,9},{8,1... | collective-permute-start | bytes 442376 | tf_op jit(solution)/shard_map/ppermute | solution.py:147
  13.8 6.3 %collective-permute-start.2 = (bf16[64,1152]{1,0:T(8,128)(2,1)}, bf16[64,1152]{1,0:T(8,128)(2,1)S(1)}, u32[]{:S(2)}, u32[]{:S(2)}) collective-permute-start(bf16[64,1152]{1,0:T(8,128)(2,1)} %get-tuple-element.34), channel_id=1, source_target_pairs={{1,0},{2,1},{3,2},{0,3},{5,4},{6,5},{7,6},{4,7},{9,8},{10,9},{11,1... | collective-permute-start | bytes 442376 | tf_op jit(solution)/shard_map/ppermute | solution.py:147
  15.8 4.3 %copy-start.5 = (bf16[64,1152]{1,0:T(8,128)(2,1)}, bf16[64,1152]{1,0:T(8,128)(2,1)S(1)}, u32[]{:S(2)}) copy-start(bf16[64,1152]{1,0:T(8,128)(2,1)S(1)} %collective-permute-done.p1) | copy-start | bytes 442372
  20.1 0.7 copy-start.6
  20.1 0.7 copy-start.7
  22.8 13.4 %collective-permute-start.7 = (bf16[256,768]{1,0:T(8,128)(2,1)}, bf16[256,768]{1,0:T(8,128)(2,1)S(1)}, u32[]{:S(2)}, u32[]{:S(2)}) collective-permute-start(bf16[256,768]{1,0:T(8,128)(2,1)} %get-tuple-element.48.refs_0_), channel_id=1, source_target_pairs={{8,0},{12,4},{16,8},{20,12},{24,16},{28,20},{32,24},{36,28},{40,32... | collective-permute-start | bytes 1179656 | tf_op jit(solution)/shard_map/ppermute | solution.py:54
  24.8 12.1 %collective-permute-start.8 = (bf16[256,768]{1,0:T(8,128)(2,1)}, bf16[256,768]{1,0:T(8,128)(2,1)S(1)}, u32[]{:S(2)}, u32[]{:S(2)}) collective-permute-start(bf16[256,768]{1,0:T(8,128)(2,1)} %get-tuple-element.48.refs_0_), channel_id=1, source_target_pairs={{248,0},{252,4},{0,8},{4,12},{8,16},{12,20},{16,24},{20,28},{24,32... | collective-permute-start | bytes 1179656 | tf_op jit(solution)/shard_map/ppermute | solution.py:54
  24.8 18.5 %collective-permute-start.3 = (bf16[256,768]{1,0:T(8,128)(2,1)}, bf16[256,768]{1,0:T(8,128)(2,1)S(1)}, u32[]{:S(2)}, u32[]{:S(2)}) collective-permute-start(bf16[256,768]{1,0:T(8,128)(2,1)} %get-tuple-element.48.refs_0_), channel_id=1, source_target_pairs={{64,0},{68,4},{72,8},{76,12},{80,16},{84,20},{88,24},{92,28},{96,3... | collective-permute-start | bytes 1179656 | tf_op jit(solution)/shard_map/ppermute | solution.py:54
  26.7 20.7 %collective-permute-start.5 = (bf16[256,768]{1,0:T(8,128)(2,1)}, bf16[256,768]{1,0:T(8,128)(2,1)S(1)}, u32[]{:S(2)}, u32[]{:S(2)}) collective-permute-start(bf16[256,768]{1,0:T(8,128)(2,1)} %get-tuple-element.48.refs_0_), channel_id=1, source_target_pairs={{192,0},{196,4},{200,8},{204,12},{208,16},{212,20},{216,24},{220,2... | collective-permute-start | bytes 1179656 | tf_op jit(solution)/shard_map/ppermute | solution.py:54
  26.7 0.8 copy-start.4
  29.3 3.6 %copy-start.1 = (bf16[256,768]{1,0:T(8,128)(2,1)S(1)}, bf16[256,768]{1,0:T(8,128)(2,1)}, u32[]{:S(2)}) copy-start(bf16[256,768]{1,0:T(8,128)(2,1)} %get-tuple-element.48.refs_0_) | copy-start | bytes 1179652
  29.3 10.1 %all-to-all-start = ((bf16[4,64,768]{2,1,0:T(8,128)(2,1)}), bf16[4,64,768]{2,1,0:T(8,128)(2,1)S(1)}, u32[]{:S(2)}, u32[]{:S(2)}) async-start(bf16[4,64,768]{2,1,0:T(8,128)(2,1)} %bitcast.4), calls=%async_computation | async-start | bytes 786432 | tf_op jit(solution)/shard_map/all_to_all | solution.py:354
  32.9 17.0 %collective-permute-start.12 = (bf16[256,768]{1,0:T(8,128)(2,1)S(1)}, bf16[256,768]{1,0:T(8,128)(2,1)S(1)}, u32[]{:S(2)}, u32[]{:S(2)}) collective-permute-start(bf16[256,768]{1,0:T(8,128)(2,1)S(1)} %copy-done.1), channel_id=1, source_target_pairs={{4,0},{0,4},{12,8},{8,12},{20,16},{16,20},{28,24},{24,28},{36,32},... | collective-permute-start | bytes 1179656 | tf_op jit(solution)/shard_map/ppermute | solution.py:54
  39.4 10.6 %copy-start = (bf16[256,384]{1,0:T(8,128)(2,1)S(1)}, bf16[256,384]{1,0:T(8,128)(2,1)}, u32[]{:S(2)}) copy-start(bf16[256,384]{1,0:T(8,128)(2,1)} %get-tuple-element.35.q_ref) | copy-start | bytes 589828
  39.4 12.7 %collective-permute-start.10 = (bf16[256,768]{1,0:T(8,128)(2,1)S(1)}, bf16[256,768]{1,0:T(8,128)(2,1)S(1)}, u32[]{:S(2)}, u32[]{:S(2)}) collective-permute-start(bf16[256,768]{1,0:T(8,128)(2,1)S(1)} %collective-permute-done.7.refs_0_), channel_id=1, source_target_pairs={{4,0},{0,4},{12,8},{8,12},{20,16},{16,20},{28,24},{24,28},{36,32},... | collective-permute-start | bytes 1179656 | tf_op jit(solution)/shard_map/ppermute | solution.py:54
  43.3 11.5 %collective-permute-start.11 = (bf16[256,768]{1,0:T(8,128)(2,1)S(1)}, bf16[256,768]{1,0:T(8,128)(2,1)S(1)}, u32[]{:S(2)}, u32[]{:S(2)}) collective-permute-start(bf16[256,768]{1,0:T(8,128)(2,1)S(1)} %collective-permute-done.8.refs_1_), channel_id=1, source_target_pairs={{4,0},{0,4},{12,8},{8,12},{20,16},{16,20},{28,24},{24,28},{36,32},... | collective-permute-start | bytes 1179656 | tf_op jit(solution)/shard_map/ppermute | solution.py:54
  47.5 17.8 %collective-permute-start.4 = (bf16[256,768]{1,0:T(8,128)(2,1)S(1)}, bf16[256,768]{1,0:T(8,128)(2,1)S(1)}, u32[]{:S(2)}, u32[]{:S(2)}) collective-permute-start(bf16[256,768]{1,0:T(8,128)(2,1)S(1)} %get-tuple-element.58), channel_id=1, source_target_pairs={{16,0},{20,4},{24,8},{28,12},{32,16},{36,20},{40,24},{44,28},{48,3... | collective-permute-start | bytes 1179656 | tf_op jit(solution)/shard_map/ppermute | solution.py:54
  48.8 1.3 %copy-start.3 = (s32[1,64]{1,0:T(1,128)S(1)}, s32[1,64]{1,0:T(1,128)}, u32[]{:S(2)}) copy-start(s32[1,64]{1,0:T(1,128)} %band_ref.7) | copy-start | bytes 772
  48.8 20.9 %collective-permute-start.6 = (bf16[256,768]{1,0:T(8,128)(2,1)S(1)}, bf16[256,768]{1,0:T(8,128)(2,1)S(1)}, u32[]{:S(2)}, u32[]{:S(2)}) collective-permute-start(bf16[256,768]{1,0:T(8,128)(2,1)S(1)} %get-tuple-element.57), channel_id=1, source_target_pairs={{48,0},{52,4},{56,8},{60,12},{0,16},{4,20},{8,24},{12,28},{16,32},... | collective-permute-start | bytes 1179656 | tf_op jit(solution)/shard_map/ppermute | solution.py:54
  49.9 20.9 %collective-permute-start.16 = (bf16[256,768]{1,0:T(8,128)(2,1)S(1)}, bf16[256,768]{1,0:T(8,128)(2,1)S(1)}, u32[]{:S(2)}, u32[]{:S(2)}) collective-permute-start(bf16[256,768]{1,0:T(8,128)(2,1)S(1)} %bitcast.2), channel_id=1, source_target_pairs={{192,0},{196,4},{200,8},{204,12},{208,16},{212,20},{216,24},{220,2... | collective-permute-start | bytes 1179656 | tf_op jit(solution)/shard_map/ppermute | solution.py:54
  52.1 18.7 %collective-permute-start.15 = (bf16[256,768]{1,0:T(8,128)(2,1)S(1)}, bf16[256,768]{1,0:T(8,128)(2,1)S(1)}, u32[]{:S(2)}, u32[]{:S(2)}) collective-permute-start(bf16[256,768]{1,0:T(8,128)(2,1)S(1)} %copy-done.1), channel_id=1, source_target_pairs={{128,0},{132,4},{136,8},{140,12},{144,16},{148,20},{152,24},{156,2... | collective-permute-start | bytes 1179656 | tf_op jit(solution)/shard_map/ppermute | solution.py:54
  69.7 3.6 %collective-permute-start.13 = (bf16[256,768]{1,0:T(8,128)(2,1)S(1)}, bf16[256,768]{1,0:T(8,128)(2,1)S(1)}, u32[]{:S(2)}, u32[]{:S(2)}) collective-permute-start(bf16[256,768]{1,0:T(8,128)(2,1)S(1)} %collective-permute-done.6.refs_3_), channel_id=1, source_target_pairs={{4,0},{0,4},{12,8},{8,12},{20,16},{16,20},{28,24},{24,28},{36,32},... | collective-permute-start | bytes 1179656 | tf_op jit(solution)/shard_map/ppermute | solution.py:54
  70.8 2.5 %collective-permute-start.14 = (bf16[256,768]{1,0:T(8,128)(2,1)S(1)}, bf16[256,768]{1,0:T(8,128)(2,1)S(1)}, u32[]{:S(2)}, u32[]{:S(2)}) collective-permute-start(bf16[256,768]{1,0:T(8,128)(2,1)S(1)} %collective-permute-done.4.refs_2_), channel_id=1, source_target_pairs={{4,0},{0,4},{12,8},{8,12},{20,16},{16,20},{28,24},{24,28},{36,32},... | collective-permute-start | bytes 1179656 | tf_op jit(solution)/shard_map/ppermute | solution.py:54
  75.5 0.6 copy-start.2
  76.2 4.2 %collective-permute-start.17 = (bf16[64,384]{1,0:T(8,128)(2,1)S(1)}, bf16[64,384]{1,0:T(8,128)(2,1)S(1)}, u32[]{:S(2)}, u32[]{:S(2)}) collective-permute-start(bf16[64,384]{1,0:T(8,128)(2,1)S(1)} %get-tuple-element.54), channel_id=1, source_target_pairs={{3,0},{0,1},{1,2},{2,3},{7,4},{4,5},{5,6},{6,7},{11,8},{8,9},{9,10... | collective-permute-start | bytes 147464 | tf_op jit(solution)/shard_map/ppermute | solution.py:147
  76.4 4.5 %collective-permute-start.18 = (bf16[64,384]{1,0:T(8,128)(2,1)S(1)}, bf16[64,384]{1,0:T(8,128)(2,1)S(1)}, u32[]{:S(2)}, u32[]{:S(2)}) collective-permute-start(bf16[64,384]{1,0:T(8,128)(2,1)S(1)} %get-tuple-element.55), channel_id=1, source_target_pairs={{2,0},{3,1},{0,2},{1,3},{6,4},{7,5},{4,6},{5,7},{10,8},{11,9},{8,1... | collective-permute-start | bytes 147464 | tf_op jit(solution)/shard_map/ppermute | solution.py:147
  78.4 3.3 %collective-permute-start.19 = (bf16[64,384]{1,0:T(8,128)(2,1)S(1)}, bf16[64,384]{1,0:T(8,128)(2,1)S(1)}, u32[]{:S(2)}, u32[]{:S(2)}) collective-permute-start(bf16[64,384]{1,0:T(8,128)(2,1)S(1)} %get-tuple-element.56), channel_id=1, source_target_pairs={{1,0},{2,1},{3,2},{0,3},{5,4},{6,5},{7,6},{4,7},{9,8},{10,9},{11,1... | collective-permute-start | bytes 147464 | tf_op jit(solution)/shard_map/ppermute | solution.py:147
  80.3 1.4 %copy-start.8 = (bf16[64,384]{1,0:T(8,128)(2,1)}, bf16[64,384]{1,0:T(8,128)(2,1)S(1)}, u32[]{:S(2)}) copy-start(bf16[64,384]{1,0:T(8,128)(2,1)S(1)} %collective-permute-done.17.p1) | copy-start | bytes 147460
  80.9 0.8 copy-start.9
  81.7 0.6 copy-start.10

commit v2 on v1

--- a/solution.py
+++ b/solution.py
@@ -357,8 +357,6 @@
         blocks = {k: b if isinstance(b, tuple) else ("joint", b) for k, b in blocks.items()}
         return attend(band, q, blocks, state, last)
 
-    state = step(None, own=own, partner=partner, xnext=xnext, xprev=xprev)
-
     z = (lax.axis_index("frame") // CS) % ZS
     next2 = move(jnp.where(z < 2, xnext, own), from_z(2))
     prev2 = move(jnp.where(z >= ZS - 2, xprev, own), from_z(-2))
@@ -366,12 +364,17 @@
     sent, sent1, sent2, *_ = barrier((own, next1, prev1, z4))
     x2 = move(sent, from_x(2))
     next1p, prev1p = move(sent1, FROM_PARTNER), move(sent2, FROM_PARTNER)
-    state = step(state, next1=next1, prev1=prev1, next1p=next1p, prev1p=prev1p, z4=z4)
-
-    next2, prev2, state = barrier((next2, prev2, state))
-    next2p, prev2p = move(next2, FROM_PARTNER), move(prev2, FROM_PARTNER)
-    state = step(state, x2=x2, z4x=z4x, next2=next2, prev2=prev2)
-    outs = step(state, True, far2p=("choice", prev2p, next2p))
+    next2, prev2, z4x, x2 = barrier((next2, prev2, z4x, x2))
+    next2p = move(next2, FROM_PARTNER)
+    sent, _ = barrier((prev2, next2p))
+    prev2p = move(sent, FROM_PARTNER)
+    state = step(None, own=own, xnext=xnext, xprev=xprev, z4=z4)
+    state = step(
+        state, partner=partner, next1=next1, prev1=prev1, next1p=next1p, prev1p=prev1p
+    )
+    outs = step(
+        state, True, x2=x2, z4x=z4x, next2=next2, prev2=prev2, far2p=("choice", prev2p, next2p)
+    )
     return place(over_heads(outs))
 
 

time: 84.4 us -> 84.6 us (level)
  starting transfers between devices: 36.2 us -> 45.6 us
  waiting for transfers between devices: 27.8 us -> 19.2 us
  Pallas kernels: 17 us -> 15.4 us
  other arithmetic: 0.07 us -> 0.98 us
    ppermute x14, starting transfers between devices: 24.9 us -> 31.3 us  [move(): return lax.ppermute(block, 'frame', pairs)]
    ppermute x6, waiting for transfers between devices: 8.1 us -> 2.05 us  [over_heads(): lax.ppermute(pieces[s], 'head', y_from(s))]
    ppermute x6, starting transfers between devices: 7.66 us -> 10.7 us  [over_heads(): lax.ppermute(pieces[s], 'head', y_from(s))]
    all_to_all x1, waiting for transfers between devices: 2.54 us -> 0.01 us  [shards(): lax.all_to_all(z4_packed, 'head', split_axis=0, concat_axis=0, tiled=True)]
    pallas_call x4 -> x3, Pallas kernels: 9.48 us -> 7.93 us  [attend(): pl.pallas_call(functools.partial(attend_kernel, names, kinds, first, last...]
    select_n x1, other arithmetic: 0.07 us -> 0.98 us  [shards(): prev2 = move(jnp.where(z >= ZS - 2, xprev, own), from_z(-2))]
  transfers between devices with their start and end apart: 21 -> 21, of which waited for: 11 -> 6; matrix products, arithmetic and copies ran while one was open for 0% -> 1% of each run, Pallas kernels for 13% -> 11%
where the time goes in v2:
time: 84.6 us; the launch traced here: 84.1 us
  starting transfers between devices  45.6 us (54%)
  waiting for transfers between devices  19.2 us (23%)
  Pallas kernels  15.4 us (18%)
  local copies, waits for them, and re-layouts  2.74 us (3%)
  other arithmetic  0.98 us (1%)
    ppermute x14, starting transfers between devices, move(): return lax.ppermute(block, 'frame', pairs)  31.3 us
    ppermute x14, waiting for transfers between devices, move(): return lax.ppermute(block, 'frame', pairs)  17.2 us
    ppermute x6, starting transfers between devices, over_heads(): lax.ppermute(pieces[s], 'head', y_from(s))  10.7 us
    pallas_call x3, Pallas kernels, attend(): pl.pallas_call(functools.partial(attend_kernel, names, kinds, first, last...  7.93 us
    pallas_call x4, Pallas kernels, copier(): pl.pallas_call(kernel, out_shape=out_shape, in_specs=[VMEM] * len(arrays)...  7.49 us
    all_to_all x1, starting transfers between devices, shards(): lax.all_to_all(z4_packed, 'head', split_axis=0, concat_axis=0, tiled=True)  3.59 us
    unnamed x22, local copies, waits for them, and re-layouts  2.74 us
    ppermute x6, waiting for transfers between devices, over_heads(): lax.ppermute(pieces[s], 'head', y_from(s))  2.05 us
  transfers between devices with their start and end apart: 21, of which 6 were waited for; matrix products, arithmetic and copies ran while one was open for 1% of the time, Pallas kernels for 11%

profile of v2, /device:TPU:1, one launch (start us, length us, event | category | flops | bytes accessed | tf_op | source)
XLA Modules:
  0.0 84.1 jit_solution(8612995286499107613)
XLA Ops:
  0.0 2.1 %pack.1 = (bf16[64,1152]{1,0:T(8,128)(2,1)}, bf16[64,1152]{1,0:T(8,128)(2,1)}, bf16[64,1152]{1,0:T(8,128)(2,1)}, bf16[64,1152]{1,0:T(8,128)(2,1)}, bf16[64,3072]{1,0:T(8,128)(2,1)}) custom-call(bf16[64,1536]{1,0:T(8,128)(2,1)} %k_ref.1, bf16[64,1536]{1,0:T(8,128)(2,1)} %v_ref.1, bf16[64,1536]{1,0:T(8,128)(2,1)} %q_ref.1), custom_call_target="tpu_custom_call" | custom-call | flops 1 | bytes 1 | tf_op jit(solution)/shard_map/pack/pallas_call | solution.py:63
  2.1 2.1 %collective-permute-start = (bf16[64,1152]{1,0:T(8,128)(2,1)}, bf16[64,1152]{1,0:T(8,128)(2,1)S(1)}, u32[]{:S(2)}, u32[]{:S(2)}) collective-permute-start(bf16[64,1152]{1,0:T(8,128)(2,1)} %get-tuple-element.31), channel_id=1, source_target_pairs={{3,0},{0,1},{1,2},{2,3},{7,4},{4,5},{5,6},{6,7},{11,8},{8,9},{9,10... | collective-permute-start | bytes 442376 | tf_op jit(solution)/shard_map/ppermute | solution.py:147
  4.3 2.6 %collective-permute-start.1 = (bf16[64,1152]{1,0:T(8,128)(2,1)}, bf16[64,1152]{1,0:T(8,128)(2,1)S(1)}, u32[]{:S(2)}, u32[]{:S(2)}) collective-permute-start(bf16[64,1152]{1,0:T(8,128)(2,1)} %get-tuple-element.32), channel_id=1, source_target_pairs={{2,0},{3,1},{0,2},{1,3},{6,4},{7,5},{4,6},{5,7},{10,8},{11,9},{8,1... | collective-permute-start | bytes 442376 | tf_op jit(solution)/shard_map/ppermute | solution.py:147
  6.9 1.1 %collective-permute-start.2 = (bf16[64,1152]{1,0:T(8,128)(2,1)}, bf16[64,1152]{1,0:T(8,128)(2,1)S(1)}, u32[]{:S(2)}, u32[]{:S(2)}) collective-permute-start(bf16[64,1152]{1,0:T(8,128)(2,1)} %get-tuple-element.33), channel_id=1, source_target_pairs={{1,0},{2,1},{3,2},{0,3},{5,4},{6,5},{7,6},{4,7},{9,8},{10,9},{11,1... | collective-permute-start | bytes 442376 | tf_op jit(solution)/shard_map/ppermute | solution.py:147
  8.0 6.9 %collective-permute-start.7 = (bf16[64,3072]{1,0:T(8,128)(2,1)}, bf16[64,3072]{1,0:T(8,128)(2,1)S(1)}, u32[]{:S(2)}, u32[]{:S(2)}) collective-permute-start(bf16[64,3072]{1,0:T(8,128)(2,1)} %get-tuple-element.36), channel_id=1, source_target_pairs={{32,0},{36,4},{40,8},{44,12},{48,16},{52,20},{56,24},{60,28},{0,32... | collective-permute-start | bytes 1179656 | tf_op jit(solution)/shard_map/ppermute | solution.py:54
  14.9 0.6 copy-done.5
  15.6 2.0 %join.1 = (bf16[256,768]{1,0:T(8,128)(2,1)}, bf16[256,384]{1,0:T(8,128)(2,1)}) custom-call(bf16[64,1152]{1,0:T(8,128)(2,1)} %get-tuple-element.30.p0, bf16[64,1152]{1,0:T(8,128)(2,1)} %copy-done.5, bf16[64,1152]{1,0:T(8,128)(2,1)} %copy-done.6, bf16[64,1152]{1,0:T(8,128)(2,1)} %copy-done.7), custom_call_target="tpu_custom_call" | custom-call | flops 1 | bytes 1 | tf_op jit(solution)/shard_map/join/pallas_call | solution.py:63
  17.6 2.5 %collective-permute-start.3 = (bf16[256,768]{1,0:T(8,128)(2,1)}, bf16[256,768]{1,0:T(8,128)(2,1)S(1)}, u32[]{:S(2)}, u32[]{:S(2)}) collective-permute-start(bf16[256,768]{1,0:T(8,128)(2,1)} %get-tuple-element.44.refs_0_), channel_id=1, source_target_pairs={{64,0},{68,4},{72,8},{76,12},{80,16},{84,20},{88,24},{92,28},{96,3... | collective-permute-start | bytes 1179656 | tf_op jit(solution)/shard_map/ppermute | solution.py:54
  20.1 0.7 collective-permute-start.10
  20.9 5.8 %collective-permute-start.9 = (bf16[256,768]{1,0:T(8,128)(2,1)}, bf16[256,768]{1,0:T(8,128)(2,1)S(1)}, u32[]{:S(2)}, u32[]{:S(2)}) collective-permute-start(bf16[256,768]{1,0:T(8,128)(2,1)} %get-tuple-element.44.refs_0_), channel_id=1, source_target_pairs={{8,0},{12,4},{16,8},{20,12},{24,16},{28,20},{32,24},{36,28},{40,32... | collective-permute-start | bytes 1179656 | tf_op jit(solution)/shard_map/ppermute | solution.py:54
  26.7 0.8 copy-done.4
  27.4 1.8 %unpack.1 = bf16[256,768]{1,0:T(8,128)(2,1)} custom-call(bf16[64,3072]{1,0:T(8,128)(2,1)} %copy-done.4), custom_call_target="tpu_custom_call" | custom-call | flops 1 | bytes 1 | tf_op jit(solution)/shard_map/unpack/pallas_call | solution.py:63
  29.2 3.6 %all-to-all-start = ((bf16[4,64,768]{2,1,0:T(8,128)(2,1)}), bf16[4,64,768]{2,1,0:T(8,128)(2,1)S(1)}, u32[]{:S(2)}, u32[]{:S(2)}) async-start(bf16[4,64,768]{2,1,0:T(8,128)(2,1)} %bitcast.4), calls=%async_computation | async-start | bytes 786432 | tf_op jit(solution)/shard_map/all_to_all | solution.py:354
  32.9 1.0 %broadcast_select_fusion = (bf16[256,768]{1,0:T(8,128)(2,1)}, bf16[256,768]{1,0:T(8,128)(2,1)}) fusion(bf16[256,768]{1,0:T(8,128)(2,1)S(1)} %collective-permute-done.5.refs_2_, bf16[256,768]{1,0:T(8,128)(2,1)S(1)} %copy-done.1, pred[]{:T(512)S(6)} %ge.3, bf16[256,768]{1,0:T(8,128)(2,1)S(1)} %collective-permute-done.3.refs_1_, pred[]{:T(512)S(6)} %lt.10), kind=kLoop, calls=%fused_computation | loop fusion | flops 393216 | bytes 1966082 | tf_op jit(solution)/shard_map/jit(_where)/select_n | solution.py:362
  33.9 8.9 %collective-permute-start.4 = (bf16[256,768]{1,0:T(8,128)(2,1)}, bf16[256,768]{1,0:T(8,128)(2,1)S(1)}, u32[]{:S(2)}, u32[]{:S(2)}) collective-permute-start(bf16[256,768]{1,0:T(8,128)(2,1)} %get-tuple-element.56), channel_id=1, source_target_pairs={{16,0},{20,4},{24,8},{28,12},{32,16},{36,20},{40,24},{44,28},{48,3... | collective-permute-start | bytes 1179656 | tf_op jit(solution)/shard_map/ppermute | solution.py:54
  43.1 2.6 %collective-permute-start.11 = (bf16[256,768]{1,0:T(8,128)(2,1)S(1)}, bf16[256,768]{1,0:T(8,128)(2,1)S(1)}, u32[]{:S(2)}, u32[]{:S(2)}) collective-permute-start(bf16[256,768]{1,0:T(8,128)(2,1)S(1)} %copy-done.1), channel_id=1, source_target_pairs={{128,0},{132,4},{136,8},{140,12},{144,16},{148,20},{152,24},{156,2... | collective-permute-start | bytes 1179656 | tf_op jit(solution)/shard_map/ppermute | solution.py:54
  46.0 13.1 %collective-permute-done.4.refs_2_ = bf16[256,768]{1,0:T(8,128)(2,1)S(1)} collective-permute-done((bf16[256,768]{1,0:T(8,128)(2,1)}, bf16[256,768]{1,0:T(8,128)(2,1)S(1)}, u32[]{:S(2)}, u32[]{:S(2)}) %collective-permute-start.4) | collective-permute-done | bytes 393248 | tf_op jit(solution)/shard_map/ppermute | solution.py:54
  59.0 3.0 %collective-permute-done.6.refs_3_ = bf16[256,768]{1,0:T(8,128)(2,1)S(1)} collective-permute-done((bf16[256,768]{1,0:T(8,128)(2,1)}, bf16[256,768]{1,0:T(8,128)(2,1)S(1)}, u32[]{:S(2)}, u32[]{:S(2)}) %collective-permute-start.6) | collective-permute-done | bytes 393248 | tf_op jit(solution)/shard_map/ppermute | solution.py:54
  62.1 2.6 %collective-permute-start.12 = (bf16[256,768]{1,0:T(8,128)(2,1)S(1)}, bf16[256,768]{1,0:T(8,128)(2,1)S(1)}, u32[]{:S(2)}, u32[]{:S(2)}) collective-permute-start(bf16[256,768]{1,0:T(8,128)(2,1)S(1)} %collective-permute-done.4.refs_2_), channel_id=1, source_target_pairs={{4,0},{0,4},{12,8},{8,12},{20,16},{16,20},{28,24},{24,28},{36,32},... | collective-permute-start | bytes 1179656 | tf_op jit(solution)/shard_map/ppermute | solution.py:54
  64.7 0.4 collective-permute-start.15
  65.3 0.7 collective-permute-done.12.refs_5_
  66.4 2.1 %attend4.1 = (f32[256,128]{1,0:T(8,128)S(1)}, f32[256,384]{1,0:T(8,128)S(1)}) custom-call(s32[1,64]{1,0:T(1,128)S(1)} %copy-done.3, bf16[256,384]{1,0:T(8,128)(2,1)S(1)} %copy-done, bf16[256,768]{1,0:T(8,128)(2,1)S(1)} %copy-done.1, bf16[256,768]{1,0:T(8,128)(2,1)S(1)} %collective-permute-done.3.refs_1_, ...), custom_call_target="tpu_custom_call" | custom-call | flops 1 | bytes 1 | tf_op jit(solution)/shard_map/attend4/pallas_call | solution.py:331
  68.5 3.0 %attend5.2 = (f32[256,128]{1,0:T(8,128)S(1)}, f32[256,384]{1,0:T(8,128)S(1)}) custom-call(s32[1,64]{1,0:T(1,128)S(1)} %copy-done.3, bf16[256,384]{1,0:T(8,128)(2,1)S(1)} %copy-done, bf16[256,768]{1,0:T(8,128)(2,1)S(1)} %collective-permute-done.14.refs_0_, bf16[256,768]{1,0:T(8,128)(2,1)S(1)} %collective-permute-done.9.refs_1_, ...), custom_call_target="tpu_custom_call" | custom-call | flops 1 | bytes 1 | tf_op jit(solution)/shard_map/attend5/pallas_call | solution.py:331
  71.5 2.9 %attend5.3 = (bf16[64,384]{1,0:T(8,128)(2,1)S(1)}, bf16[64,384]{1,0:T(8,128)(2,1)S(1)}, bf16[64,384]{1,0:T(8,128)(2,1)S(1)}, bf16[64,384]{1,0:T(8,128)(2,1)S(1)}) custom-call(s32[1,64]{1,0:T(1,128)S(1)} %copy-done.3, bf16[256,384]{1,0:T(8,128)(2,1)S(1)} %copy-done, bf16[256,768]{1,0:T(8,128)(2,1)S(1)} %collective-permute-done.11.refs_0_, ...), custom_call_target="tpu_custom_call" | custom-call | flops 1 | bytes 1 | tf_op jit(solution)/shard_map/attend5/pallas_call | solution.py:331
  74.4 0.6 copy-done.2
  75.0 1.3 %collective-permute-start.17 = (bf16[64,384]{1,0:T(8,128)(2,1)S(1)}, bf16[64,384]{1,0:T(8,128)(2,1)S(1)}, u32[]{:S(2)}, u32[]{:S(2)}) collective-permute-start(bf16[64,384]{1,0:T(8,128)(2,1)S(1)} %get-tuple-element.52), channel_id=1, source_target_pairs={{3,0},{0,1},{1,2},{2,3},{7,4},{4,5},{5,6},{6,7},{11,8},{8,9},{9,10... | collective-permute-start | bytes 147464 | tf_op jit(solution)/shard_map/ppermute | solution.py:147
  76.3 2.4 %collective-permute-start.18 = (bf16[64,384]{1,0:T(8,128)(2,1)S(1)}, bf16[64,384]{1,0:T(8,128)(2,1)S(1)}, u32[]{:S(2)}, u32[]{:S(2)}) collective-permute-start(bf16[64,384]{1,0:T(8,128)(2,1)S(1)} %get-tuple-element.53), channel_id=1, source_target_pairs={{2,0},{3,1},{0,2},{1,3},{6,4},{7,5},{4,6},{5,7},{10,8},{11,9},{8,1... | collective-permute-start | bytes 147464 | tf_op jit(solution)/shard_map/ppermute | solution.py:147
  78.7 1.2 %collective-permute-start.19 = (bf16[64,384]{1,0:T(8,128)(2,1)S(1)}, bf16[64,384]{1,0:T(8,128)(2,1)S(1)}, u32[]{:S(2)}, u32[]{:S(2)}) collective-permute-start(bf16[64,384]{1,0:T(8,128)(2,1)S(1)} %get-tuple-element.54), channel_id=1, source_target_pairs={{1,0},{2,1},{3,2},{0,3},{5,4},{6,5},{7,6},{4,7},{9,8},{10,9},{11,1... | collective-permute-start | bytes 147464 | tf_op jit(solution)/shard_map/ppermute | solution.py:147
  79.9 1.3 %collective-permute-done.18.p2 = bf16[64,384]{1,0:T(8,128)(2,1)S(1)} collective-permute-done((bf16[64,384]{1,0:T(8,128)(2,1)S(1)}, bf16[64,384]{1,0:T(8,128)(2,1)S(1)}, u32[]{:S(2)}, u32[]{:S(2)}) %collective-permute-start.18) | collective-permute-done | bytes 49184 | tf_op jit(solution)/shard_map/ppermute | solution.py:147
  81.2 0.7 collective-permute-done.19.p3
  82.0 0.6 copy-done.10
  82.6 1.6 %place.1 = bf16[64,1536]{1,0:T(8,128)(2,1)} custom-call(bf16[64,384]{1,0:T(8,128)(2,1)} %copy-done.2, bf16[64,384]{1,0:T(8,128)(2,1)} %copy-done.8, bf16[64,384]{1,0:T(8,128)(2,1)} %copy-done.9, bf16[64,384]{1,0:T(8,128)(2,1)} %copy-done.10), custom_call_target="tpu_custom_call" | custom-call | flops 1 | bytes 1 | tf_op jit(solution)/shard_map/place/pallas_call | solution.py:63
  (40 shorter events, 1.3 us)
Async XLA Ops:
  2.1 12.7 %collective-permute-start = (bf16[64,1152]{1,0:T(8,128)(2,1)}, bf16[64,1152]{1,0:T(8,128)(2,1)S(1)}, u32[]{:S(2)}, u32[]{:S(2)}) collective-permute-start(bf16[64,1152]{1,0:T(8,128)(2,1)} %get-tuple-element.31), channel_id=1, source_target_pairs={{3,0},{0,1},{1,2},{2,3},{7,4},{4,5},{5,6},{6,7},{11,8},{8,9},{9,10... | collective-permute-start | bytes 442376 | tf_op jit(solution)/shard_map/ppermute | solution.py:147
  4.3 10.6 %collective-permute-start.1 = (bf16[64,1152]{1,0:T(8,128)(2,1)}, bf16[64,1152]{1,0:T(8,128)(2,1)S(1)}, u32[]{:S(2)}, u32[]{:S(2)}) collective-permute-start(bf16[64,1152]{1,0:T(8,128)(2,1)} %get-tuple-element.32), channel_id=1, source_target_pairs={{2,0},{3,1},{0,2},{1,3},{6,4},{7,5},{4,6},{5,7},{10,8},{11,9},{8,1... | collective-permute-start | bytes 442376 | tf_op jit(solution)/shard_map/ppermute | solution.py:147
  6.9 8.0 %collective-permute-start.2 = (bf16[64,1152]{1,0:T(8,128)(2,1)}, bf16[64,1152]{1,0:T(8,128)(2,1)S(1)}, u32[]{:S(2)}, u32[]{:S(2)}) collective-permute-start(bf16[64,1152]{1,0:T(8,128)(2,1)} %get-tuple-element.33), channel_id=1, source_target_pairs={{1,0},{2,1},{3,2},{0,3},{5,4},{6,5},{7,6},{4,7},{9,8},{10,9},{11,1... | collective-permute-start | bytes 442376 | tf_op jit(solution)/shard_map/ppermute | solution.py:147
  8.0 18.7 %collective-permute-start.7 = (bf16[64,3072]{1,0:T(8,128)(2,1)}, bf16[64,3072]{1,0:T(8,128)(2,1)S(1)}, u32[]{:S(2)}, u32[]{:S(2)}) collective-permute-start(bf16[64,3072]{1,0:T(8,128)(2,1)} %get-tuple-element.36), channel_id=1, source_target_pairs={{32,0},{36,4},{40,8},{44,12},{48,16},{52,20},{56,24},{60,28},{0,32... | collective-permute-start | bytes 1179656 | tf_op jit(solution)/shard_map/ppermute | solution.py:54
  14.9 0.7 copy-start.5
  14.9 0.7 copy-start.6
  14.9 0.7 copy-start.7
  17.6 15.2 %collective-permute-start.3 = (bf16[256,768]{1,0:T(8,128)(2,1)}, bf16[256,768]{1,0:T(8,128)(2,1)S(1)}, u32[]{:S(2)}, u32[]{:S(2)}) collective-permute-start(bf16[256,768]{1,0:T(8,128)(2,1)} %get-tuple-element.44.refs_0_), channel_id=1, source_target_pairs={{64,0},{68,4},{72,8},{76,12},{80,16},{84,20},{88,24},{92,28},{96,3... | collective-permute-start | bytes 1179656 | tf_op jit(solution)/shard_map/ppermute | solution.py:54
  20.1 12.8 %collective-permute-start.5 = (bf16[256,768]{1,0:T(8,128)(2,1)}, bf16[256,768]{1,0:T(8,128)(2,1)S(1)}, u32[]{:S(2)}, u32[]{:S(2)}) collective-permute-start(bf16[256,768]{1,0:T(8,128)(2,1)} %get-tuple-element.44.refs_0_), channel_id=1, source_target_pairs={{192,0},{196,4},{200,8},{204,12},{208,16},{212,20},{216,24},{220,2... | collective-permute-start | bytes 1179656 | tf_op jit(solution)/shard_map/ppermute | solution.py:54
  20.1 23.0 %collective-permute-start.10 = (bf16[256,768]{1,0:T(8,128)(2,1)}, bf16[256,768]{1,0:T(8,128)(2,1)S(1)}, u32[]{:S(2)}, u32[]{:S(2)}) collective-permute-start(bf16[256,768]{1,0:T(8,128)(2,1)} %get-tuple-element.44.refs_0_), channel_id=1, source_target_pairs={{248,0},{252,4},{0,8},{4,12},{8,16},{12,20},{16,24},{20,28},{24,32... | collective-permute-start | bytes 1179656 | tf_op jit(solution)/shard_map/ppermute | solution.py:54
  20.9 22.2 %collective-permute-start.9 = (bf16[256,768]{1,0:T(8,128)(2,1)}, bf16[256,768]{1,0:T(8,128)(2,1)S(1)}, u32[]{:S(2)}, u32[]{:S(2)}) collective-permute-start(bf16[256,768]{1,0:T(8,128)(2,1)} %get-tuple-element.44.refs_0_), channel_id=1, source_target_pairs={{8,0},{12,4},{16,8},{20,12},{24,16},{28,20},{32,24},{36,28},{40,32... | collective-permute-start | bytes 1179656 | tf_op jit(solution)/shard_map/ppermute | solution.py:54
  26.7 0.8 copy-start.4
  29.2 3.7 %copy-start.1 = (bf16[256,768]{1,0:T(8,128)(2,1)S(1)}, bf16[256,768]{1,0:T(8,128)(2,1)}, u32[]{:S(2)}) copy-start(bf16[256,768]{1,0:T(8,128)(2,1)} %get-tuple-element.44.refs_0_) | copy-start | bytes 1179652
  29.2 13.9 %all-to-all-start = ((bf16[4,64,768]{2,1,0:T(8,128)(2,1)}), bf16[4,64,768]{2,1,0:T(8,128)(2,1)S(1)}, u32[]{:S(2)}, u32[]{:S(2)}) async-start(bf16[4,64,768]{2,1,0:T(8,128)(2,1)} %bitcast.4), calls=%async_computation | async-start | bytes 786432 | tf_op jit(solution)/shard_map/all_to_all | solution.py:354
  32.9 33.5 %copy-start = (bf16[256,384]{1,0:T(8,128)(2,1)S(1)}, bf16[256,384]{1,0:T(8,128)(2,1)}, u32[]{:S(2)}) copy-start(bf16[256,384]{1,0:T(8,128)(2,1)} %get-tuple-element.34.q_ref) | copy-start | bytes 589828
  33.9 25.2 %collective-permute-start.4 = (bf16[256,768]{1,0:T(8,128)(2,1)}, bf16[256,768]{1,0:T(8,128)(2,1)S(1)}, u32[]{:S(2)}, u32[]{:S(2)}) collective-permute-start(bf16[256,768]{1,0:T(8,128)(2,1)} %get-tuple-element.56), channel_id=1, source_target_pairs={{16,0},{20,4},{24,8},{28,12},{32,16},{36,20},{40,24},{44,28},{48,3... | collective-permute-start | bytes 1179656 | tf_op jit(solution)/shard_map/ppermute | solution.py:54
  42.8 19.3 %collective-permute-start.6 = (bf16[256,768]{1,0:T(8,128)(2,1)}, bf16[256,768]{1,0:T(8,128)(2,1)S(1)}, u32[]{:S(2)}, u32[]{:S(2)}) collective-permute-start(bf16[256,768]{1,0:T(8,128)(2,1)} %get-tuple-element.55), channel_id=1, source_target_pairs={{48,0},{52,4},{56,8},{60,12},{0,16},{4,20},{8,24},{12,28},{16,32},... | collective-permute-start | bytes 1179656 | tf_op jit(solution)/shard_map/ppermute | solution.py:54
  43.1 23.3 %copy-start.3 = (s32[1,64]{1,0:T(1,128)S(1)}, s32[1,64]{1,0:T(1,128)}, u32[]{:S(2)}) copy-start(s32[1,64]{1,0:T(1,128)} %band_ref.5) | copy-start | bytes 772
  43.1 19.0 %collective-permute-start.11 = (bf16[256,768]{1,0:T(8,128)(2,1)S(1)}, bf16[256,768]{1,0:T(8,128)(2,1)S(1)}, u32[]{:S(2)}, u32[]{:S(2)}) collective-permute-start(bf16[256,768]{1,0:T(8,128)(2,1)S(1)} %copy-done.1), channel_id=1, source_target_pairs={{128,0},{132,4},{136,8},{140,12},{144,16},{148,20},{152,24},{156,2... | collective-permute-start | bytes 1179656 | tf_op jit(solution)/shard_map/ppermute | solution.py:54
  45.7 16.4 %collective-permute-start.8 = (bf16[256,768]{1,0:T(8,128)(2,1)S(1)}, bf16[256,768]{1,0:T(8,128)(2,1)S(1)}, u32[]{:S(2)}, u32[]{:S(2)}) collective-permute-start(bf16[256,768]{1,0:T(8,128)(2,1)S(1)} %bitcast.2), channel_id=1, source_target_pairs={{192,0},{196,4},{200,8},{204,12},{208,16},{212,20},{216,24},{220,2... | collective-permute-start | bytes 1179656 | tf_op jit(solution)/shard_map/ppermute | solution.py:54
  62.1 3.9 %collective-permute-start.12 = (bf16[256,768]{1,0:T(8,128)(2,1)S(1)}, bf16[256,768]{1,0:T(8,128)(2,1)S(1)}, u32[]{:S(2)}, u32[]{:S(2)}) collective-permute-start(bf16[256,768]{1,0:T(8,128)(2,1)S(1)} %collective-permute-done.4.refs_2_), channel_id=1, source_target_pairs={{4,0},{0,4},{12,8},{8,12},{20,16},{16,20},{28,24},{24,28},{36,32},... | collective-permute-start | bytes 1179656 | tf_op jit(solution)/shard_map/ppermute | solution.py:54
  64.7 3.8 %collective-permute-start.14 = (bf16[256,768]{1,0:T(8,128)(2,1)S(1)}, bf16[256,768]{1,0:T(8,128)(2,1)S(1)}, u32[]{:S(2)}, u32[]{:S(2)}) collective-permute-start(bf16[256,768]{1,0:T(8,128)(2,1)S(1)} %copy-done.1), channel_id=1, source_target_pairs={{4,0},{0,4},{12,8},{8,12},{20,16},{16,20},{28,24},{24,28},{36,32},... | collective-permute-start | bytes 1179656 | tf_op jit(solution)/shard_map/ppermute | solution.py:54
  64.7 3.7 %collective-permute-start.15 = (bf16[256,768]{1,0:T(8,128)(2,1)S(1)}, bf16[256,768]{1,0:T(8,128)(2,1)S(1)}, u32[]{:S(2)}, u32[]{:S(2)}) collective-permute-start(bf16[256,768]{1,0:T(8,128)(2,1)S(1)} %collective-permute-done.9.refs_1_), channel_id=1, source_target_pairs={{4,0},{0,4},{12,8},{8,12},{20,16},{16,20},{28,24},{24,28},{36,32},... | collective-permute-start | bytes 1179656 | tf_op jit(solution)/shard_map/ppermute | solution.py:54
  65.2 3.3 %collective-permute-start.16 = (bf16[256,768]{1,0:T(8,128)(2,1)S(1)}, bf16[256,768]{1,0:T(8,128)(2,1)S(1)}, u32[]{:S(2)}, u32[]{:S(2)}) collective-permute-start(bf16[256,768]{1,0:T(8,128)(2,1)S(1)} %collective-permute-done.10.refs_2_), channel_id=1, source_target_pairs={{4,0},{0,4},{12,8},{8,12},{20,16},{16,20},{28,24},{24,28},{36,32},... | collective-permute-start | bytes 1179656 | tf_op jit(solution)/shard_map/ppermute | solution.py:54
  66.0 5.5 %collective-permute-start.13 = (bf16[256,768]{1,0:T(8,128)(2,1)S(1)}, bf16[256,768]{1,0:T(8,128)(2,1)S(1)}, u32[]{:S(2)}, u32[]{:S(2)}) collective-permute-start(bf16[256,768]{1,0:T(8,128)(2,1)S(1)} %collective-permute-done.6.refs_3_), channel_id=1, source_target_pairs={{4,0},{0,4},{12,8},{8,12},{20,16},{16,20},{28,24},{24,28},{36,32},... | collective-permute-start | bytes 1179656 | tf_op jit(solution)/shard_map/ppermute | solution.py:54
  74.4 0.6 copy-start.2
  75.0 4.9 %collective-permute-start.17 = (bf16[64,384]{1,0:T(8,128)(2,1)S(1)}, bf16[64,384]{1,0:T(8,128)(2,1)S(1)}, u32[]{:S(2)}, u32[]{:S(2)}) collective-permute-start(bf16[64,384]{1,0:T(8,128)(2,1)S(1)} %get-tuple-element.52), channel_id=1, source_target_pairs={{3,0},{0,1},{1,2},{2,3},{7,4},{4,5},{5,6},{6,7},{11,8},{8,9},{9,10... | collective-permute-start | bytes 147464 | tf_op jit(solution)/shard_map/ppermute | solution.py:147
  76.3 4.9 %collective-permute-start.18 = (bf16[64,384]{1,0:T(8,128)(2,1)S(1)}, bf16[64,384]{1,0:T(8,128)(2,1)S(1)}, u32[]{:S(2)}, u32[]{:S(2)}) collective-permute-start(bf16[64,384]{1,0:T(8,128)(2,1)S(1)} %get-tuple-element.53), channel_id=1, source_target_pairs={{2,0},{3,1},{0,2},{1,3},{6,4},{7,5},{4,6},{5,7},{10,8},{11,9},{8,1... | collective-permute-start | bytes 147464 | tf_op jit(solution)/shard_map/ppermute | solution.py:147
  78.7 3.2 %collective-permute-start.19 = (bf16[64,384]{1,0:T(8,128)(2,1)S(1)}, bf16[64,384]{1,0:T(8,128)(2,1)S(1)}, u32[]{:S(2)}, u32[]{:S(2)}) collective-permute-start(bf16[64,384]{1,0:T(8,128)(2,1)S(1)} %get-tuple-element.54), channel_id=1, source_target_pairs={{1,0},{2,1},{3,2},{0,3},{5,4},{6,5},{7,6},{4,7},{9,8},{10,9},{11,1... | collective-permute-start | bytes 147464 | tf_op jit(solution)/shard_map/ppermute | solution.py:147
  79.9 2.1 %copy-start.8 = (bf16[64,384]{1,0:T(8,128)(2,1)}, bf16[64,384]{1,0:T(8,128)(2,1)S(1)}, u32[]{:S(2)}) copy-start(bf16[64,384]{1,0:T(8,128)(2,1)S(1)} %collective-permute-done.17.p1) | copy-start | bytes 147460
  81.2 0.7 copy-start.9
  81.9 0.6 copy-start.10

commit v3 on v2

--- a/solution.py
+++ b/solution.py
@@ -364,11 +364,11 @@
     sent, sent1, sent2, *_ = barrier((own, next1, prev1, z4))
     x2 = move(sent, from_x(2))
     next1p, prev1p = move(sent1, FROM_PARTNER), move(sent2, FROM_PARTNER)
-    next2, prev2, z4x, x2 = barrier((next2, prev2, z4x, x2))
+    state = step(None, own=own, xnext=xnext, xprev=xprev, z4=z4)
+    next2, prev2, z4x, x2, state = barrier((next2, prev2, z4x, x2, state))
     next2p = move(next2, FROM_PARTNER)
     sent, _ = barrier((prev2, next2p))
     prev2p = move(sent, FROM_PARTNER)
-    state = step(None, own=own, xnext=xnext, xprev=xprev, z4=z4)
     state = step(
         state, partner=partner, next1=next1, prev1=prev1, next1p=next1p, prev1p=prev1p
     )

time: 84.6 us -> 84 us (level)
  transfers between devices with their start and end apart: 21 -> 21, of which waited for: 6 -> 9; matrix products, arithmetic and copies ran while one was open for 1% -> 1% of each run, Pallas kernels for 11% -> 11%
where the time goes in v3:
time: 84 us; the launch traced here: 83.4 us
  starting transfers between devices  45.6 us (54%)
  waiting for transfers between devices  18.5 us (22%)
  Pallas kernels  15.4 us (18%)
  local copies, waits for them, and re-layouts  2.74 us (3%)
  other arithmetic  0.98 us (1%)
    ppermute x14, starting transfers between devices, move(): return lax.ppermute(block, 'frame', pairs)  31.3 us
    ppermute x14, waiting for transfers between devices, move(): return lax.ppermute(block, 'frame', pairs)  16.4 us
    ppermute x6, starting transfers between devices, over_heads(): lax.ppermute(pieces[s], 'head', y_from(s))  10.7 us
    pallas_call x3, Pallas kernels, attend(): pl.pallas_call(functools.partial(attend_kernel, names, kinds, first, last...  7.93 us
    pallas_call x4, Pallas kernels, copier(): pl.pallas_call(kernel, out_shape=out_shape, in_specs=[VMEM] * len(arrays)...  7.49 us
    all_to_all x1, starting transfers between devices, shards(): lax.all_to_all(z4_packed, 'head', split_axis=0, concat_axis=0, tiled=True)  3.59 us
    unnamed x22, local copies, waits for them, and re-layouts  2.74 us
    ppermute x6, waiting for transfers between devices, over_heads(): lax.ppermute(pieces[s], 'head', y_from(s))  2.05 us
  transfers between devices with their start and end apart: 21, of which 9 were waited for; matrix products, arithmetic and copies ran while one was open for 1% of the time, Pallas kernels for 11%

profile of v3, /device:TPU:1, one launch (start us, length us, event | category | flops | bytes accessed | tf_op | source)
XLA Modules:
  0.0 83.4 jit_solution(16803048011685532996)
XLA Ops:
  0.0 2.1 %pack.1 = (bf16[64,1152]{1,0:T(8,128)(2,1)}, bf16[64,1152]{1,0:T(8,128)(2,1)}, bf16[64,1152]{1,0:T(8,128)(2,1)}, bf16[64,1152]{1,0:T(8,128)(2,1)}, bf16[64,3072]{1,0:T(8,128)(2,1)}) custom-call(bf16[64,1536]{1,0:T(8,128)(2,1)} %k_ref.1, bf16[64,1536]{1,0:T(8,128)(2,1)} %v_ref.1, bf16[64,1536]{1,0:T(8,128)(2,1)} %q_ref.1), custom_call_target="tpu_custom_call" | custom-call | flops 1 | bytes 1 | tf_op jit(solution)/shard_map/pack/pallas_call | solution.py:63
  2.1 2.1 %collective-permute-start = (bf16[64,1152]{1,0:T(8,128)(2,1)}, bf16[64,1152]{1,0:T(8,128)(2,1)S(1)}, u32[]{:S(2)}, u32[]{:S(2)}) collective-permute-start(bf16[64,1152]{1,0:T(8,128)(2,1)} %get-tuple-element.33), channel_id=1, source_target_pairs={{3,0},{0,1},{1,2},{2,3},{7,4},{4,5},{5,6},{6,7},{11,8},{8,9},{9,10... | collective-permute-start | bytes 442376 | tf_op jit(solution)/shard_map/ppermute | solution.py:147
  4.3 2.6 %collective-permute-start.1 = (bf16[64,1152]{1,0:T(8,128)(2,1)}, bf16[64,1152]{1,0:T(8,128)(2,1)S(1)}, u32[]{:S(2)}, u32[]{:S(2)}) collective-permute-start(bf16[64,1152]{1,0:T(8,128)(2,1)} %get-tuple-element.34), channel_id=1, source_target_pairs={{2,0},{3,1},{0,2},{1,3},{6,4},{7,5},{4,6},{5,7},{10,8},{11,9},{8,1... | collective-permute-start | bytes 442376 | tf_op jit(solution)/shard_map/ppermute | solution.py:147
  6.9 1.1 %collective-permute-start.2 = (bf16[64,1152]{1,0:T(8,128)(2,1)}, bf16[64,1152]{1,0:T(8,128)(2,1)S(1)}, u32[]{:S(2)}, u32[]{:S(2)}) collective-permute-start(bf16[64,1152]{1,0:T(8,128)(2,1)} %get-tuple-element.35), channel_id=1, source_target_pairs={{1,0},{2,1},{3,2},{0,3},{5,4},{6,5},{7,6},{4,7},{9,8},{10,9},{11,1... | collective-permute-start | bytes 442376 | tf_op jit(solution)/shard_map/ppermute | solution.py:147
  8.0 6.9 %collective-permute-start.7 = (bf16[64,3072]{1,0:T(8,128)(2,1)}, bf16[64,3072]{1,0:T(8,128)(2,1)S(1)}, u32[]{:S(2)}, u32[]{:S(2)}) collective-permute-start(bf16[64,3072]{1,0:T(8,128)(2,1)} %get-tuple-element.38), channel_id=1, source_target_pairs={{32,0},{36,4},{40,8},{44,12},{48,16},{52,20},{56,24},{60,28},{0,32... | collective-permute-start | bytes 1179656 | tf_op jit(solution)/shard_map/ppermute | solution.py:54
  14.9 0.6 copy-done.5
  15.6 2.0 %join.1 = (bf16[256,768]{1,0:T(8,128)(2,1)}, bf16[256,384]{1,0:T(8,128)(2,1)}) custom-call(bf16[64,1152]{1,0:T(8,128)(2,1)} %get-tuple-element.32.p0, bf16[64,1152]{1,0:T(8,128)(2,1)} %copy-done.5, bf16[64,1152]{1,0:T(8,128)(2,1)} %copy-done.6, bf16[64,1152]{1,0:T(8,128)(2,1)} %copy-done.7), custom_call_target="tpu_custom_call" | custom-call | flops 1 | bytes 1 | tf_op jit(solution)/shard_map/join/pallas_call | solution.py:63
  17.6 2.5 %collective-permute-start.3 = (bf16[256,768]{1,0:T(8,128)(2,1)}, bf16[256,768]{1,0:T(8,128)(2,1)S(1)}, u32[]{:S(2)}, u32[]{:S(2)}) collective-permute-start(bf16[256,768]{1,0:T(8,128)(2,1)} %get-tuple-element.48.refs_0_), channel_id=1, source_target_pairs={{64,0},{68,4},{72,8},{76,12},{80,16},{84,20},{88,24},{92,28},{96,3... | collective-permute-start | bytes 1179656 | tf_op jit(solution)/shard_map/ppermute | solution.py:54
  20.1 0.7 collective-permute-start.10
  20.9 5.8 %collective-permute-start.9 = (bf16[256,768]{1,0:T(8,128)(2,1)}, bf16[256,768]{1,0:T(8,128)(2,1)S(1)}, u32[]{:S(2)}, u32[]{:S(2)}) collective-permute-start(bf16[256,768]{1,0:T(8,128)(2,1)} %get-tuple-element.48.refs_0_), channel_id=1, source_target_pairs={{8,0},{12,4},{16,8},{20,12},{24,16},{28,20},{32,24},{36,28},{40,32... | collective-permute-start | bytes 1179656 | tf_op jit(solution)/shard_map/ppermute | solution.py:54
  26.7 0.8 copy-done.4
  27.4 1.8 %unpack.1 = bf16[256,768]{1,0:T(8,128)(2,1)} custom-call(bf16[64,3072]{1,0:T(8,128)(2,1)} %copy-done.4), custom_call_target="tpu_custom_call" | custom-call | flops 1 | bytes 1 | tf_op jit(solution)/shard_map/unpack/pallas_call | solution.py:63
  29.2 3.6 %all-to-all-start = ((bf16[4,64,768]{2,1,0:T(8,128)(2,1)}), bf16[4,64,768]{2,1,0:T(8,128)(2,1)S(1)}, u32[]{:S(2)}, u32[]{:S(2)}) async-start(bf16[4,64,768]{2,1,0:T(8,128)(2,1)} %bitcast.4), calls=%async_computation | async-start | bytes 786432 | tf_op jit(solution)/shard_map/all_to_all | solution.py:354
  32.9 1.0 %broadcast_select_fusion = (bf16[256,768]{1,0:T(8,128)(2,1)}, bf16[256,768]{1,0:T(8,128)(2,1)}) fusion(bf16[256,768]{1,0:T(8,128)(2,1)S(1)} %collective-permute-done.5.refs_2_, bf16[256,768]{1,0:T(8,128)(2,1)S(1)} %copy-done.1, pred[]{:T(512)S(6)} %ge.3, bf16[256,768]{1,0:T(8,128)(2,1)S(1)} %collective-permute-done.3.refs_1_, pred[]{:T(512)S(6)} %lt.10), kind=kLoop, calls=%fused_computation | loop fusion | flops 393216 | bytes 1966082 | tf_op jit(solution)/shard_map/jit(_where)/select_n | solution.py:362
  33.9 8.9 %collective-permute-start.4 = (bf16[256,768]{1,0:T(8,128)(2,1)}, bf16[256,768]{1,0:T(8,128)(2,1)S(1)}, u32[]{:S(2)}, u32[]{:S(2)}) collective-permute-start(bf16[256,768]{1,0:T(8,128)(2,1)} %get-tuple-element.60), channel_id=1, source_target_pairs={{16,0},{20,4},{24,8},{28,12},{32,16},{36,20},{40,24},{44,28},{48,3... | collective-permute-start | bytes 1179656 | tf_op jit(solution)/shard_map/ppermute | solution.py:54
  43.1 2.6 %collective-permute-start.11 = (bf16[256,768]{1,0:T(8,128)(2,1)S(1)}, bf16[256,768]{1,0:T(8,128)(2,1)S(1)}, u32[]{:S(2)}, u32[]{:S(2)}) collective-permute-start(bf16[256,768]{1,0:T(8,128)(2,1)S(1)} %copy-done.1), channel_id=1, source_target_pairs={{128,0},{132,4},{136,8},{140,12},{144,16},{148,20},{152,24},{156,2... | collective-permute-start | bytes 1179656 | tf_op jit(solution)/shard_map/ppermute | solution.py:54
  46.0 2.1 %attend4.1 = (f32[256,128]{1,0:T(8,128)S(1)}, f32[256,384]{1,0:T(8,128)S(1)}) custom-call(s32[1,64]{1,0:T(1,128)S(1)} %copy-done.3, bf16[256,384]{1,0:T(8,128)(2,1)S(1)} %copy-done, bf16[256,768]{1,0:T(8,128)(2,1)S(1)} %copy-done.1, bf16[256,768]{1,0:T(8,128)(2,1)S(1)} %collective-permute-done.3.refs_1_, ...), custom_call_target="tpu_custom_call" | custom-call | flops 1 | bytes 1 | tf_op jit(solution)/shard_map/attend4/pallas_call | solution.py:331
  48.0 11.0 %collective-permute-done.4.refs_2_ = bf16[256,768]{1,0:T(8,128)(2,1)S(1)} collective-permute-done((bf16[256,768]{1,0:T(8,128)(2,1)}, bf16[256,768]{1,0:T(8,128)(2,1)S(1)}, u32[]{:S(2)}, u32[]{:S(2)}) %collective-permute-start.4) | collective-permute-done | bytes 393248 | tf_op jit(solution)/shard_map/ppermute | solution.py:54
  59.0 3.0 %collective-permute-done.6.refs_3_ = bf16[256,768]{1,0:T(8,128)(2,1)S(1)} collective-permute-done((bf16[256,768]{1,0:T(8,128)(2,1)}, bf16[256,768]{1,0:T(8,128)(2,1)S(1)}, u32[]{:S(2)}, u32[]{:S(2)}) %collective-permute-start.6) | collective-permute-done | bytes 393248 | tf_op jit(solution)/shard_map/ppermute | solution.py:54
  62.1 2.6 %collective-permute-start.12 = (bf16[256,768]{1,0:T(8,128)(2,1)S(1)}, bf16[256,768]{1,0:T(8,128)(2,1)S(1)}, u32[]{:S(2)}, u32[]{:S(2)}) collective-permute-start(bf16[256,768]{1,0:T(8,128)(2,1)S(1)} %collective-permute-done.4.refs_2_), channel_id=1, source_target_pairs={{4,0},{0,4},{12,8},{8,12},{20,16},{16,20},{28,24},{24,28},{36,32},... | collective-permute-start | bytes 1179656 | tf_op jit(solution)/shard_map/ppermute | solution.py:54
  65.3 0.7 collective-permute-done.12.refs_5_
  67.1 0.6 collective-permute-done.16.refs_4_
  67.7 3.0 %attend5.2 = (f32[256,128]{1,0:T(8,128)S(1)}, f32[256,384]{1,0:T(8,128)S(1)}) custom-call(s32[1,64]{1,0:T(1,128)S(1)} %copy-done.3, bf16[256,384]{1,0:T(8,128)(2,1)S(1)} %copy-done, bf16[256,768]{1,0:T(8,128)(2,1)S(1)} %collective-permute-done.14.refs_0_, bf16[256,768]{1,0:T(8,128)(2,1)S(1)} %collective-permute-done.9.refs_1_, ...), custom_call_target="tpu_custom_call" | custom-call | flops 1 | bytes 1 | tf_op jit(solution)/shard_map/attend5/pallas_call | solution.py:331
  70.7 2.9 %attend5.3 = (bf16[64,384]{1,0:T(8,128)(2,1)S(1)}, bf16[64,384]{1,0:T(8,128)(2,1)S(1)}, bf16[64,384]{1,0:T(8,128)(2,1)S(1)}, bf16[64,384]{1,0:T(8,128)(2,1)S(1)}) custom-call(s32[1,64]{1,0:T(1,128)S(1)} %copy-done.3, bf16[256,384]{1,0:T(8,128)(2,1)S(1)} %copy-done, bf16[256,768]{1,0:T(8,128)(2,1)S(1)} %collective-permute-done.11.refs_0_, ...), custom_call_target="tpu_custom_call" | custom-call | flops 1 | bytes 1 | tf_op jit(solution)/shard_map/attend5/pallas_call | solution.py:331
  73.6 0.6 copy-done.2
  74.2 1.3 %collective-permute-start.17 = (bf16[64,384]{1,0:T(8,128)(2,1)S(1)}, bf16[64,384]{1,0:T(8,128)(2,1)S(1)}, u32[]{:S(2)}, u32[]{:S(2)}) collective-permute-start(bf16[64,384]{1,0:T(8,128)(2,1)S(1)} %get-tuple-element.56), channel_id=1, source_target_pairs={{3,0},{0,1},{1,2},{2,3},{7,4},{4,5},{5,6},{6,7},{11,8},{8,9},{9,10... | collective-permute-start | bytes 147464 | tf_op jit(solution)/shard_map/ppermute | solution.py:147
  75.5 2.4 %collective-permute-start.18 = (bf16[64,384]{1,0:T(8,128)(2,1)S(1)}, bf16[64,384]{1,0:T(8,128)(2,1)S(1)}, u32[]{:S(2)}, u32[]{:S(2)}) collective-permute-start(bf16[64,384]{1,0:T(8,128)(2,1)S(1)} %get-tuple-element.57), channel_id=1, source_target_pairs={{2,0},{3,1},{0,2},{1,3},{6,4},{7,5},{4,6},{5,7},{10,8},{11,9},{8,1... | collective-permute-start | bytes 147464 | tf_op jit(solution)/shard_map/ppermute | solution.py:147
  77.9 1.2 %collective-permute-start.19 = (bf16[64,384]{1,0:T(8,128)(2,1)S(1)}, bf16[64,384]{1,0:T(8,128)(2,1)S(1)}, u32[]{:S(2)}, u32[]{:S(2)}) collective-permute-start(bf16[64,384]{1,0:T(8,128)(2,1)S(1)} %get-tuple-element.58), channel_id=1, source_target_pairs={{1,0},{2,1},{3,2},{0,3},{5,4},{6,5},{7,6},{4,7},{9,8},{10,9},{11,1... | collective-permute-start | bytes 147464 | tf_op jit(solution)/shard_map/ppermute | solution.py:147
  79.1 1.1 %collective-permute-done.18.p2 = bf16[64,384]{1,0:T(8,128)(2,1)S(1)} collective-permute-done((bf16[64,384]{1,0:T(8,128)(2,1)S(1)}, bf16[64,384]{1,0:T(8,128)(2,1)S(1)}, u32[]{:S(2)}, u32[]{:S(2)}) %collective-permute-start.18) | collective-permute-done | bytes 49184 | tf_op jit(solution)/shard_map/ppermute | solution.py:147
  80.2 0.9 %collective-permute-done.19.p3 = bf16[64,384]{1,0:T(8,128)(2,1)S(1)} collective-permute-done((bf16[64,384]{1,0:T(8,128)(2,1)S(1)}, bf16[64,384]{1,0:T(8,128)(2,1)S(1)}, u32[]{:S(2)}, u32[]{:S(2)}) %collective-permute-start.19) | collective-permute-done | bytes 49184 | tf_op jit(solution)/shard_map/ppermute | solution.py:147
  81.2 0.6 copy-done.10
  81.8 1.6 %place.1 = bf16[64,1536]{1,0:T(8,128)(2,1)} custom-call(bf16[64,384]{1,0:T(8,128)(2,1)} %copy-done.2, bf16[64,384]{1,0:T(8,128)(2,1)} %copy-done.8, bf16[64,384]{1,0:T(8,128)(2,1)} %copy-done.9, bf16[64,384]{1,0:T(8,128)(2,1)} %copy-done.10), custom_call_target="tpu_custom_call" | custom-call | flops 1 | bytes 1 | tf_op jit(solution)/shard_map/place/pallas_call | solution.py:63
  (40 shorter events, 2.5 us)
Async XLA Ops:
  2.1 12.7 %collective-permute-start = (bf16[64,1152]{1,0:T(8,128)(2,1)}, bf16[64,1152]{1,0:T(8,128)(2,1)S(1)}, u32[]{:S(2)}, u32[]{:S(2)}) collective-permute-start(bf16[64,1152]{1,0:T(8,128)(2,1)} %get-tuple-element.33), channel_id=1, source_target_pairs={{3,0},{0,1},{1,2},{2,3},{7,4},{4,5},{5,6},{6,7},{11,8},{8,9},{9,10... | collective-permute-start | bytes 442376 | tf_op jit(solution)/shard_map/ppermute | solution.py:147
  4.3 10.6 %collective-permute-start.1 = (bf16[64,1152]{1,0:T(8,128)(2,1)}, bf16[64,1152]{1,0:T(8,128)(2,1)S(1)}, u32[]{:S(2)}, u32[]{:S(2)}) collective-permute-start(bf16[64,1152]{1,0:T(8,128)(2,1)} %get-tuple-element.34), channel_id=1, source_target_pairs={{2,0},{3,1},{0,2},{1,3},{6,4},{7,5},{4,6},{5,7},{10,8},{11,9},{8,1... | collective-permute-start | bytes 442376 | tf_op jit(solution)/shard_map/ppermute | solution.py:147
  6.9 8.0 %collective-permute-start.2 = (bf16[64,1152]{1,0:T(8,128)(2,1)}, bf16[64,1152]{1,0:T(8,128)(2,1)S(1)}, u32[]{:S(2)}, u32[]{:S(2)}) collective-permute-start(bf16[64,1152]{1,0:T(8,128)(2,1)} %get-tuple-element.35), channel_id=1, source_target_pairs={{1,0},{2,1},{3,2},{0,3},{5,4},{6,5},{7,6},{4,7},{9,8},{10,9},{11,1... | collective-permute-start | bytes 442376 | tf_op jit(solution)/shard_map/ppermute | solution.py:147
  8.0 18.7 %collective-permute-start.7 = (bf16[64,3072]{1,0:T(8,128)(2,1)}, bf16[64,3072]{1,0:T(8,128)(2,1)S(1)}, u32[]{:S(2)}, u32[]{:S(2)}) collective-permute-start(bf16[64,3072]{1,0:T(8,128)(2,1)} %get-tuple-element.38), channel_id=1, source_target_pairs={{32,0},{36,4},{40,8},{44,12},{48,16},{52,20},{56,24},{60,28},{0,32... | collective-permute-start | bytes 1179656 | tf_op jit(solution)/shard_map/ppermute | solution.py:54
  14.9 0.7 copy-start.5
  14.9 0.7 copy-start.6
  14.9 0.7 copy-start.7
  17.6 15.2 %collective-permute-start.3 = (bf16[256,768]{1,0:T(8,128)(2,1)}, bf16[256,768]{1,0:T(8,128)(2,1)S(1)}, u32[]{:S(2)}, u32[]{:S(2)}) collective-permute-start(bf16[256,768]{1,0:T(8,128)(2,1)} %get-tuple-element.48.refs_0_), channel_id=1, source_target_pairs={{64,0},{68,4},{72,8},{76,12},{80,16},{84,20},{88,24},{92,28},{96,3... | collective-permute-start | bytes 1179656 | tf_op jit(solution)/shard_map/ppermute | solution.py:54
  20.1 12.8 %collective-permute-start.5 = (bf16[256,768]{1,0:T(8,128)(2,1)}, bf16[256,768]{1,0:T(8,128)(2,1)S(1)}, u32[]{:S(2)}, u32[]{:S(2)}) collective-permute-start(bf16[256,768]{1,0:T(8,128)(2,1)} %get-tuple-element.48.refs_0_), channel_id=1, source_target_pairs={{192,0},{196,4},{200,8},{204,12},{208,16},{212,20},{216,24},{220,2... | collective-permute-start | bytes 1179656 | tf_op jit(solution)/shard_map/ppermute | solution.py:54
  20.1 23.0 %collective-permute-start.10 = (bf16[256,768]{1,0:T(8,128)(2,1)}, bf16[256,768]{1,0:T(8,128)(2,1)S(1)}, u32[]{:S(2)}, u32[]{:S(2)}) collective-permute-start(bf16[256,768]{1,0:T(8,128)(2,1)} %get-tuple-element.48.refs_0_), channel_id=1, source_target_pairs={{248,0},{252,4},{0,8},{4,12},{8,16},{12,20},{16,24},{20,28},{24,32... | collective-permute-start | bytes 1179656 | tf_op jit(solution)/shard_map/ppermute | solution.py:54
  20.9 22.2 %collective-permute-start.9 = (bf16[256,768]{1,0:T(8,128)(2,1)}, bf16[256,768]{1,0:T(8,128)(2,1)S(1)}, u32[]{:S(2)}, u32[]{:S(2)}) collective-permute-start(bf16[256,768]{1,0:T(8,128)(2,1)} %get-tuple-element.48.refs_0_), channel_id=1, source_target_pairs={{8,0},{12,4},{16,8},{20,12},{24,16},{28,20},{32,24},{36,28},{40,32... | collective-permute-start | bytes 1179656 | tf_op jit(solution)/shard_map/ppermute | solution.py:54
  26.7 0.8 copy-start.4
  29.2 3.7 %copy-start.1 = (bf16[256,768]{1,0:T(8,128)(2,1)S(1)}, bf16[256,768]{1,0:T(8,128)(2,1)}, u32[]{:S(2)}) copy-start(bf16[256,768]{1,0:T(8,128)(2,1)} %get-tuple-element.48.refs_0_) | copy-start | bytes 1179652
  29.2 13.9 %all-to-all-start = ((bf16[4,64,768]{2,1,0:T(8,128)(2,1)}), bf16[4,64,768]{2,1,0:T(8,128)(2,1)S(1)}, u32[]{:S(2)}, u32[]{:S(2)}) async-start(bf16[4,64,768]{2,1,0:T(8,128)(2,1)} %bitcast.4), calls=%async_computation | async-start | bytes 786432 | tf_op jit(solution)/shard_map/all_to_all | solution.py:354
  32.9 13.1 %copy-start = (bf16[256,384]{1,0:T(8,128)(2,1)S(1)}, bf16[256,384]{1,0:T(8,128)(2,1)}, u32[]{:S(2)}) copy-start(bf16[256,384]{1,0:T(8,128)(2,1)} %get-tuple-element.36.q_ref) | copy-start | bytes 589828
  33.9 25.2 %collective-permute-start.4 = (bf16[256,768]{1,0:T(8,128)(2,1)}, bf16[256,768]{1,0:T(8,128)(2,1)S(1)}, u32[]{:S(2)}, u32[]{:S(2)}) collective-permute-start(bf16[256,768]{1,0:T(8,128)(2,1)} %get-tuple-element.60), channel_id=1, source_target_pairs={{16,0},{20,4},{24,8},{28,12},{32,16},{36,20},{40,24},{44,28},{48,3... | collective-permute-start | bytes 1179656 | tf_op jit(solution)/shard_map/ppermute | solution.py:54
  42.8 19.3 %collective-permute-start.6 = (bf16[256,768]{1,0:T(8,128)(2,1)}, bf16[256,768]{1,0:T(8,128)(2,1)S(1)}, u32[]{:S(2)}, u32[]{:S(2)}) collective-permute-start(bf16[256,768]{1,0:T(8,128)(2,1)} %get-tuple-element.59), channel_id=1, source_target_pairs={{48,0},{52,4},{56,8},{60,12},{0,16},{4,20},{8,24},{12,28},{16,32},... | collective-permute-start | bytes 1179656 | tf_op jit(solution)/shard_map/ppermute | solution.py:54
  43.1 2.9 %copy-start.3 = (s32[1,64]{1,0:T(1,128)S(1)}, s32[1,64]{1,0:T(1,128)}, u32[]{:S(2)}) copy-start(s32[1,64]{1,0:T(1,128)} %band_ref.5) | copy-start | bytes 772
  43.1 19.0 %collective-permute-start.11 = (bf16[256,768]{1,0:T(8,128)(2,1)S(1)}, bf16[256,768]{1,0:T(8,128)(2,1)S(1)}, u32[]{:S(2)}, u32[]{:S(2)}) collective-permute-start(bf16[256,768]{1,0:T(8,128)(2,1)S(1)} %copy-done.1), channel_id=1, source_target_pairs={{128,0},{132,4},{136,8},{140,12},{144,16},{148,20},{152,24},{156,2... | collective-permute-start | bytes 1179656 | tf_op jit(solution)/shard_map/ppermute | solution.py:54
  45.7 16.4 %collective-permute-start.8 = (bf16[256,768]{1,0:T(8,128)(2,1)S(1)}, bf16[256,768]{1,0:T(8,128)(2,1)S(1)}, u32[]{:S(2)}, u32[]{:S(2)}) collective-permute-start(bf16[256,768]{1,0:T(8,128)(2,1)S(1)} %bitcast.2), channel_id=1, source_target_pairs={{192,0},{196,4},{200,8},{204,12},{208,16},{212,20},{216,24},{220,2... | collective-permute-start | bytes 1179656 | tf_op jit(solution)/shard_map/ppermute | solution.py:54
  62.1 3.9 %collective-permute-start.12 = (bf16[256,768]{1,0:T(8,128)(2,1)S(1)}, bf16[256,768]{1,0:T(8,128)(2,1)S(1)}, u32[]{:S(2)}, u32[]{:S(2)}) collective-permute-start(bf16[256,768]{1,0:T(8,128)(2,1)S(1)} %collective-permute-done.4.refs_2_), channel_id=1, source_target_pairs={{4,0},{0,4},{12,8},{8,12},{20,16},{16,20},{28,24},{24,28},{36,32},... | collective-permute-start | bytes 1179656 | tf_op jit(solution)/shard_map/ppermute | solution.py:54
  64.7 1.9 %collective-permute-start.14 = (bf16[256,768]{1,0:T(8,128)(2,1)S(1)}, bf16[256,768]{1,0:T(8,128)(2,1)S(1)}, u32[]{:S(2)}, u32[]{:S(2)}) collective-permute-start(bf16[256,768]{1,0:T(8,128)(2,1)S(1)} %copy-done.1), channel_id=1, source_target_pairs={{4,0},{0,4},{12,8},{8,12},{20,16},{16,20},{28,24},{24,28},{36,32},... | collective-permute-start | bytes 1179656 | tf_op jit(solution)/shard_map/ppermute | solution.py:54
  64.7 2.4 %collective-permute-start.15 = (bf16[256,768]{1,0:T(8,128)(2,1)S(1)}, bf16[256,768]{1,0:T(8,128)(2,1)S(1)}, u32[]{:S(2)}, u32[]{:S(2)}) collective-permute-start(bf16[256,768]{1,0:T(8,128)(2,1)S(1)} %collective-permute-done.9.refs_1_), channel_id=1, source_target_pairs={{4,0},{0,4},{12,8},{8,12},{20,16},{16,20},{28,24},{24,28},{36,32},... | collective-permute-start | bytes 1179656 | tf_op jit(solution)/shard_map/ppermute | solution.py:54
  65.2 2.5 %collective-permute-start.16 = (bf16[256,768]{1,0:T(8,128)(2,1)S(1)}, bf16[256,768]{1,0:T(8,128)(2,1)S(1)}, u32[]{:S(2)}, u32[]{:S(2)}) collective-permute-start(bf16[256,768]{1,0:T(8,128)(2,1)S(1)} %collective-permute-done.10.refs_2_), channel_id=1, source_target_pairs={{4,0},{0,4},{12,8},{8,12},{20,16},{16,20},{28,24},{24,28},{36,32},... | collective-permute-start | bytes 1179656 | tf_op jit(solution)/shard_map/ppermute | solution.py:54
  66.0 4.7 %collective-permute-start.13 = (bf16[256,768]{1,0:T(8,128)(2,1)S(1)}, bf16[256,768]{1,0:T(8,128)(2,1)S(1)}, u32[]{:S(2)}, u32[]{:S(2)}) collective-permute-start(bf16[256,768]{1,0:T(8,128)(2,1)S(1)} %collective-permute-done.6.refs_3_), channel_id=1, source_target_pairs={{4,0},{0,4},{12,8},{8,12},{20,16},{16,20},{28,24},{24,28},{36,32},... | collective-permute-start | bytes 1179656 | tf_op jit(solution)/shard_map/ppermute | solution.py:54
  73.6 0.6 copy-start.2
  74.2 4.9 %collective-permute-start.17 = (bf16[64,384]{1,0:T(8,128)(2,1)S(1)}, bf16[64,384]{1,0:T(8,128)(2,1)S(1)}, u32[]{:S(2)}, u32[]{:S(2)}) collective-permute-start(bf16[64,384]{1,0:T(8,128)(2,1)S(1)} %get-tuple-element.56), channel_id=1, source_target_pairs={{3,0},{0,1},{1,2},{2,3},{7,4},{4,5},{5,6},{6,7},{11,8},{8,9},{9,10... | collective-permute-start | bytes 147464 | tf_op jit(solution)/shard_map/ppermute | solution.py:147
  75.5 4.7 %collective-permute-start.18 = (bf16[64,384]{1,0:T(8,128)(2,1)S(1)}, bf16[64,384]{1,0:T(8,128)(2,1)S(1)}, u32[]{:S(2)}, u32[]{:S(2)}) collective-permute-start(bf16[64,384]{1,0:T(8,128)(2,1)S(1)} %get-tuple-element.57), channel_id=1, source_target_pairs={{2,0},{3,1},{0,2},{1,3},{6,4},{7,5},{4,6},{5,7},{10,8},{11,9},{8,1... | collective-permute-start | bytes 147464 | tf_op jit(solution)/shard_map/ppermute | solution.py:147
  77.9 3.2 %collective-permute-start.19 = (bf16[64,384]{1,0:T(8,128)(2,1)S(1)}, bf16[64,384]{1,0:T(8,128)(2,1)S(1)}, u32[]{:S(2)}, u32[]{:S(2)}) collective-permute-start(bf16[64,384]{1,0:T(8,128)(2,1)S(1)} %get-tuple-element.58), channel_id=1, source_target_pairs={{1,0},{2,1},{3,2},{0,3},{5,4},{6,5},{7,6},{4,7},{9,8},{10,9},{11,1... | collective-permute-start | bytes 147464 | tf_op jit(solution)/shard_map/ppermute | solution.py:147
  79.1 2.1 %copy-start.8 = (bf16[64,384]{1,0:T(8,128)(2,1)}, bf16[64,384]{1,0:T(8,128)(2,1)S(1)}, u32[]{:S(2)}) copy-start(bf16[64,384]{1,0:T(8,128)(2,1)S(1)} %collective-permute-done.17.p1) | copy-start | bytes 147460
  80.2 0.9 %copy-start.9 = (bf16[64,384]{1,0:T(8,128)(2,1)}, bf16[64,384]{1,0:T(8,128)(2,1)S(1)}, u32[]{:S(2)}) copy-start(bf16[64,384]{1,0:T(8,128)(2,1)S(1)} %collective-permute-done.18.p2) | copy-start | bytes 147460
  81.2 0.6 copy-start.10

commit v4 on v3

--- a/solution.py
+++ b/solution.py
@@ -364,16 +364,22 @@
     sent, sent1, sent2, *_ = barrier((own, next1, prev1, z4))
     x2 = move(sent, from_x(2))
     next1p, prev1p = move(sent1, FROM_PARTNER), move(sent2, FROM_PARTNER)
-    state = step(None, own=own, xnext=xnext, xprev=xprev, z4=z4)
+    state = step(None, own=own, xnext=xnext, xprev=xprev, z4=z4, next1=next1, prev1=prev1)
     next2, prev2, z4x, x2, state = barrier((next2, prev2, z4x, x2, state))
     next2p = move(next2, FROM_PARTNER)
     sent, _ = barrier((prev2, next2p))
     prev2p = move(sent, FROM_PARTNER)
-    state = step(
-        state, partner=partner, next1=next1, prev1=prev1, next1p=next1p, prev1p=prev1p
-    )
     outs = step(
-        state, True, x2=x2, z4x=z4x, next2=next2, prev2=prev2, far2p=("choice", prev2p, next2p)
+        state,
+        True,
+        partner=partner,
+        next1p=next1p,
+        prev1p=prev1p,
+        x2=x2,
+        z4x=z4x,
+        next2=next2,
+        prev2=prev2,
+        far2p=("choice", prev2p, next2p),
     )
     return place(over_heads(outs))
 

time: 84 us -> 82.9 us (0.987)
  Pallas kernels: 15.4 us -> 14.1 us
  waiting for transfers between devices: 18.5 us -> 19.7 us
    pallas_call x3 -> x2, Pallas kernels: 7.93 us -> 6.65 us  [attend(): pl.pallas_call(functools.partial(attend_kernel, names, kinds, first, last...]
    ppermute x14, waiting for transfers between devices: 16.4 us -> 17.7 us  [move(): return lax.ppermute(block, 'frame', pairs)]
  transfers between devices with their start and end apart: 21 -> 21, of which waited for: 9 -> 10; matrix products, arithmetic and copies ran while one was open for 1% -> 1% of each run, Pallas kernels for 11% -> 8%
where the time goes in v4:
time: 82.9 us; the launch traced here: 82.6 us
  starting transfers between devices  44.9 us (54%)
  waiting for transfers between devices  19.7 us (24%)
  Pallas kernels  14.1 us (17%)
  local copies, waits for them, and re-layouts  2.73 us (3%)
  other arithmetic  0.98 us (1%)
    ppermute x14, starting transfers between devices, move(): return lax.ppermute(block, 'frame', pairs)  30.6 us
    ppermute x14, waiting for transfers between devices, move(): return lax.ppermute(block, 'frame', pairs)  17.7 us
    ppermute x6, starting transfers between devices, over_heads(): lax.ppermute(pieces[s], 'head', y_from(s))  10.8 us
    pallas_call x4, Pallas kernels, copier(): pl.pallas_call(kernel, out_shape=out_shape, in_specs=[VMEM] * len(arrays)...  7.46 us
    pallas_call x2, Pallas kernels, attend(): pl.pallas_call(functools.partial(attend_kernel, names, kinds, first, last...  6.65 us
    all_to_all x1, starting transfers between devices, shards(): lax.all_to_all(z4_packed, 'head', split_axis=0, concat_axis=0, tiled=True)  3.59 us
    unnamed x22, local copies, waits for them, and re-layouts  2.73 us
    ppermute x6, waiting for transfers between devices, over_heads(): lax.ppermute(pieces[s], 'head', y_from(s))  2.06 us
  transfers between devices with their start and end apart: 21, of which 10 were waited for; matrix products, arithmetic and copies ran while one was open for 1% of the time, Pallas kernels for 8%

profile of v4, /device:TPU:1, one launch (start us, length us, event | category | flops | bytes accessed | tf_op | source)
XLA Modules:
  0.0 82.6 jit_solution(4834099943940147391)
XLA Ops:
  0.0 2.1 %pack.1 = (bf16[64,1152]{1,0:T(8,128)(2,1)}, bf16[64,1152]{1,0:T(8,128)(2,1)}, bf16[64,1152]{1,0:T(8,128)(2,1)}, bf16[64,1152]{1,0:T(8,128)(2,1)}, bf16[64,3072]{1,0:T(8,128)(2,1)}) custom-call(bf16[64,1536]{1,0:T(8,128)(2,1)} %k_ref.1, bf16[64,1536]{1,0:T(8,128)(2,1)} %v_ref.1, bf16[64,1536]{1,0:T(8,128)(2,1)} %q_ref.1), custom_call_target="tpu_custom_call" | custom-call | flops 1 | bytes 1 | tf_op jit(solution)/shard_map/pack/pallas_call | solution.py:63
  2.1 2.1 %collective-permute-start = (bf16[64,1152]{1,0:T(8,128)(2,1)}, bf16[64,1152]{1,0:T(8,128)(2,1)S(1)}, u32[]{:S(2)}, u32[]{:S(2)}) collective-permute-start(bf16[64,1152]{1,0:T(8,128)(2,1)} %get-tuple-element.31), channel_id=1, source_target_pairs={{3,0},{0,1},{1,2},{2,3},{7,4},{4,5},{5,6},{6,7},{11,8},{8,9},{9,10... | collective-permute-start | bytes 442376 | tf_op jit(solution)/shard_map/ppermute | solution.py:147
  4.3 2.6 %collective-permute-start.1 = (bf16[64,1152]{1,0:T(8,128)(2,1)}, bf16[64,1152]{1,0:T(8,128)(2,1)S(1)}, u32[]{:S(2)}, u32[]{:S(2)}) collective-permute-start(bf16[64,1152]{1,0:T(8,128)(2,1)} %get-tuple-element.32), channel_id=1, source_target_pairs={{2,0},{3,1},{0,2},{1,3},{6,4},{7,5},{4,6},{5,7},{10,8},{11,9},{8,1... | collective-permute-start | bytes 442376 | tf_op jit(solution)/shard_map/ppermute | solution.py:147
  6.9 1.1 %collective-permute-start.2 = (bf16[64,1152]{1,0:T(8,128)(2,1)}, bf16[64,1152]{1,0:T(8,128)(2,1)S(1)}, u32[]{:S(2)}, u32[]{:S(2)}) collective-permute-start(bf16[64,1152]{1,0:T(8,128)(2,1)} %get-tuple-element.33), channel_id=1, source_target_pairs={{1,0},{2,1},{3,2},{0,3},{5,4},{6,5},{7,6},{4,7},{9,8},{10,9},{11,1... | collective-permute-start | bytes 442376 | tf_op jit(solution)/shard_map/ppermute | solution.py:147
  7.9 6.9 %collective-permute-start.3 = (bf16[64,3072]{1,0:T(8,128)(2,1)}, bf16[64,3072]{1,0:T(8,128)(2,1)S(1)}, u32[]{:S(2)}, u32[]{:S(2)}) collective-permute-start(bf16[64,3072]{1,0:T(8,128)(2,1)} %get-tuple-element.36), channel_id=1, source_target_pairs={{32,0},{36,4},{40,8},{44,12},{48,16},{52,20},{56,24},{60,28},{0,32... | collective-permute-start | bytes 1179656 | tf_op jit(solution)/shard_map/ppermute | solution.py:54
  14.9 0.6 copy-done.5
  15.6 2.0 %join.1 = (bf16[256,768]{1,0:T(8,128)(2,1)}, bf16[256,384]{1,0:T(8,128)(2,1)}) custom-call(bf16[64,1152]{1,0:T(8,128)(2,1)} %get-tuple-element.30.p0, bf16[64,1152]{1,0:T(8,128)(2,1)} %copy-done.5, bf16[64,1152]{1,0:T(8,128)(2,1)} %copy-done.6, bf16[64,1152]{1,0:T(8,128)(2,1)} %copy-done.7), custom_call_target="tpu_custom_call" | custom-call | flops 1 | bytes 1 | tf_op jit(solution)/shard_map/join/pallas_call | solution.py:63
  17.6 1.2 %collective-permute-start.11 = (bf16[256,768]{1,0:T(8,128)(2,1)}, bf16[256,768]{1,0:T(8,128)(2,1)S(1)}, u32[]{:S(2)}, u32[]{:S(2)}) collective-permute-start(bf16[256,768]{1,0:T(8,128)(2,1)} %get-tuple-element.41.refs_0_), channel_id=1, source_target_pairs={{192,0},{196,4},{200,8},{204,12},{208,16},{212,20},{216,24},{220,2... | collective-permute-start | bytes 1179656 | tf_op jit(solution)/shard_map/ppermute | solution.py:54
  18.8 1.5 %collective-permute-start.9 = (bf16[256,768]{1,0:T(8,128)(2,1)}, bf16[256,768]{1,0:T(8,128)(2,1)S(1)}, u32[]{:S(2)}, u32[]{:S(2)}) collective-permute-start(bf16[256,768]{1,0:T(8,128)(2,1)} %get-tuple-element.41.refs_0_), channel_id=1, source_target_pairs={{64,0},{68,4},{72,8},{76,12},{80,16},{84,20},{88,24},{92,28},{96,3... | collective-permute-start | bytes 1179656 | tf_op jit(solution)/shard_map/ppermute | solution.py:54
  20.3 5.1 %collective-permute-start.5 = (bf16[256,768]{1,0:T(8,128)(2,1)}, bf16[256,768]{1,0:T(8,128)(2,1)S(1)}, u32[]{:S(2)}, u32[]{:S(2)}) collective-permute-start(bf16[256,768]{1,0:T(8,128)(2,1)} %get-tuple-element.41.refs_0_), channel_id=1, source_target_pairs={{8,0},{12,4},{16,8},{20,12},{24,16},{28,20},{32,24},{36,28},{40,32... | collective-permute-start | bytes 1179656 | tf_op jit(solution)/shard_map/ppermute | solution.py:54
  25.4 0.8 copy-done.4
  26.2 1.8 %unpack.1 = bf16[256,768]{1,0:T(8,128)(2,1)} custom-call(bf16[64,3072]{1,0:T(8,128)(2,1)} %copy-done.4), custom_call_target="tpu_custom_call" | custom-call | flops 1 | bytes 1 | tf_op jit(solution)/shard_map/unpack/pallas_call | solution.py:63
  28.0 3.6 %all-to-all-start = ((bf16[4,64,768]{2,1,0:T(8,128)(2,1)}), bf16[4,64,768]{2,1,0:T(8,128)(2,1)S(1)}, u32[]{:S(2)}, u32[]{:S(2)}) async-start(bf16[4,64,768]{2,1,0:T(8,128)(2,1)} %bitcast.4), calls=%async_computation | async-start | bytes 786432 | tf_op jit(solution)/shard_map/all_to_all | solution.py:354
  31.6 1.0 %broadcast_select_fusion = (bf16[256,768]{1,0:T(8,128)(2,1)}, bf16[256,768]{1,0:T(8,128)(2,1)}) fusion(bf16[256,768]{1,0:T(8,128)(2,1)S(1)} %collective-permute-done.11.refs_2_, bf16[256,768]{1,0:T(8,128)(2,1)S(1)} %copy-done, pred[]{:T(512)S(6)} %ge.3, bf16[256,768]{1,0:T(8,128)(2,1)S(1)} %collective-permute-done.9.refs_1_, pred[]{:T(512)S(6)} %lt.10), kind=kLoop, calls=%fused_computation | loop fusion | flops 393216 | bytes 1966082 | tf_op jit(solution)/shard_map/jit(_where)/select_n | solution.py:362
  32.6 11.0 %collective-permute-start.10 = (bf16[256,768]{1,0:T(8,128)(2,1)}, bf16[256,768]{1,0:T(8,128)(2,1)S(1)}, u32[]{:S(2)}, u32[]{:S(2)}) collective-permute-start(bf16[256,768]{1,0:T(8,128)(2,1)} %get-tuple-element.56), channel_id=1, source_target_pairs={{16,0},{20,4},{24,8},{28,12},{32,16},{36,20},{40,24},{44,28},{48,3... | collective-permute-start | bytes 1179656 | tf_op jit(solution)/shard_map/ppermute | solution.py:54
  43.7 2.4 %collective-permute-start.14 = (bf16[256,768]{1,0:T(8,128)(2,1)S(1)}, bf16[256,768]{1,0:T(8,128)(2,1)S(1)}, u32[]{:S(2)}, u32[]{:S(2)}) collective-permute-start(bf16[256,768]{1,0:T(8,128)(2,1)S(1)} %copy-done), channel_id=1, source_target_pairs={{128,0},{132,4},{136,8},{140,12},{144,16},{148,20},{152,24},{156,2... | collective-permute-start | bytes 1179656 | tf_op jit(solution)/shard_map/ppermute | solution.py:54
  46.6 2.7 %attend6.1 = (f32[256,128]{1,0:T(8,128)S(1)}, f32[256,384]{1,0:T(8,128)S(1)}) custom-call(s32[1,64]{1,0:T(1,128)S(1)} %copy-done.3, bf16[256,384]{1,0:T(8,128)(2,1)S(1)} %copy-done.1, bf16[256,768]{1,0:T(8,128)(2,1)S(1)} %copy-done, bf16[256,768]{1,0:T(8,128)(2,1)S(1)} %collective-permute-done.9.refs_1_, ...), custom_call_target="tpu_custom_call" | custom-call | flops 1 | bytes 1 | tf_op jit(solution)/shard_map/attend6/pallas_call | solution.py:331
  49.2 9.8 %collective-permute-done.10.refs_5_ = bf16[256,768]{1,0:T(8,128)(2,1)S(1)} collective-permute-done((bf16[256,768]{1,0:T(8,128)(2,1)}, bf16[256,768]{1,0:T(8,128)(2,1)S(1)}, u32[]{:S(2)}, u32[]{:S(2)}) %collective-permute-start.10) | collective-permute-done | bytes 393248 | tf_op jit(solution)/shard_map/ppermute | solution.py:54
  59.1 1.1 %collective-permute-done.12.refs_6_ = bf16[256,768]{1,0:T(8,128)(2,1)S(1)} collective-permute-done((bf16[256,768]{1,0:T(8,128)(2,1)}, bf16[256,768]{1,0:T(8,128)(2,1)S(1)}, u32[]{:S(2)}, u32[]{:S(2)}) %collective-permute-start.12) | collective-permute-done | bytes 393248 | tf_op jit(solution)/shard_map/ppermute | solution.py:54
  60.1 4.1 %collective-permute-done.13.refs_4_ = bf16[256,768]{1,0:T(8,128)(2,1)S(1)} collective-permute-done((bf16[256,768]{1,0:T(8,128)(2,1)S(1)}, bf16[256,768]{1,0:T(8,128)(2,1)S(1)}, u32[]{:S(2)}, u32[]{:S(2)}) %collective-permute-start.13) | collective-permute-done | bytes 393248 | tf_op jit(solution)/shard_map/ppermute | solution.py:54
  64.2 1.1 %collective-permute-start.15 = (bf16[256,768]{1,0:T(8,128)(2,1)S(1)}, bf16[256,768]{1,0:T(8,128)(2,1)S(1)}, u32[]{:S(2)}, u32[]{:S(2)}) collective-permute-start(bf16[256,768]{1,0:T(8,128)(2,1)S(1)} %collective-permute-done.10.refs_5_), channel_id=1, source_target_pairs={{4,0},{0,4},{12,8},{8,12},{20,16},{16,20},{28,24},{24,28},{36,32},... | collective-permute-start | bytes 1179656 | tf_op jit(solution)/shard_map/ppermute | solution.py:54
  65.8 0.8 %collective-permute-done.15.refs_8_ = bf16[256,768]{1,0:T(8,128)(2,1)S(1)} collective-permute-done((bf16[256,768]{1,0:T(8,128)(2,1)S(1)}, bf16[256,768]{1,0:T(8,128)(2,1)S(1)}, u32[]{:S(2)}, u32[]{:S(2)}) %collective-permute-start.15) | collective-permute-done | bytes 393248 | tf_op jit(solution)/shard_map/ppermute | solution.py:54
  67.7 0.6 collective-permute-done.8.refs_2_
  68.8 4.0 %attend8.1 = (bf16[64,384]{1,0:T(8,128)(2,1)S(1)}, bf16[64,384]{1,0:T(8,128)(2,1)S(1)}, bf16[64,384]{1,0:T(8,128)(2,1)S(1)}, bf16[64,384]{1,0:T(8,128)(2,1)S(1)}) custom-call(s32[1,64]{1,0:T(1,128)S(1)} %copy-done.3, bf16[256,384]{1,0:T(8,128)(2,1)S(1)} %copy-done.1, bf16[256,768]{1,0:T(8,128)(2,1)S(1)} %collective-permute-done.4.refs_0_, ...), custom_call_target="tpu_custom_call" | custom-call | flops 1 | bytes 1 | tf_op jit(solution)/shard_map/attend8/pallas_call | solution.py:331
  72.9 0.6 copy-done.2
  73.5 1.4 %collective-permute-start.17 = (bf16[64,384]{1,0:T(8,128)(2,1)S(1)}, bf16[64,384]{1,0:T(8,128)(2,1)S(1)}, u32[]{:S(2)}, u32[]{:S(2)}) collective-permute-start(bf16[64,384]{1,0:T(8,128)(2,1)S(1)} %get-tuple-element.52), channel_id=1, source_target_pairs={{3,0},{0,1},{1,2},{2,3},{7,4},{4,5},{5,6},{6,7},{11,8},{8,9},{9,10... | collective-permute-start | bytes 147464 | tf_op jit(solution)/shard_map/ppermute | solution.py:147
  74.8 2.4 %collective-permute-start.18 = (bf16[64,384]{1,0:T(8,128)(2,1)S(1)}, bf16[64,384]{1,0:T(8,128)(2,1)S(1)}, u32[]{:S(2)}, u32[]{:S(2)}) collective-permute-start(bf16[64,384]{1,0:T(8,128)(2,1)S(1)} %get-tuple-element.53), channel_id=1, source_target_pairs={{2,0},{3,1},{0,2},{1,3},{6,4},{7,5},{4,6},{5,7},{10,8},{11,9},{8,1... | collective-permute-start | bytes 147464 | tf_op jit(solution)/shard_map/ppermute | solution.py:147
  77.2 1.2 %collective-permute-start.19 = (bf16[64,384]{1,0:T(8,128)(2,1)S(1)}, bf16[64,384]{1,0:T(8,128)(2,1)S(1)}, u32[]{:S(2)}, u32[]{:S(2)}) collective-permute-start(bf16[64,384]{1,0:T(8,128)(2,1)S(1)} %get-tuple-element.54), channel_id=1, source_target_pairs={{1,0},{2,1},{3,2},{0,3},{5,4},{6,5},{7,6},{4,7},{9,8},{10,9},{11,1... | collective-permute-start | bytes 147464 | tf_op jit(solution)/shard_map/ppermute | solution.py:147
  78.4 1.1 %collective-permute-done.18.p2 = bf16[64,384]{1,0:T(8,128)(2,1)S(1)} collective-permute-done((bf16[64,384]{1,0:T(8,128)(2,1)S(1)}, bf16[64,384]{1,0:T(8,128)(2,1)S(1)}, u32[]{:S(2)}, u32[]{:S(2)}) %collective-permute-start.18) | collective-permute-done | bytes 49184 | tf_op jit(solution)/shard_map/ppermute | solution.py:147
  79.5 0.9 %collective-permute-done.19.p3 = bf16[64,384]{1,0:T(8,128)(2,1)S(1)} collective-permute-done((bf16[64,384]{1,0:T(8,128)(2,1)S(1)}, bf16[64,384]{1,0:T(8,128)(2,1)S(1)}, u32[]{:S(2)}, u32[]{:S(2)}) %collective-permute-start.19) | collective-permute-done | bytes 49184 | tf_op jit(solution)/shard_map/ppermute | solution.py:147
  80.5 0.6 copy-done.10
  81.1 1.6 %place.1 = bf16[64,1536]{1,0:T(8,128)(2,1)} custom-call(bf16[64,384]{1,0:T(8,128)(2,1)} %copy-done.2, bf16[64,384]{1,0:T(8,128)(2,1)} %copy-done.8, bf16[64,384]{1,0:T(8,128)(2,1)} %copy-done.9, bf16[64,384]{1,0:T(8,128)(2,1)} %copy-done.10), custom_call_target="tpu_custom_call" | custom-call | flops 1 | bytes 1 | tf_op jit(solution)/shard_map/place/pallas_call | solution.py:63
  (39 shorter events, 2.8 us)
Async XLA Ops:
  2.1 12.7 %collective-permute-start = (bf16[64,1152]{1,0:T(8,128)(2,1)}, bf16[64,1152]{1,0:T(8,128)(2,1)S(1)}, u32[]{:S(2)}, u32[]{:S(2)}) collective-permute-start(bf16[64,1152]{1,0:T(8,128)(2,1)} %get-tuple-element.31), channel_id=1, source_target_pairs={{3,0},{0,1},{1,2},{2,3},{7,4},{4,5},{5,6},{6,7},{11,8},{8,9},{9,10... | collective-permute-start | bytes 442376 | tf_op jit(solution)/shard_map/ppermute | solution.py:147
  4.3 10.6 %collective-permute-start.1 = (bf16[64,1152]{1,0:T(8,128)(2,1)}, bf16[64,1152]{1,0:T(8,128)(2,1)S(1)}, u32[]{:S(2)}, u32[]{:S(2)}) collective-permute-start(bf16[64,1152]{1,0:T(8,128)(2,1)} %get-tuple-element.32), channel_id=1, source_target_pairs={{2,0},{3,1},{0,2},{1,3},{6,4},{7,5},{4,6},{5,7},{10,8},{11,9},{8,1... | collective-permute-start | bytes 442376 | tf_op jit(solution)/shard_map/ppermute | solution.py:147
  6.9 8.0 %collective-permute-start.2 = (bf16[64,1152]{1,0:T(8,128)(2,1)}, bf16[64,1152]{1,0:T(8,128)(2,1)S(1)}, u32[]{:S(2)}, u32[]{:S(2)}) collective-permute-start(bf16[64,1152]{1,0:T(8,128)(2,1)} %get-tuple-element.33), channel_id=1, source_target_pairs={{1,0},{2,1},{3,2},{0,3},{5,4},{6,5},{7,6},{4,7},{9,8},{10,9},{11,1... | collective-permute-start | bytes 442376 | tf_op jit(solution)/shard_map/ppermute | solution.py:147
  7.9 17.5 %collective-permute-start.3 = (bf16[64,3072]{1,0:T(8,128)(2,1)}, bf16[64,3072]{1,0:T(8,128)(2,1)S(1)}, u32[]{:S(2)}, u32[]{:S(2)}) collective-permute-start(bf16[64,3072]{1,0:T(8,128)(2,1)} %get-tuple-element.36), channel_id=1, source_target_pairs={{32,0},{36,4},{40,8},{44,12},{48,16},{52,20},{56,24},{60,28},{0,32... | collective-permute-start | bytes 1179656 | tf_op jit(solution)/shard_map/ppermute | solution.py:54
  14.9 0.7 copy-start.5
  14.9 0.7 copy-start.6
  14.9 0.7 copy-start.7
  17.6 14.0 %collective-permute-start.11 = (bf16[256,768]{1,0:T(8,128)(2,1)}, bf16[256,768]{1,0:T(8,128)(2,1)S(1)}, u32[]{:S(2)}, u32[]{:S(2)}) collective-permute-start(bf16[256,768]{1,0:T(8,128)(2,1)} %get-tuple-element.41.refs_0_), channel_id=1, source_target_pairs={{192,0},{196,4},{200,8},{204,12},{208,16},{212,20},{216,24},{220,2... | collective-permute-start | bytes 1179656 | tf_op jit(solution)/shard_map/ppermute | solution.py:54
  18.8 12.8 %collective-permute-start.9 = (bf16[256,768]{1,0:T(8,128)(2,1)}, bf16[256,768]{1,0:T(8,128)(2,1)S(1)}, u32[]{:S(2)}, u32[]{:S(2)}) collective-permute-start(bf16[256,768]{1,0:T(8,128)(2,1)} %get-tuple-element.41.refs_0_), channel_id=1, source_target_pairs={{64,0},{68,4},{72,8},{76,12},{80,16},{84,20},{88,24},{92,28},{96,3... | collective-permute-start | bytes 1179656 | tf_op jit(solution)/shard_map/ppermute | solution.py:54
  20.3 23.4 %collective-permute-start.5 = (bf16[256,768]{1,0:T(8,128)(2,1)}, bf16[256,768]{1,0:T(8,128)(2,1)S(1)}, u32[]{:S(2)}, u32[]{:S(2)}) collective-permute-start(bf16[256,768]{1,0:T(8,128)(2,1)} %get-tuple-element.41.refs_0_), channel_id=1, source_target_pairs={{8,0},{12,4},{16,8},{20,12},{24,16},{28,20},{32,24},{36,28},{40,32... | collective-permute-start | bytes 1179656 | tf_op jit(solution)/shard_map/ppermute | solution.py:54
  25.4 18.3 %collective-permute-start.6 = (bf16[256,768]{1,0:T(8,128)(2,1)}, bf16[256,768]{1,0:T(8,128)(2,1)S(1)}, u32[]{:S(2)}, u32[]{:S(2)}) collective-permute-start(bf16[256,768]{1,0:T(8,128)(2,1)} %get-tuple-element.41.refs_0_), channel_id=1, source_target_pairs={{248,0},{252,4},{0,8},{4,12},{8,16},{12,20},{16,24},{20,28},{24,32... | collective-permute-start | bytes 1179656 | tf_op jit(solution)/shard_map/ppermute | solution.py:54
  25.4 0.8 copy-start.4
  28.0 3.7 %copy-start = (bf16[256,768]{1,0:T(8,128)(2,1)S(1)}, bf16[256,768]{1,0:T(8,128)(2,1)}, u32[]{:S(2)}) copy-start(bf16[256,768]{1,0:T(8,128)(2,1)} %get-tuple-element.41.refs_0_) | copy-start | bytes 1179652
  28.0 15.7 %all-to-all-start = ((bf16[4,64,768]{2,1,0:T(8,128)(2,1)}), bf16[4,64,768]{2,1,0:T(8,128)(2,1)S(1)}, u32[]{:S(2)}, u32[]{:S(2)}) async-start(bf16[4,64,768]{2,1,0:T(8,128)(2,1)} %bitcast.4), calls=%async_computation | async-start | bytes 786432 | tf_op jit(solution)/shard_map/all_to_all | solution.py:354
  31.6 14.9 %copy-start.1 = (bf16[256,384]{1,0:T(8,128)(2,1)S(1)}, bf16[256,384]{1,0:T(8,128)(2,1)}, u32[]{:S(2)}) copy-start(bf16[256,384]{1,0:T(8,128)(2,1)} %get-tuple-element.34.q_ref) | copy-start | bytes 589828
  32.6 26.4 %collective-permute-start.10 = (bf16[256,768]{1,0:T(8,128)(2,1)}, bf16[256,768]{1,0:T(8,128)(2,1)S(1)}, u32[]{:S(2)}, u32[]{:S(2)}) collective-permute-start(bf16[256,768]{1,0:T(8,128)(2,1)} %get-tuple-element.56), channel_id=1, source_target_pairs={{16,0},{20,4},{24,8},{28,12},{32,16},{36,20},{40,24},{44,28},{48,3... | collective-permute-start | bytes 1179656 | tf_op jit(solution)/shard_map/ppermute | solution.py:54
  43.7 16.5 %collective-permute-start.12 = (bf16[256,768]{1,0:T(8,128)(2,1)}, bf16[256,768]{1,0:T(8,128)(2,1)S(1)}, u32[]{:S(2)}, u32[]{:S(2)}) collective-permute-start(bf16[256,768]{1,0:T(8,128)(2,1)} %get-tuple-element.55), channel_id=1, source_target_pairs={{48,0},{52,4},{56,8},{60,12},{0,16},{4,20},{8,24},{12,28},{16,32},... | collective-permute-start | bytes 1179656 | tf_op jit(solution)/shard_map/ppermute | solution.py:54
  43.7 2.9 %copy-start.3 = (s32[1,64]{1,0:T(1,128)S(1)}, s32[1,64]{1,0:T(1,128)}, u32[]{:S(2)}) copy-start(s32[1,64]{1,0:T(1,128)} %band_ref.3) | copy-start | bytes 772
  43.7 16.4 %collective-permute-start.14 = (bf16[256,768]{1,0:T(8,128)(2,1)S(1)}, bf16[256,768]{1,0:T(8,128)(2,1)S(1)}, u32[]{:S(2)}, u32[]{:S(2)}) collective-permute-start(bf16[256,768]{1,0:T(8,128)(2,1)S(1)} %copy-done), channel_id=1, source_target_pairs={{128,0},{132,4},{136,8},{140,12},{144,16},{148,20},{152,24},{156,2... | collective-permute-start | bytes 1179656 | tf_op jit(solution)/shard_map/ppermute | solution.py:54
  46.1 18.1 %collective-permute-start.13 = (bf16[256,768]{1,0:T(8,128)(2,1)S(1)}, bf16[256,768]{1,0:T(8,128)(2,1)S(1)}, u32[]{:S(2)}, u32[]{:S(2)}) collective-permute-start(bf16[256,768]{1,0:T(8,128)(2,1)S(1)} %bitcast.2), channel_id=1, source_target_pairs={{192,0},{196,4},{200,8},{204,12},{208,16},{212,20},{216,24},{220,2... | collective-permute-start | bytes 1179656 | tf_op jit(solution)/shard_map/ppermute | solution.py:54
  64.2 2.4 %collective-permute-start.15 = (bf16[256,768]{1,0:T(8,128)(2,1)S(1)}, bf16[256,768]{1,0:T(8,128)(2,1)S(1)}, u32[]{:S(2)}, u32[]{:S(2)}) collective-permute-start(bf16[256,768]{1,0:T(8,128)(2,1)S(1)} %collective-permute-done.10.refs_5_), channel_id=1, source_target_pairs={{4,0},{0,4},{12,8},{8,12},{20,16},{16,20},{28,24},{24,28},{36,32},... | collective-permute-start | bytes 1179656 | tf_op jit(solution)/shard_map/ppermute | solution.py:54
  65.2 1.9 %collective-permute-start.4 = (bf16[256,768]{1,0:T(8,128)(2,1)S(1)}, bf16[256,768]{1,0:T(8,128)(2,1)S(1)}, u32[]{:S(2)}, u32[]{:S(2)}) collective-permute-start(bf16[256,768]{1,0:T(8,128)(2,1)S(1)} %copy-done), channel_id=1, source_target_pairs={{4,0},{0,4},{12,8},{8,12},{20,16},{16,20},{28,24},{24,28},{36,32},... | collective-permute-start | bytes 1179656 | tf_op jit(solution)/shard_map/ppermute | solution.py:54
  65.3 2.5 %collective-permute-start.7 = (bf16[256,768]{1,0:T(8,128)(2,1)S(1)}, bf16[256,768]{1,0:T(8,128)(2,1)S(1)}, u32[]{:S(2)}, u32[]{:S(2)}) collective-permute-start(bf16[256,768]{1,0:T(8,128)(2,1)S(1)} %collective-permute-done.5.refs_4_), channel_id=1, source_target_pairs={{4,0},{0,4},{12,8},{8,12},{20,16},{16,20},{28,24},{24,28},{36,32},... | collective-permute-start | bytes 1179656 | tf_op jit(solution)/shard_map/ppermute | solution.py:54
  65.8 2.5 %collective-permute-start.8 = (bf16[256,768]{1,0:T(8,128)(2,1)S(1)}, bf16[256,768]{1,0:T(8,128)(2,1)S(1)}, u32[]{:S(2)}, u32[]{:S(2)}) collective-permute-start(bf16[256,768]{1,0:T(8,128)(2,1)S(1)} %collective-permute-done.6.refs_5_), channel_id=1, source_target_pairs={{4,0},{0,4},{12,8},{8,12},{20,16},{16,20},{28,24},{24,28},{36,32},... | collective-permute-start | bytes 1179656 | tf_op jit(solution)/shard_map/ppermute | solution.py:54
  66.6 2.2 %collective-permute-start.16 = (bf16[256,768]{1,0:T(8,128)(2,1)S(1)}, bf16[256,768]{1,0:T(8,128)(2,1)S(1)}, u32[]{:S(2)}, u32[]{:S(2)}) collective-permute-start(bf16[256,768]{1,0:T(8,128)(2,1)S(1)} %collective-permute-done.12.refs_6_), channel_id=1, source_target_pairs={{4,0},{0,4},{12,8},{8,12},{20,16},{16,20},{28,24},{24,28},{36,32},... | collective-permute-start | bytes 1179656 | tf_op jit(solution)/shard_map/ppermute | solution.py:54
  72.8 0.6 copy-start.2
  73.5 4.9 %collective-permute-start.17 = (bf16[64,384]{1,0:T(8,128)(2,1)S(1)}, bf16[64,384]{1,0:T(8,128)(2,1)S(1)}, u32[]{:S(2)}, u32[]{:S(2)}) collective-permute-start(bf16[64,384]{1,0:T(8,128)(2,1)S(1)} %get-tuple-element.52), channel_id=1, source_target_pairs={{3,0},{0,1},{1,2},{2,3},{7,4},{4,5},{5,6},{6,7},{11,8},{8,9},{9,10... | collective-permute-start | bytes 147464 | tf_op jit(solution)/shard_map/ppermute | solution.py:147
  74.8 4.7 %collective-permute-start.18 = (bf16[64,384]{1,0:T(8,128)(2,1)S(1)}, bf16[64,384]{1,0:T(8,128)(2,1)S(1)}, u32[]{:S(2)}, u32[]{:S(2)}) collective-permute-start(bf16[64,384]{1,0:T(8,128)(2,1)S(1)} %get-tuple-element.53), channel_id=1, source_target_pairs={{2,0},{3,1},{0,2},{1,3},{6,4},{7,5},{4,6},{5,7},{10,8},{11,9},{8,1... | collective-permute-start | bytes 147464 | tf_op jit(solution)/shard_map/ppermute | solution.py:147
  77.2 3.2 %collective-permute-start.19 = (bf16[64,384]{1,0:T(8,128)(2,1)S(1)}, bf16[64,384]{1,0:T(8,128)(2,1)S(1)}, u32[]{:S(2)}, u32[]{:S(2)}) collective-permute-start(bf16[64,384]{1,0:T(8,128)(2,1)S(1)} %get-tuple-element.54), channel_id=1, source_target_pairs={{1,0},{2,1},{3,2},{0,3},{5,4},{6,5},{7,6},{4,7},{9,8},{10,9},{11,1... | collective-permute-start | bytes 147464 | tf_op jit(solution)/shard_map/ppermute | solution.py:147
  78.4 2.1 %copy-start.8 = (bf16[64,384]{1,0:T(8,128)(2,1)}, bf16[64,384]{1,0:T(8,128)(2,1)S(1)}, u32[]{:S(2)}) copy-start(bf16[64,384]{1,0:T(8,128)(2,1)S(1)} %collective-permute-done.17.p1) | copy-start | bytes 147460
  79.5 0.9 %copy-start.9 = (bf16[64,384]{1,0:T(8,128)(2,1)}, bf16[64,384]{1,0:T(8,128)(2,1)S(1)}, u32[]{:S(2)}) copy-start(bf16[64,384]{1,0:T(8,128)(2,1)S(1)} %collective-permute-done.18.p2) | copy-start | bytes 147460
  80.5 0.6 copy-start.10

commit v5 on v4

--- a/solution.py
+++ b/solution.py
@@ -364,7 +364,9 @@
     sent, sent1, sent2, *_ = barrier((own, next1, prev1, z4))
     x2 = move(sent, from_x(2))
     next1p, prev1p = move(sent1, FROM_PARTNER), move(sent2, FROM_PARTNER)
-    state = step(None, own=own, xnext=xnext, xprev=xprev, z4=z4, next1=next1, prev1=prev1)
+    state = step(
+        None, own=own, partner=partner, xnext=xnext, xprev=xprev, z4=z4, next1=next1, prev1=prev1
+    )
     next2, prev2, z4x, x2, state = barrier((next2, prev2, z4x, x2, state))
     next2p = move(next2, FROM_PARTNER)
     sent, _ = barrier((prev2, next2p))
@@ -372,7 +374,6 @@
     outs = step(
         state,
         True,
-        partner=partner,
         next1p=next1p,
         prev1p=prev1p,
         x2=x2,

time: 82.9 us -> 85 us (1.025)
  starting transfers between devices: 44.9 us -> 47.6 us
  waiting for transfers between devices: 19.7 us -> 18.7 us
    ppermute x14, starting transfers between devices: 30.6 us -> 33 us  [move(): return lax.ppermute(block, 'frame', pairs)]
    ppermute x14, waiting for transfers between devices: 17.7 us -> 16.6 us  [move(): return lax.ppermute(block, 'frame', pairs)]
  transfers between devices with their start and end apart: 21 -> 21, of which waited for: 10 -> 9; matrix products, arithmetic and copies ran while one was open for 1% -> 1% of each run, Pallas kernels for 8% -> 9%
where the time goes in v5:
time: 85 us; the launch traced here: 84.6 us
  starting transfers between devices  47.6 us (56%)
  waiting for transfers between devices  18.7 us (22%)
  Pallas kernels  14.5 us (17%)
  local copies, waits for them, and re-layouts  2.73 us (3%)
  other arithmetic  0.98 us (1%)
    ppermute x14, starting transfers between devices, move(): return lax.ppermute(block, 'frame', pairs)  33 us
    ppermute x14, waiting for transfers between devices, move(): return lax.ppermute(block, 'frame', pairs)  16.6 us
    ppermute x6, starting transfers between devices, over_heads(): lax.ppermute(pieces[s], 'head', y_from(s))  11 us
    pallas_call x4, Pallas kernels, copier(): pl.pallas_call(kernel, out_shape=out_shape, in_specs=[VMEM] * len(arrays)...  7.47 us
    pallas_call x2, Pallas kernels, attend(): pl.pallas_call(functools.partial(attend_kernel, names, kinds, first, last...  7 us
    all_to_all x1, starting transfers between devices, shards(): lax.all_to_all(z4_packed, 'head', split_axis=0, concat_axis=0, tiled=True)  3.59 us
    unnamed x22, local copies, waits for them, and re-layouts  2.73 us
    ppermute x6, waiting for transfers between devices, over_heads(): lax.ppermute(pieces[s], 'head', y_from(s))  2.06 us
  transfers between devices with their start and end apart: 21, of which 9 were waited for; matrix products, arithmetic and copies ran while one was open for 1% of the time, Pallas kernels for 9%

profile of v5, /device:TPU:1, one launch (start us, length us, event | category | flops | bytes accessed | tf_op | source)
XLA Modules:
  0.0 84.6 jit_solution(12872020418771636002)
XLA Ops:
  0.0 2.1 %pack.1 = (bf16[64,1152]{1,0:T(8,128)(2,1)}, bf16[64,1152]{1,0:T(8,128)(2,1)}, bf16[64,1152]{1,0:T(8,128)(2,1)}, bf16[64,1152]{1,0:T(8,128)(2,1)}, bf16[64,3072]{1,0:T(8,128)(2,1)}) custom-call(bf16[64,1536]{1,0:T(8,128)(2,1)} %k_ref.1, bf16[64,1536]{1,0:T(8,128)(2,1)} %v_ref.1, bf16[64,1536]{1,0:T(8,128)(2,1)} %q_ref.1), custom_call_target="tpu_custom_call" | custom-call | flops 1 | bytes 1 | tf_op jit(solution)/shard_map/pack/pallas_call | solution.py:63
  2.1 2.1 %collective-permute-start = (bf16[64,1152]{1,0:T(8,128)(2,1)}, bf16[64,1152]{1,0:T(8,128)(2,1)S(1)}, u32[]{:S(2)}, u32[]{:S(2)}) collective-permute-start(bf16[64,1152]{1,0:T(8,128)(2,1)} %get-tuple-element.31), channel_id=1, source_target_pairs={{3,0},{0,1},{1,2},{2,3},{7,4},{4,5},{5,6},{6,7},{11,8},{8,9},{9,10... | collective-permute-start | bytes 442376 | tf_op jit(solution)/shard_map/ppermute | solution.py:147
  4.3 2.6 %collective-permute-start.1 = (bf16[64,1152]{1,0:T(8,128)(2,1)}, bf16[64,1152]{1,0:T(8,128)(2,1)S(1)}, u32[]{:S(2)}, u32[]{:S(2)}) collective-permute-start(bf16[64,1152]{1,0:T(8,128)(2,1)} %get-tuple-element.32), channel_id=1, source_target_pairs={{2,0},{3,1},{0,2},{1,3},{6,4},{7,5},{4,6},{5,7},{10,8},{11,9},{8,1... | collective-permute-start | bytes 442376 | tf_op jit(solution)/shard_map/ppermute | solution.py:147
  6.9 1.1 %collective-permute-start.2 = (bf16[64,1152]{1,0:T(8,128)(2,1)}, bf16[64,1152]{1,0:T(8,128)(2,1)S(1)}, u32[]{:S(2)}, u32[]{:S(2)}) collective-permute-start(bf16[64,1152]{1,0:T(8,128)(2,1)} %get-tuple-element.33), channel_id=1, source_target_pairs={{1,0},{2,1},{3,2},{0,3},{5,4},{6,5},{7,6},{4,7},{9,8},{10,9},{11,1... | collective-permute-start | bytes 442376 | tf_op jit(solution)/shard_map/ppermute | solution.py:147
  7.9 6.9 %collective-permute-start.5 = (bf16[64,3072]{1,0:T(8,128)(2,1)}, bf16[64,3072]{1,0:T(8,128)(2,1)S(1)}, u32[]{:S(2)}, u32[]{:S(2)}) collective-permute-start(bf16[64,3072]{1,0:T(8,128)(2,1)} %get-tuple-element.36), channel_id=1, source_target_pairs={{32,0},{36,4},{40,8},{44,12},{48,16},{52,20},{56,24},{60,28},{0,32... | collective-permute-start | bytes 1179656 | tf_op jit(solution)/shard_map/ppermute | solution.py:54
  14.9 0.6 copy-done.5
  15.6 2.0 %join.1 = (bf16[256,768]{1,0:T(8,128)(2,1)}, bf16[256,384]{1,0:T(8,128)(2,1)}) custom-call(bf16[64,1152]{1,0:T(8,128)(2,1)} %get-tuple-element.30.p0, bf16[64,1152]{1,0:T(8,128)(2,1)} %copy-done.5, bf16[64,1152]{1,0:T(8,128)(2,1)} %copy-done.6, bf16[64,1152]{1,0:T(8,128)(2,1)} %copy-done.7), custom_call_target="tpu_custom_call" | custom-call | flops 1 | bytes 1 | tf_op jit(solution)/shard_map/join/pallas_call | solution.py:63
  17.6 1.2 %collective-permute-start.10 = (bf16[256,768]{1,0:T(8,128)(2,1)}, bf16[256,768]{1,0:T(8,128)(2,1)S(1)}, u32[]{:S(2)}, u32[]{:S(2)}) collective-permute-start(bf16[256,768]{1,0:T(8,128)(2,1)} %get-tuple-element.41.refs_0_), channel_id=1, source_target_pairs={{192,0},{196,4},{200,8},{204,12},{208,16},{212,20},{216,24},{220,2... | collective-permute-start | bytes 1179656 | tf_op jit(solution)/shard_map/ppermute | solution.py:54
  18.8 1.5 %collective-permute-start.8 = (bf16[256,768]{1,0:T(8,128)(2,1)}, bf16[256,768]{1,0:T(8,128)(2,1)S(1)}, u32[]{:S(2)}, u32[]{:S(2)}) collective-permute-start(bf16[256,768]{1,0:T(8,128)(2,1)} %get-tuple-element.41.refs_0_), channel_id=1, source_target_pairs={{64,0},{68,4},{72,8},{76,12},{80,16},{84,20},{88,24},{92,28},{96,3... | collective-permute-start | bytes 1179656 | tf_op jit(solution)/shard_map/ppermute | solution.py:54
  20.3 5.1 %collective-permute-start.3 = (bf16[256,768]{1,0:T(8,128)(2,1)}, bf16[256,768]{1,0:T(8,128)(2,1)S(1)}, u32[]{:S(2)}, u32[]{:S(2)}) collective-permute-start(bf16[256,768]{1,0:T(8,128)(2,1)} %get-tuple-element.41.refs_0_), channel_id=1, source_target_pairs={{8,0},{12,4},{16,8},{20,12},{24,16},{28,20},{32,24},{36,28},{40,32... | collective-permute-start | bytes 1179656 | tf_op jit(solution)/shard_map/ppermute | solution.py:54
  25.4 0.8 copy-done.4
  26.2 1.8 %unpack.1 = bf16[256,768]{1,0:T(8,128)(2,1)} custom-call(bf16[64,3072]{1,0:T(8,128)(2,1)} %copy-done.4), custom_call_target="tpu_custom_call" | custom-call | flops 1 | bytes 1 | tf_op jit(solution)/shard_map/unpack/pallas_call | solution.py:63
  28.0 3.6 %all-to-all-start = ((bf16[4,64,768]{2,1,0:T(8,128)(2,1)}), bf16[4,64,768]{2,1,0:T(8,128)(2,1)S(1)}, u32[]{:S(2)}, u32[]{:S(2)}) async-start(bf16[4,64,768]{2,1,0:T(8,128)(2,1)} %bitcast.4), calls=%async_computation | async-start | bytes 786432 | tf_op jit(solution)/shard_map/all_to_all | solution.py:354
  31.6 4.7 %collective-permute-start.14 = (bf16[256,768]{1,0:T(8,128)(2,1)S(1)}, bf16[256,768]{1,0:T(8,128)(2,1)}, u32[]{:S(2)}, u32[]{:S(2)}) collective-permute-start(bf16[256,768]{1,0:T(8,128)(2,1)S(1)} %copy-done), channel_id=1, source_target_pairs={{4,0},{0,4},{12,8},{8,12},{20,16},{16,20},{28,24},{24,28},{36,32},... | collective-permute-start | bytes 1179656 | tf_op jit(solution)/shard_map/ppermute | solution.py:54
  36.3 1.0 %broadcast_select_fusion = (bf16[256,768]{1,0:T(8,128)(2,1)}, bf16[256,768]{1,0:T(8,128)(2,1)}) fusion(bf16[256,768]{1,0:T(8,128)(2,1)S(1)} %collective-permute-done.10.refs_3_, bf16[256,768]{1,0:T(8,128)(2,1)S(1)} %copy-done, pred[]{:T(512)S(6)} %ge.3, bf16[256,768]{1,0:T(8,128)(2,1)S(1)} %collective-permute-done.8.refs_2_, pred[]{:T(512)S(6)} %lt.10), kind=kLoop, calls=%fused_computation | loop fusion | flops 393216 | bytes 1966082 | tf_op jit(solution)/shard_map/jit(_where)/select_n | solution.py:362
  37.3 5.8 %collective-permute-start.11 = (bf16[256,768]{1,0:T(8,128)(2,1)}, bf16[256,768]{1,0:T(8,128)(2,1)S(1)}, u32[]{:S(2)}, u32[]{:S(2)}) collective-permute-start(bf16[256,768]{1,0:T(8,128)(2,1)} %get-tuple-element.55), channel_id=1, source_target_pairs={{48,0},{52,4},{56,8},{60,12},{0,16},{4,20},{8,24},{12,28},{16,32},... | collective-permute-start | bytes 1179656 | tf_op jit(solution)/shard_map/ppermute | solution.py:54
  43.2 3.2 %collective-permute-start.9 = (bf16[256,768]{1,0:T(8,128)(2,1)}, bf16[256,768]{1,0:T(8,128)(2,1)S(1)}, u32[]{:S(2)}, u32[]{:S(2)}) collective-permute-start(bf16[256,768]{1,0:T(8,128)(2,1)} %get-tuple-element.56), channel_id=1, source_target_pairs={{16,0},{20,4},{24,8},{28,12},{32,16},{36,20},{40,24},{44,28},{48,3... | collective-permute-start | bytes 1179656 | tf_op jit(solution)/shard_map/ppermute | solution.py:54
  46.4 2.6 %collective-permute-start.13 = (bf16[256,768]{1,0:T(8,128)(2,1)S(1)}, bf16[256,768]{1,0:T(8,128)(2,1)S(1)}, u32[]{:S(2)}, u32[]{:S(2)}) collective-permute-start(bf16[256,768]{1,0:T(8,128)(2,1)S(1)} %copy-done), channel_id=1, source_target_pairs={{128,0},{132,4},{136,8},{140,12},{144,16},{148,20},{152,24},{156,2... | collective-permute-start | bytes 1179656 | tf_op jit(solution)/shard_map/ppermute | solution.py:54
  49.6 3.5 %attend7.2 = (f32[256,128]{1,0:T(8,128)S(1)}, f32[256,384]{1,0:T(8,128)S(1)}) custom-call(s32[1,64]{1,0:T(1,128)S(1)} %copy-done.3, bf16[256,384]{1,0:T(8,128)(2,1)S(1)} %copy-done.1, bf16[256,768]{1,0:T(8,128)(2,1)S(1)} %copy-done, bf16[256,768]{1,0:T(8,128)(2,1)} %collective-permute-done.14.refs_1_, bf16[256,768]{1,0:T(8,128)(2,1)S(1)} %collective-permute-done.8.refs_2_, ...), custom_call_target="tpu_custom_call" | custom-call | flops 1 | bytes 1 | tf_op jit(solution)/shard_map/attend7/pallas_call | solution.py:331
  53.1 6.2 %collective-permute-done.11.refs_5_ = bf16[256,768]{1,0:T(8,128)(2,1)S(1)} collective-permute-done((bf16[256,768]{1,0:T(8,128)(2,1)}, bf16[256,768]{1,0:T(8,128)(2,1)S(1)}, u32[]{:S(2)}, u32[]{:S(2)}) %collective-permute-start.11) | collective-permute-done | bytes 393248 | tf_op jit(solution)/shard_map/ppermute | solution.py:54
  59.3 4.2 %collective-permute-done.9.refs_4_ = bf16[256,768]{1,0:T(8,128)(2,1)S(1)} collective-permute-done((bf16[256,768]{1,0:T(8,128)(2,1)}, bf16[256,768]{1,0:T(8,128)(2,1)S(1)}, u32[]{:S(2)}, u32[]{:S(2)}) %collective-permute-start.9) | collective-permute-done | bytes 393248 | tf_op jit(solution)/shard_map/ppermute | solution.py:54
  63.6 3.9 %collective-permute-done.12.refs_3_ = bf16[256,768]{1,0:T(8,128)(2,1)S(1)} collective-permute-done((bf16[256,768]{1,0:T(8,128)(2,1)S(1)}, bf16[256,768]{1,0:T(8,128)(2,1)S(1)}, u32[]{:S(2)}, u32[]{:S(2)}) %collective-permute-start.12) | collective-permute-done | bytes 393248 | tf_op jit(solution)/shard_map/ppermute | solution.py:54
  68.5 0.8 collective-permute-done.15.refs_7_
  71.1 3.5 %attend7.3 = (bf16[64,384]{1,0:T(8,128)(2,1)S(1)}, bf16[64,384]{1,0:T(8,128)(2,1)S(1)}, bf16[64,384]{1,0:T(8,128)(2,1)S(1)}, bf16[64,384]{1,0:T(8,128)(2,1)S(1)}) custom-call(s32[1,64]{1,0:T(1,128)S(1)} %copy-done.3, bf16[256,384]{1,0:T(8,128)(2,1)S(1)} %copy-done.1, bf16[256,768]{1,0:T(8,128)(2,1)S(1)} %collective-permute-done.6.refs_0_, ...), custom_call_target="tpu_custom_call" | custom-call | flops 1 | bytes 1 | tf_op jit(solution)/shard_map/attend7/pallas_call | solution.py:331
  74.6 0.6 copy-done.2
  75.2 1.6 %collective-permute-start.17 = (bf16[64,384]{1,0:T(8,128)(2,1)S(1)}, bf16[64,384]{1,0:T(8,128)(2,1)S(1)}, u32[]{:S(2)}, u32[]{:S(2)}) collective-permute-start(bf16[64,384]{1,0:T(8,128)(2,1)S(1)} %get-tuple-element.52), channel_id=1, source_target_pairs={{3,0},{0,1},{1,2},{2,3},{7,4},{4,5},{5,6},{6,7},{11,8},{8,9},{9,10... | collective-permute-start | bytes 147464 | tf_op jit(solution)/shard_map/ppermute | solution.py:147
  76.8 2.4 %collective-permute-start.18 = (bf16[64,384]{1,0:T(8,128)(2,1)S(1)}, bf16[64,384]{1,0:T(8,128)(2,1)S(1)}, u32[]{:S(2)}, u32[]{:S(2)}) collective-permute-start(bf16[64,384]{1,0:T(8,128)(2,1)S(1)} %get-tuple-element.53), channel_id=1, source_target_pairs={{2,0},{3,1},{0,2},{1,3},{6,4},{7,5},{4,6},{5,7},{10,8},{11,9},{8,1... | collective-permute-start | bytes 147464 | tf_op jit(solution)/shard_map/ppermute | solution.py:147
  79.2 1.2 %collective-permute-start.19 = (bf16[64,384]{1,0:T(8,128)(2,1)S(1)}, bf16[64,384]{1,0:T(8,128)(2,1)S(1)}, u32[]{:S(2)}, u32[]{:S(2)}) collective-permute-start(bf16[64,384]{1,0:T(8,128)(2,1)S(1)} %get-tuple-element.54), channel_id=1, source_target_pairs={{1,0},{2,1},{3,2},{0,3},{5,4},{6,5},{7,6},{4,7},{9,8},{10,9},{11,1... | collective-permute-start | bytes 147464 | tf_op jit(solution)/shard_map/ppermute | solution.py:147
  80.3 1.1 %collective-permute-done.18.p2 = bf16[64,384]{1,0:T(8,128)(2,1)S(1)} collective-permute-done((bf16[64,384]{1,0:T(8,128)(2,1)S(1)}, bf16[64,384]{1,0:T(8,128)(2,1)S(1)}, u32[]{:S(2)}, u32[]{:S(2)}) %collective-permute-start.18) | collective-permute-done | bytes 49184 | tf_op jit(solution)/shard_map/ppermute | solution.py:147
  81.5 0.9 %collective-permute-done.19.p3 = bf16[64,384]{1,0:T(8,128)(2,1)S(1)} collective-permute-done((bf16[64,384]{1,0:T(8,128)(2,1)S(1)}, bf16[64,384]{1,0:T(8,128)(2,1)S(1)}, u32[]{:S(2)}, u32[]{:S(2)}) %collective-permute-start.19) | collective-permute-done | bytes 49184 | tf_op jit(solution)/shard_map/ppermute | solution.py:147
  82.4 0.6 copy-done.10
  83.0 1.6 %place.1 = bf16[64,1536]{1,0:T(8,128)(2,1)} custom-call(bf16[64,384]{1,0:T(8,128)(2,1)} %copy-done.2, bf16[64,384]{1,0:T(8,128)(2,1)} %copy-done.8, bf16[64,384]{1,0:T(8,128)(2,1)} %copy-done.9, bf16[64,384]{1,0:T(8,128)(2,1)} %copy-done.10), custom_call_target="tpu_custom_call" | custom-call | flops 1 | bytes 1 | tf_op jit(solution)/shard_map/place/pallas_call | solution.py:63
  (39 shorter events, 3.5 us)
Async XLA Ops:
  2.1 12.7 %collective-permute-start = (bf16[64,1152]{1,0:T(8,128)(2,1)}, bf16[64,1152]{1,0:T(8,128)(2,1)S(1)}, u32[]{:S(2)}, u32[]{:S(2)}) collective-permute-start(bf16[64,1152]{1,0:T(8,128)(2,1)} %get-tuple-element.31), channel_id=1, source_target_pairs={{3,0},{0,1},{1,2},{2,3},{7,4},{4,5},{5,6},{6,7},{11,8},{8,9},{9,10... | collective-permute-start | bytes 442376 | tf_op jit(solution)/shard_map/ppermute | solution.py:147
  4.3 10.6 %collective-permute-start.1 = (bf16[64,1152]{1,0:T(8,128)(2,1)}, bf16[64,1152]{1,0:T(8,128)(2,1)S(1)}, u32[]{:S(2)}, u32[]{:S(2)}) collective-permute-start(bf16[64,1152]{1,0:T(8,128)(2,1)} %get-tuple-element.32), channel_id=1, source_target_pairs={{2,0},{3,1},{0,2},{1,3},{6,4},{7,5},{4,6},{5,7},{10,8},{11,9},{8,1... | collective-permute-start | bytes 442376 | tf_op jit(solution)/shard_map/ppermute | solution.py:147
  6.9 8.0 %collective-permute-start.2 = (bf16[64,1152]{1,0:T(8,128)(2,1)}, bf16[64,1152]{1,0:T(8,128)(2,1)S(1)}, u32[]{:S(2)}, u32[]{:S(2)}) collective-permute-start(bf16[64,1152]{1,0:T(8,128)(2,1)} %get-tuple-element.33), channel_id=1, source_target_pairs={{1,0},{2,1},{3,2},{0,3},{5,4},{6,5},{7,6},{4,7},{9,8},{10,9},{11,1... | collective-permute-start | bytes 442376 | tf_op jit(solution)/shard_map/ppermute | solution.py:147
  7.9 17.5 %collective-permute-start.5 = (bf16[64,3072]{1,0:T(8,128)(2,1)}, bf16[64,3072]{1,0:T(8,128)(2,1)S(1)}, u32[]{:S(2)}, u32[]{:S(2)}) collective-permute-start(bf16[64,3072]{1,0:T(8,128)(2,1)} %get-tuple-element.36), channel_id=1, source_target_pairs={{32,0},{36,4},{40,8},{44,12},{48,16},{52,20},{56,24},{60,28},{0,32... | collective-permute-start | bytes 1179656 | tf_op jit(solution)/shard_map/ppermute | solution.py:54
  14.9 0.7 copy-start.5
  14.9 0.7 copy-start.6
  14.9 0.7 copy-start.7
  17.6 18.7 %collective-permute-start.10 = (bf16[256,768]{1,0:T(8,128)(2,1)}, bf16[256,768]{1,0:T(8,128)(2,1)S(1)}, u32[]{:S(2)}, u32[]{:S(2)}) collective-permute-start(bf16[256,768]{1,0:T(8,128)(2,1)} %get-tuple-element.41.refs_0_), channel_id=1, source_target_pairs={{192,0},{196,4},{200,8},{204,12},{208,16},{212,20},{216,24},{220,2... | collective-permute-start | bytes 1179656 | tf_op jit(solution)/shard_map/ppermute | solution.py:54
  18.8 17.5 %collective-permute-start.8 = (bf16[256,768]{1,0:T(8,128)(2,1)}, bf16[256,768]{1,0:T(8,128)(2,1)S(1)}, u32[]{:S(2)}, u32[]{:S(2)}) collective-permute-start(bf16[256,768]{1,0:T(8,128)(2,1)} %get-tuple-element.41.refs_0_), channel_id=1, source_target_pairs={{64,0},{68,4},{72,8},{76,12},{80,16},{84,20},{88,24},{92,28},{96,3... | collective-permute-start | bytes 1179656 | tf_op jit(solution)/shard_map/ppermute | solution.py:54
  20.3 26.1 %collective-permute-start.3 = (bf16[256,768]{1,0:T(8,128)(2,1)}, bf16[256,768]{1,0:T(8,128)(2,1)S(1)}, u32[]{:S(2)}, u32[]{:S(2)}) collective-permute-start(bf16[256,768]{1,0:T(8,128)(2,1)} %get-tuple-element.41.refs_0_), channel_id=1, source_target_pairs={{8,0},{12,4},{16,8},{20,12},{24,16},{28,20},{32,24},{36,28},{40,32... | collective-permute-start | bytes 1179656 | tf_op jit(solution)/shard_map/ppermute | solution.py:54
  25.4 21.0 %collective-permute-start.4 = (bf16[256,768]{1,0:T(8,128)(2,1)}, bf16[256,768]{1,0:T(8,128)(2,1)S(1)}, u32[]{:S(2)}, u32[]{:S(2)}) collective-permute-start(bf16[256,768]{1,0:T(8,128)(2,1)} %get-tuple-element.41.refs_0_), channel_id=1, source_target_pairs={{248,0},{252,4},{0,8},{4,12},{8,16},{12,20},{16,24},{20,28},{24,32... | collective-permute-start | bytes 1179656 | tf_op jit(solution)/shard_map/ppermute | solution.py:54
  25.4 0.8 copy-start.4
  28.0 3.6 %copy-start = (bf16[256,768]{1,0:T(8,128)(2,1)S(1)}, bf16[256,768]{1,0:T(8,128)(2,1)}, u32[]{:S(2)}) copy-start(bf16[256,768]{1,0:T(8,128)(2,1)} %get-tuple-element.41.refs_0_) | copy-start | bytes 1179652
  28.0 18.4 %all-to-all-start = ((bf16[4,64,768]{2,1,0:T(8,128)(2,1)}), bf16[4,64,768]{2,1,0:T(8,128)(2,1)S(1)}, u32[]{:S(2)}, u32[]{:S(2)}) async-start(bf16[4,64,768]{2,1,0:T(8,128)(2,1)} %bitcast.4), calls=%async_computation | async-start | bytes 786432 | tf_op jit(solution)/shard_map/all_to_all | solution.py:354
  31.6 18.0 %copy-start.1 = (bf16[256,384]{1,0:T(8,128)(2,1)S(1)}, bf16[256,384]{1,0:T(8,128)(2,1)}, u32[]{:S(2)}) copy-start(bf16[256,384]{1,0:T(8,128)(2,1)} %get-tuple-element.34.q_ref) | copy-start | bytes 589828
  31.6 18.0 %collective-permute-start.14 = (bf16[256,768]{1,0:T(8,128)(2,1)S(1)}, bf16[256,768]{1,0:T(8,128)(2,1)}, u32[]{:S(2)}, u32[]{:S(2)}) collective-permute-start(bf16[256,768]{1,0:T(8,128)(2,1)S(1)} %copy-done), channel_id=1, source_target_pairs={{4,0},{0,4},{12,8},{8,12},{20,16},{16,20},{28,24},{24,28},{36,32},... | collective-permute-start | bytes 1179656 | tf_op jit(solution)/shard_map/ppermute | solution.py:54
  37.3 22.0 %collective-permute-start.11 = (bf16[256,768]{1,0:T(8,128)(2,1)}, bf16[256,768]{1,0:T(8,128)(2,1)S(1)}, u32[]{:S(2)}, u32[]{:S(2)}) collective-permute-start(bf16[256,768]{1,0:T(8,128)(2,1)} %get-tuple-element.55), channel_id=1, source_target_pairs={{48,0},{52,4},{56,8},{60,12},{0,16},{4,20},{8,24},{12,28},{16,32},... | collective-permute-start | bytes 1179656 | tf_op jit(solution)/shard_map/ppermute | solution.py:54
  43.2 20.4 %collective-permute-start.9 = (bf16[256,768]{1,0:T(8,128)(2,1)}, bf16[256,768]{1,0:T(8,128)(2,1)S(1)}, u32[]{:S(2)}, u32[]{:S(2)}) collective-permute-start(bf16[256,768]{1,0:T(8,128)(2,1)} %get-tuple-element.56), channel_id=1, source_target_pairs={{16,0},{20,4},{24,8},{28,12},{32,16},{36,20},{40,24},{44,28},{48,3... | collective-permute-start | bytes 1179656 | tf_op jit(solution)/shard_map/ppermute | solution.py:54
  46.4 3.2 %copy-start.3 = (s32[1,64]{1,0:T(1,128)S(1)}, s32[1,64]{1,0:T(1,128)}, u32[]{:S(2)}) copy-start(s32[1,64]{1,0:T(1,128)} %band_ref.3) | copy-start | bytes 772
  46.4 17.1 %collective-permute-start.13 = (bf16[256,768]{1,0:T(8,128)(2,1)S(1)}, bf16[256,768]{1,0:T(8,128)(2,1)S(1)}, u32[]{:S(2)}, u32[]{:S(2)}) collective-permute-start(bf16[256,768]{1,0:T(8,128)(2,1)S(1)} %copy-done), channel_id=1, source_target_pairs={{128,0},{132,4},{136,8},{140,12},{144,16},{148,20},{152,24},{156,2... | collective-permute-start | bytes 1179656 | tf_op jit(solution)/shard_map/ppermute | solution.py:54
  49.0 18.5 %collective-permute-start.12 = (bf16[256,768]{1,0:T(8,128)(2,1)S(1)}, bf16[256,768]{1,0:T(8,128)(2,1)S(1)}, u32[]{:S(2)}, u32[]{:S(2)}) collective-permute-start(bf16[256,768]{1,0:T(8,128)(2,1)S(1)} %bitcast.2), channel_id=1, source_target_pairs={{192,0},{196,4},{200,8},{204,12},{208,16},{212,20},{216,24},{220,2... | collective-permute-start | bytes 1179656 | tf_op jit(solution)/shard_map/ppermute | solution.py:54
  67.5 1.8 %collective-permute-start.15 = (bf16[256,768]{1,0:T(8,128)(2,1)S(1)}, bf16[256,768]{1,0:T(8,128)(2,1)S(1)}, u32[]{:S(2)}, u32[]{:S(2)}) collective-permute-start(bf16[256,768]{1,0:T(8,128)(2,1)S(1)} %collective-permute-done.9.refs_4_), channel_id=1, source_target_pairs={{4,0},{0,4},{12,8},{8,12},{20,16},{16,20},{28,24},{24,28},{36,32},... | collective-permute-start | bytes 1179656 | tf_op jit(solution)/shard_map/ppermute | solution.py:54
  68.0 1.9 %collective-permute-start.6 = (bf16[256,768]{1,0:T(8,128)(2,1)S(1)}, bf16[256,768]{1,0:T(8,128)(2,1)S(1)}, u32[]{:S(2)}, u32[]{:S(2)}) collective-permute-start(bf16[256,768]{1,0:T(8,128)(2,1)S(1)} %collective-permute-done.3.refs_5_), channel_id=1, source_target_pairs={{4,0},{0,4},{12,8},{8,12},{20,16},{16,20},{28,24},{24,28},{36,32},... | collective-permute-start | bytes 1179656 | tf_op jit(solution)/shard_map/ppermute | solution.py:54
  68.0 2.5 %collective-permute-start.7 = (bf16[256,768]{1,0:T(8,128)(2,1)S(1)}, bf16[256,768]{1,0:T(8,128)(2,1)S(1)}, u32[]{:S(2)}, u32[]{:S(2)}) collective-permute-start(bf16[256,768]{1,0:T(8,128)(2,1)S(1)} %collective-permute-done.4.refs_6_), channel_id=1, source_target_pairs={{4,0},{0,4},{12,8},{8,12},{20,16},{16,20},{28,24},{24,28},{36,32},... | collective-permute-start | bytes 1179656 | tf_op jit(solution)/shard_map/ppermute | solution.py:54
  69.3 1.7 %collective-permute-start.16 = (bf16[256,768]{1,0:T(8,128)(2,1)S(1)}, bf16[256,768]{1,0:T(8,128)(2,1)S(1)}, u32[]{:S(2)}, u32[]{:S(2)}) collective-permute-start(bf16[256,768]{1,0:T(8,128)(2,1)S(1)} %collective-permute-done.11.refs_5_), channel_id=1, source_target_pairs={{4,0},{0,4},{12,8},{8,12},{20,16},{16,20},{28,24},{24,28},{36,32},... | collective-permute-start | bytes 1179656 | tf_op jit(solution)/shard_map/ppermute | solution.py:54
  74.6 0.6 copy-start.2
  75.2 5.2 %collective-permute-start.17 = (bf16[64,384]{1,0:T(8,128)(2,1)S(1)}, bf16[64,384]{1,0:T(8,128)(2,1)S(1)}, u32[]{:S(2)}, u32[]{:S(2)}) collective-permute-start(bf16[64,384]{1,0:T(8,128)(2,1)S(1)} %get-tuple-element.52), channel_id=1, source_target_pairs={{3,0},{0,1},{1,2},{2,3},{7,4},{4,5},{5,6},{6,7},{11,8},{8,9},{9,10... | collective-permute-start | bytes 147464 | tf_op jit(solution)/shard_map/ppermute | solution.py:147
  76.8 4.7 %collective-permute-start.18 = (bf16[64,384]{1,0:T(8,128)(2,1)S(1)}, bf16[64,384]{1,0:T(8,128)(2,1)S(1)}, u32[]{:S(2)}, u32[]{:S(2)}) collective-permute-start(bf16[64,384]{1,0:T(8,128)(2,1)S(1)} %get-tuple-element.53), channel_id=1, source_target_pairs={{2,0},{3,1},{0,2},{1,3},{6,4},{7,5},{4,6},{5,7},{10,8},{11,9},{8,1... | collective-permute-start | bytes 147464 | tf_op jit(solution)/shard_map/ppermute | solution.py:147
  79.2 3.2 %collective-permute-start.19 = (bf16[64,384]{1,0:T(8,128)(2,1)S(1)}, bf16[64,384]{1,0:T(8,128)(2,1)S(1)}, u32[]{:S(2)}, u32[]{:S(2)}) collective-permute-start(bf16[64,384]{1,0:T(8,128)(2,1)S(1)} %get-tuple-element.54), channel_id=1, source_target_pairs={{1,0},{2,1},{3,2},{0,3},{5,4},{6,5},{7,6},{4,7},{9,8},{10,9},{11,1... | collective-permute-start | bytes 147464 | tf_op jit(solution)/shard_map/ppermute | solution.py:147
  80.3 2.1 %copy-start.8 = (bf16[64,384]{1,0:T(8,128)(2,1)}, bf16[64,384]{1,0:T(8,128)(2,1)S(1)}, u32[]{:S(2)}) copy-start(bf16[64,384]{1,0:T(8,128)(2,1)S(1)} %collective-permute-done.17.p1) | copy-start | bytes 147460
  81.5 0.9 %copy-start.9 = (bf16[64,384]{1,0:T(8,128)(2,1)}, bf16[64,384]{1,0:T(8,128)(2,1)S(1)}, u32[]{:S(2)}) copy-start(bf16[64,384]{1,0:T(8,128)(2,1)S(1)} %collective-permute-done.18.p2) | copy-start | bytes 147460
  82.4 0.6 copy-start.10

commit v6 on v5

--- a/solution.py
+++ b/solution.py
@@ -348,8 +348,7 @@
 
     xnext, xprev = move(own, from_x(1)), move(own, from_x(-1))
     next1, prev1 = move(own, from_chip(1)), move(own, from_chip(-1))
-    sent, z4_raw = barrier((own, z4_raw))
-    partner = move(sent, FROM_PARTNER)
+    own_then, z4_raw = barrier((own, z4_raw))
     z4_packed = unpack(z4_raw)
     z4 = lax.all_to_all(z4_packed, "head", split_axis=0, concat_axis=0, tiled=True)
 
@@ -358,8 +357,10 @@
         return attend(band, q, blocks, state, last)
 
     z = (lax.axis_index("frame") // CS) % ZS
-    next2 = move(jnp.where(z < 2, xnext, own), from_z(2))
-    prev2 = move(jnp.where(z >= ZS - 2, xprev, own), from_z(-2))
+    up, down = jnp.where(z < 2, xnext, own), jnp.where(z >= ZS - 2, xprev, own)
+    next2, prev2 = move(up, from_z(2)), move(down, from_z(-2))
+    sent, *_ = barrier((own_then, next1, prev1, up, down))
+    partner = move(sent, FROM_PARTNER)
     z4x = move(z4, FROM_X_FOR_8)
     sent, sent1, sent2, *_ = barrier((own, next1, prev1, z4))
     x2 = move(sent, from_x(2))

time: 85 us -> 85.2 us (level)
  transfers between devices with their start and end apart: 21 -> 21, of which waited for: 9 -> 8; matrix products, arithmetic and copies ran while one was open for 1% -> 1% of each run, Pallas kernels for 9% -> 9%
where the time goes in v6:
time: 85.2 us; the launch traced here: 84.8 us
  starting transfers between devices  47.8 us (56%)
  waiting for transfers between devices  18.7 us (22%)
  Pallas kernels  14.5 us (17%)
  local copies, waits for them, and re-layouts  2.72 us (3%)
  other arithmetic  0.98 us (1%)
    ppermute x14, starting transfers between devices, move(): return lax.ppermute(block, 'frame', pairs)  33.2 us
    ppermute x14, waiting for transfers between devices, move(): return lax.ppermute(block, 'frame', pairs)  16.6 us
    ppermute x6, starting transfers between devices, over_heads(): lax.ppermute(pieces[s], 'head', y_from(s))  11 us
    pallas_call x4, Pallas kernels, copier(): pl.pallas_call(kernel, out_shape=out_shape, in_specs=[VMEM] * len(arrays)...  7.46 us
    pallas_call x2, Pallas kernels, attend(): pl.pallas_call(functools.partial(attend_kernel, names, kinds, first, last...  7 us
    all_to_all x1, starting transfers between devices, shards(): lax.all_to_all(z4_packed, 'head', split_axis=0, concat_axis=0, tiled=True)  3.59 us
    unnamed x22, local copies, waits for them, and re-layouts  2.72 us
    ppermute x6, waiting for transfers between devices, over_heads(): lax.ppermute(pieces[s], 'head', y_from(s))  2.06 us
  transfers between devices with their start and end apart: 21, of which 8 were waited for; matrix products, arithmetic and copies ran while one was open for 1% of the time, Pallas kernels for 9%

profile of v6, /device:TPU:1, one launch (start us, length us, event | category | flops | bytes accessed | tf_op | source)
XLA Modules:
  0.0 84.8 jit_solution(957436475047154023)
XLA Ops:
  0.0 2.1 %pack.1 = (bf16[64,1152]{1,0:T(8,128)(2,1)}, bf16[64,1152]{1,0:T(8,128)(2,1)}, bf16[64,1152]{1,0:T(8,128)(2,1)}, bf16[64,1152]{1,0:T(8,128)(2,1)}, bf16[64,3072]{1,0:T(8,128)(2,1)}) custom-call(bf16[64,1536]{1,0:T(8,128)(2,1)} %k_ref.1, bf16[64,1536]{1,0:T(8,128)(2,1)} %v_ref.1, bf16[64,1536]{1,0:T(8,128)(2,1)} %q_ref.1), custom_call_target="tpu_custom_call" | custom-call | flops 1 | bytes 1 | tf_op jit(solution)/shard_map/pack/pallas_call | solution.py:63
  2.1 2.1 %collective-permute-start = (bf16[64,1152]{1,0:T(8,128)(2,1)}, bf16[64,1152]{1,0:T(8,128)(2,1)S(1)}, u32[]{:S(2)}, u32[]{:S(2)}) collective-permute-start(bf16[64,1152]{1,0:T(8,128)(2,1)} %get-tuple-element.32), channel_id=1, source_target_pairs={{3,0},{0,1},{1,2},{2,3},{7,4},{4,5},{5,6},{6,7},{11,8},{8,9},{9,10... | collective-permute-start | bytes 442376 | tf_op jit(solution)/shard_map/ppermute | solution.py:147
  4.3 2.6 %collective-permute-start.1 = (bf16[64,1152]{1,0:T(8,128)(2,1)}, bf16[64,1152]{1,0:T(8,128)(2,1)S(1)}, u32[]{:S(2)}, u32[]{:S(2)}) collective-permute-start(bf16[64,1152]{1,0:T(8,128)(2,1)} %get-tuple-element.33), channel_id=1, source_target_pairs={{2,0},{3,1},{0,2},{1,3},{6,4},{7,5},{4,6},{5,7},{10,8},{11,9},{8,1... | collective-permute-start | bytes 442376 | tf_op jit(solution)/shard_map/ppermute | solution.py:147
  6.9 1.1 %collective-permute-start.2 = (bf16[64,1152]{1,0:T(8,128)(2,1)}, bf16[64,1152]{1,0:T(8,128)(2,1)S(1)}, u32[]{:S(2)}, u32[]{:S(2)}) collective-permute-start(bf16[64,1152]{1,0:T(8,128)(2,1)} %get-tuple-element.34), channel_id=1, source_target_pairs={{1,0},{2,1},{3,2},{0,3},{5,4},{6,5},{7,6},{4,7},{9,8},{10,9},{11,1... | collective-permute-start | bytes 442376 | tf_op jit(solution)/shard_map/ppermute | solution.py:147
  7.9 6.9 %collective-permute-start.5 = (bf16[64,3072]{1,0:T(8,128)(2,1)}, bf16[64,3072]{1,0:T(8,128)(2,1)S(1)}, u32[]{:S(2)}, u32[]{:S(2)}) collective-permute-start(bf16[64,3072]{1,0:T(8,128)(2,1)} %get-tuple-element.37), channel_id=1, source_target_pairs={{32,0},{36,4},{40,8},{44,12},{48,16},{52,20},{56,24},{60,28},{0,32... | collective-permute-start | bytes 1179656 | tf_op jit(solution)/shard_map/ppermute | solution.py:54
  14.9 0.6 copy-done.5
  15.6 2.0 %join.1 = (bf16[256,768]{1,0:T(8,128)(2,1)}, bf16[256,384]{1,0:T(8,128)(2,1)}) custom-call(bf16[64,1152]{1,0:T(8,128)(2,1)} %get-tuple-element.31.p0, bf16[64,1152]{1,0:T(8,128)(2,1)} %copy-done.5, bf16[64,1152]{1,0:T(8,128)(2,1)} %copy-done.6, bf16[64,1152]{1,0:T(8,128)(2,1)} %copy-done.7), custom_call_target="tpu_custom_call" | custom-call | flops 1 | bytes 1 | tf_op jit(solution)/shard_map/join/pallas_call | solution.py:63
  17.6 1.2 %collective-permute-start.10 = (bf16[256,768]{1,0:T(8,128)(2,1)}, bf16[256,768]{1,0:T(8,128)(2,1)S(1)}, u32[]{:S(2)}, u32[]{:S(2)}) collective-permute-start(bf16[256,768]{1,0:T(8,128)(2,1)} %get-tuple-element.43.refs_0_), channel_id=1, source_target_pairs={{192,0},{196,4},{200,8},{204,12},{208,16},{212,20},{216,24},{220,2... | collective-permute-start | bytes 1179656 | tf_op jit(solution)/shard_map/ppermute | solution.py:54
  18.8 1.5 %collective-permute-start.8 = (bf16[256,768]{1,0:T(8,128)(2,1)}, bf16[256,768]{1,0:T(8,128)(2,1)S(1)}, u32[]{:S(2)}, u32[]{:S(2)}) collective-permute-start(bf16[256,768]{1,0:T(8,128)(2,1)} %get-tuple-element.43.refs_0_), channel_id=1, source_target_pairs={{64,0},{68,4},{72,8},{76,12},{80,16},{84,20},{88,24},{92,28},{96,3... | collective-permute-start | bytes 1179656 | tf_op jit(solution)/shard_map/ppermute | solution.py:54
  20.3 5.1 %collective-permute-start.3 = (bf16[256,768]{1,0:T(8,128)(2,1)}, bf16[256,768]{1,0:T(8,128)(2,1)S(1)}, u32[]{:S(2)}, u32[]{:S(2)}) collective-permute-start(bf16[256,768]{1,0:T(8,128)(2,1)} %get-tuple-element.43.refs_0_), channel_id=1, source_target_pairs={{8,0},{12,4},{16,8},{20,12},{24,16},{28,20},{32,24},{36,28},{40,32... | collective-permute-start | bytes 1179656 | tf_op jit(solution)/shard_map/ppermute | solution.py:54
  25.4 0.8 copy-done.4
  26.2 1.8 %unpack.1 = bf16[256,768]{1,0:T(8,128)(2,1)} custom-call(bf16[64,3072]{1,0:T(8,128)(2,1)} %copy-done.4), custom_call_target="tpu_custom_call" | custom-call | flops 1 | bytes 1 | tf_op jit(solution)/shard_map/unpack/pallas_call | solution.py:63
  28.0 3.6 %all-to-all-start = ((bf16[4,64,768]{2,1,0:T(8,128)(2,1)}), bf16[4,64,768]{2,1,0:T(8,128)(2,1)S(1)}, u32[]{:S(2)}, u32[]{:S(2)}) async-start(bf16[4,64,768]{2,1,0:T(8,128)(2,1)} %bitcast.4), calls=%async_computation | async-start | bytes 786432 | tf_op jit(solution)/shard_map/all_to_all | solution.py:353
  31.6 1.0 %broadcast_select_fusion = (bf16[256,768]{1,0:T(8,128)(2,1)}, bf16[256,768]{1,0:T(8,128)(2,1)}) fusion(bf16[256,768]{1,0:T(8,128)(2,1)S(1)} %collective-permute-done.10.refs_3_, bf16[256,768]{1,0:T(8,128)(2,1)S(1)} %copy-done, pred[]{:T(512)S(6)} %ge.3, bf16[256,768]{1,0:T(8,128)(2,1)S(1)} %collective-permute-done.8.refs_2_, pred[]{:T(512)S(6)} %lt.10), kind=kLoop, calls=%fused_computation | loop fusion | flops 393216 | bytes 1966082 | tf_op jit(solution)/shard_map/jit(_where)/select_n | solution.py:360
  32.6 8.5 %collective-permute-start.11 = (bf16[256,768]{1,0:T(8,128)(2,1)}, bf16[256,768]{1,0:T(8,128)(2,1)S(1)}, u32[]{:S(2)}, u32[]{:S(2)}) collective-permute-start(bf16[256,768]{1,0:T(8,128)(2,1)} %get-tuple-element.57), channel_id=1, source_target_pairs={{48,0},{52,4},{56,8},{60,12},{0,16},{4,20},{8,24},{12,28},{16,32},... | collective-permute-start | bytes 1179656 | tf_op jit(solution)/shard_map/ppermute | solution.py:54
  41.1 2.6 %collective-permute-start.9 = (bf16[256,768]{1,0:T(8,128)(2,1)}, bf16[256,768]{1,0:T(8,128)(2,1)S(1)}, u32[]{:S(2)}, u32[]{:S(2)}) collective-permute-start(bf16[256,768]{1,0:T(8,128)(2,1)} %get-tuple-element.58), channel_id=1, source_target_pairs={{16,0},{20,4},{24,8},{28,12},{32,16},{36,20},{40,24},{44,28},{48,3... | collective-permute-start | bytes 1179656 | tf_op jit(solution)/shard_map/ppermute | solution.py:54
  43.7 2.9 %collective-permute-start.14 = (bf16[256,768]{1,0:T(8,128)(2,1)S(1)}, bf16[256,768]{1,0:T(8,128)(2,1)}, u32[]{:S(2)}, u32[]{:S(2)}) collective-permute-start(bf16[256,768]{1,0:T(8,128)(2,1)S(1)} %copy-done), channel_id=1, source_target_pairs={{4,0},{0,4},{12,8},{8,12},{20,16},{16,20},{28,24},{24,28},{36,32},... | collective-permute-start | bytes 1179656 | tf_op jit(solution)/shard_map/ppermute | solution.py:54
  46.6 2.5 %collective-permute-start.13 = (bf16[256,768]{1,0:T(8,128)(2,1)S(1)}, bf16[256,768]{1,0:T(8,128)(2,1)S(1)}, u32[]{:S(2)}, u32[]{:S(2)}) collective-permute-start(bf16[256,768]{1,0:T(8,128)(2,1)S(1)} %copy-done), channel_id=1, source_target_pairs={{128,0},{132,4},{136,8},{140,12},{144,16},{148,20},{152,24},{156,2... | collective-permute-start | bytes 1179656 | tf_op jit(solution)/shard_map/ppermute | solution.py:54
  49.7 3.5 %attend7.2 = (f32[256,128]{1,0:T(8,128)S(1)}, f32[256,384]{1,0:T(8,128)S(1)}) custom-call(s32[1,64]{1,0:T(1,128)S(1)} %copy-done.3, bf16[256,384]{1,0:T(8,128)(2,1)S(1)} %copy-done.1, bf16[256,768]{1,0:T(8,128)(2,1)S(1)} %copy-done, bf16[256,768]{1,0:T(8,128)(2,1)} %collective-permute-done.14.refs_1_, bf16[256,768]{1,0:T(8,128)(2,1)S(1)} %collective-permute-done.8.refs_2_, ...), custom_call_target="tpu_custom_call" | custom-call | flops 1 | bytes 1 | tf_op jit(solution)/shard_map/attend7/pallas_call | solution.py:331
  53.2 7.6 %collective-permute-done.11.refs_5_ = bf16[256,768]{1,0:T(8,128)(2,1)S(1)} collective-permute-done((bf16[256,768]{1,0:T(8,128)(2,1)}, bf16[256,768]{1,0:T(8,128)(2,1)S(1)}, u32[]{:S(2)}, u32[]{:S(2)}) %collective-permute-start.11) | collective-permute-done | bytes 393248 | tf_op jit(solution)/shard_map/ppermute | solution.py:54
  60.9 6.8 %collective-permute-done.12.refs_3_ = bf16[256,768]{1,0:T(8,128)(2,1)S(1)} collective-permute-done((bf16[256,768]{1,0:T(8,128)(2,1)S(1)}, bf16[256,768]{1,0:T(8,128)(2,1)S(1)}, u32[]{:S(2)}, u32[]{:S(2)}) %collective-permute-start.12) | collective-permute-done | bytes 393248 | tf_op jit(solution)/shard_map/ppermute | solution.py:54
  68.6 0.8 collective-permute-done.15.refs_7_
  70.6 0.6 collective-permute-done.16.refs_6_
  71.2 3.5 %attend7.3 = (bf16[64,384]{1,0:T(8,128)(2,1)S(1)}, bf16[64,384]{1,0:T(8,128)(2,1)S(1)}, bf16[64,384]{1,0:T(8,128)(2,1)S(1)}, bf16[64,384]{1,0:T(8,128)(2,1)S(1)}) custom-call(s32[1,64]{1,0:T(1,128)S(1)} %copy-done.3, bf16[256,384]{1,0:T(8,128)(2,1)S(1)} %copy-done.1, bf16[256,768]{1,0:T(8,128)(2,1)S(1)} %collective-permute-done.6.refs_0_, ...), custom_call_target="tpu_custom_call" | custom-call | flops 1 | bytes 1 | tf_op jit(solution)/shard_map/attend7/pallas_call | solution.py:331
  74.7 0.6 copy-done.2
  75.3 1.7 %collective-permute-start.17 = (bf16[64,384]{1,0:T(8,128)(2,1)S(1)}, bf16[64,384]{1,0:T(8,128)(2,1)S(1)}, u32[]{:S(2)}, u32[]{:S(2)}) collective-permute-start(bf16[64,384]{1,0:T(8,128)(2,1)S(1)} %get-tuple-element.54), channel_id=1, source_target_pairs={{3,0},{0,1},{1,2},{2,3},{7,4},{4,5},{5,6},{6,7},{11,8},{8,9},{9,10... | collective-permute-start | bytes 147464 | tf_op jit(solution)/shard_map/ppermute | solution.py:147
  77.0 2.4 %collective-permute-start.18 = (bf16[64,384]{1,0:T(8,128)(2,1)S(1)}, bf16[64,384]{1,0:T(8,128)(2,1)S(1)}, u32[]{:S(2)}, u32[]{:S(2)}) collective-permute-start(bf16[64,384]{1,0:T(8,128)(2,1)S(1)} %get-tuple-element.55), channel_id=1, source_target_pairs={{2,0},{3,1},{0,2},{1,3},{6,4},{7,5},{4,6},{5,7},{10,8},{11,9},{8,1... | collective-permute-start | bytes 147464 | tf_op jit(solution)/shard_map/ppermute | solution.py:147
  79.4 1.2 %collective-permute-start.19 = (bf16[64,384]{1,0:T(8,128)(2,1)S(1)}, bf16[64,384]{1,0:T(8,128)(2,1)S(1)}, u32[]{:S(2)}, u32[]{:S(2)}) collective-permute-start(bf16[64,384]{1,0:T(8,128)(2,1)S(1)} %get-tuple-element.56), channel_id=1, source_target_pairs={{1,0},{2,1},{3,2},{0,3},{5,4},{6,5},{7,6},{4,7},{9,8},{10,9},{11,1... | collective-permute-start | bytes 147464 | tf_op jit(solution)/shard_map/ppermute | solution.py:147
  80.6 1.1 %collective-permute-done.18.p2 = bf16[64,384]{1,0:T(8,128)(2,1)S(1)} collective-permute-done((bf16[64,384]{1,0:T(8,128)(2,1)S(1)}, bf16[64,384]{1,0:T(8,128)(2,1)S(1)}, u32[]{:S(2)}, u32[]{:S(2)}) %collective-permute-start.18) | collective-permute-done | bytes 49184 | tf_op jit(solution)/shard_map/ppermute | solution.py:147
  81.7 0.9 %collective-permute-done.19.p3 = bf16[64,384]{1,0:T(8,128)(2,1)S(1)} collective-permute-done((bf16[64,384]{1,0:T(8,128)(2,1)S(1)}, bf16[64,384]{1,0:T(8,128)(2,1)S(1)}, u32[]{:S(2)}, u32[]{:S(2)}) %collective-permute-start.19) | collective-permute-done | bytes 49184 | tf_op jit(solution)/shard_map/ppermute | solution.py:147
  82.6 0.6 copy-done.10
  83.2 1.6 %place.1 = bf16[64,1536]{1,0:T(8,128)(2,1)} custom-call(bf16[64,384]{1,0:T(8,128)(2,1)} %copy-done.2, bf16[64,384]{1,0:T(8,128)(2,1)} %copy-done.8, bf16[64,384]{1,0:T(8,128)(2,1)} %copy-done.9, bf16[64,384]{1,0:T(8,128)(2,1)} %copy-done.10), custom_call_target="tpu_custom_call" | custom-call | flops 1 | bytes 1 | tf_op jit(solution)/shard_map/place/pallas_call | solution.py:63
  (39 shorter events, 2.9 us)
Async XLA Ops:
  2.1 12.7 %collective-permute-start = (bf16[64,1152]{1,0:T(8,128)(2,1)}, bf16[64,1152]{1,0:T(8,128)(2,1)S(1)}, u32[]{:S(2)}, u32[]{:S(2)}) collective-permute-start(bf16[64,1152]{1,0:T(8,128)(2,1)} %get-tuple-element.32), channel_id=1, source_target_pairs={{3,0},{0,1},{1,2},{2,3},{7,4},{4,5},{5,6},{6,7},{11,8},{8,9},{9,10... | collective-permute-start | bytes 442376 | tf_op jit(solution)/shard_map/ppermute | solution.py:147
  4.3 10.6 %collective-permute-start.1 = (bf16[64,1152]{1,0:T(8,128)(2,1)}, bf16[64,1152]{1,0:T(8,128)(2,1)S(1)}, u32[]{:S(2)}, u32[]{:S(2)}) collective-permute-start(bf16[64,1152]{1,0:T(8,128)(2,1)} %get-tuple-element.33), channel_id=1, source_target_pairs={{2,0},{3,1},{0,2},{1,3},{6,4},{7,5},{4,6},{5,7},{10,8},{11,9},{8,1... | collective-permute-start | bytes 442376 | tf_op jit(solution)/shard_map/ppermute | solution.py:147
  6.9 8.0 %collective-permute-start.2 = (bf16[64,1152]{1,0:T(8,128)(2,1)}, bf16[64,1152]{1,0:T(8,128)(2,1)S(1)}, u32[]{:S(2)}, u32[]{:S(2)}) collective-permute-start(bf16[64,1152]{1,0:T(8,128)(2,1)} %get-tuple-element.34), channel_id=1, source_target_pairs={{1,0},{2,1},{3,2},{0,3},{5,4},{6,5},{7,6},{4,7},{9,8},{10,9},{11,1... | collective-permute-start | bytes 442376 | tf_op jit(solution)/shard_map/ppermute | solution.py:147
  7.9 17.5 %collective-permute-start.5 = (bf16[64,3072]{1,0:T(8,128)(2,1)}, bf16[64,3072]{1,0:T(8,128)(2,1)S(1)}, u32[]{:S(2)}, u32[]{:S(2)}) collective-permute-start(bf16[64,3072]{1,0:T(8,128)(2,1)} %get-tuple-element.37), channel_id=1, source_target_pairs={{32,0},{36,4},{40,8},{44,12},{48,16},{52,20},{56,24},{60,28},{0,32... | collective-permute-start | bytes 1179656 | tf_op jit(solution)/shard_map/ppermute | solution.py:54
  14.9 0.7 copy-start.5
  14.9 0.7 copy-start.6
  14.9 0.7 copy-start.7
  17.6 14.0 %collective-permute-start.10 = (bf16[256,768]{1,0:T(8,128)(2,1)}, bf16[256,768]{1,0:T(8,128)(2,1)S(1)}, u32[]{:S(2)}, u32[]{:S(2)}) collective-permute-start(bf16[256,768]{1,0:T(8,128)(2,1)} %get-tuple-element.43.refs_0_), channel_id=1, source_target_pairs={{192,0},{196,4},{200,8},{204,12},{208,16},{212,20},{216,24},{220,2... | collective-permute-start | bytes 1179656 | tf_op jit(solution)/shard_map/ppermute | solution.py:54
  18.8 12.8 %collective-permute-start.8 = (bf16[256,768]{1,0:T(8,128)(2,1)}, bf16[256,768]{1,0:T(8,128)(2,1)S(1)}, u32[]{:S(2)}, u32[]{:S(2)}) collective-permute-start(bf16[256,768]{1,0:T(8,128)(2,1)} %get-tuple-element.43.refs_0_), channel_id=1, source_target_pairs={{64,0},{68,4},{72,8},{76,12},{80,16},{84,20},{88,24},{92,28},{96,3... | collective-permute-start | bytes 1179656 | tf_op jit(solution)/shard_map/ppermute | solution.py:54
  20.3 23.4 %collective-permute-start.3 = (bf16[256,768]{1,0:T(8,128)(2,1)}, bf16[256,768]{1,0:T(8,128)(2,1)S(1)}, u32[]{:S(2)}, u32[]{:S(2)}) collective-permute-start(bf16[256,768]{1,0:T(8,128)(2,1)} %get-tuple-element.43.refs_0_), channel_id=1, source_target_pairs={{8,0},{12,4},{16,8},{20,12},{24,16},{28,20},{32,24},{36,28},{40,32... | collective-permute-start | bytes 1179656 | tf_op jit(solution)/shard_map/ppermute | solution.py:54
  25.4 18.3 %collective-permute-start.4 = (bf16[256,768]{1,0:T(8,128)(2,1)}, bf16[256,768]{1,0:T(8,128)(2,1)S(1)}, u32[]{:S(2)}, u32[]{:S(2)}) collective-permute-start(bf16[256,768]{1,0:T(8,128)(2,1)} %get-tuple-element.43.refs_0_), channel_id=1, source_target_pairs={{248,0},{252,4},{0,8},{4,12},{8,16},{12,20},{16,24},{20,28},{24,32... | collective-permute-start | bytes 1179656 | tf_op jit(solution)/shard_map/ppermute | solution.py:54
  25.4 0.8 copy-start.4
  28.0 3.7 %copy-start = (bf16[256,768]{1,0:T(8,128)(2,1)S(1)}, bf16[256,768]{1,0:T(8,128)(2,1)}, u32[]{:S(2)}) copy-start(bf16[256,768]{1,0:T(8,128)(2,1)} %get-tuple-element.43.refs_0_) | copy-start | bytes 1179652
  28.0 18.6 %all-to-all-start = ((bf16[4,64,768]{2,1,0:T(8,128)(2,1)}), bf16[4,64,768]{2,1,0:T(8,128)(2,1)S(1)}, u32[]{:S(2)}, u32[]{:S(2)}) async-start(bf16[4,64,768]{2,1,0:T(8,128)(2,1)} %bitcast.4), calls=%async_computation | async-start | bytes 786432 | tf_op jit(solution)/shard_map/all_to_all | solution.py:353
  31.6 18.1 %copy-start.1 = (bf16[256,384]{1,0:T(8,128)(2,1)S(1)}, bf16[256,384]{1,0:T(8,128)(2,1)}, u32[]{:S(2)}) copy-start(bf16[256,384]{1,0:T(8,128)(2,1)} %get-tuple-element.35.q_ref) | copy-start | bytes 589828
  32.6 28.2 %collective-permute-start.11 = (bf16[256,768]{1,0:T(8,128)(2,1)}, bf16[256,768]{1,0:T(8,128)(2,1)S(1)}, u32[]{:S(2)}, u32[]{:S(2)}) collective-permute-start(bf16[256,768]{1,0:T(8,128)(2,1)} %get-tuple-element.57), channel_id=1, source_target_pairs={{48,0},{52,4},{56,8},{60,12},{0,16},{4,20},{8,24},{12,28},{16,32},... | collective-permute-start | bytes 1179656 | tf_op jit(solution)/shard_map/ppermute | solution.py:54
  41.1 19.8 %collective-permute-start.9 = (bf16[256,768]{1,0:T(8,128)(2,1)}, bf16[256,768]{1,0:T(8,128)(2,1)S(1)}, u32[]{:S(2)}, u32[]{:S(2)}) collective-permute-start(bf16[256,768]{1,0:T(8,128)(2,1)} %get-tuple-element.58), channel_id=1, source_target_pairs={{16,0},{20,4},{24,8},{28,12},{32,16},{36,20},{40,24},{44,28},{48,3... | collective-permute-start | bytes 1179656 | tf_op jit(solution)/shard_map/ppermute | solution.py:54
  43.7 6.0 %collective-permute-start.14 = (bf16[256,768]{1,0:T(8,128)(2,1)S(1)}, bf16[256,768]{1,0:T(8,128)(2,1)}, u32[]{:S(2)}, u32[]{:S(2)}) collective-permute-start(bf16[256,768]{1,0:T(8,128)(2,1)S(1)} %copy-done), channel_id=1, source_target_pairs={{4,0},{0,4},{12,8},{8,12},{20,16},{16,20},{28,24},{24,28},{36,32},... | collective-permute-start | bytes 1179656 | tf_op jit(solution)/shard_map/ppermute | solution.py:54
  46.6 3.1 %copy-start.3 = (s32[1,64]{1,0:T(1,128)S(1)}, s32[1,64]{1,0:T(1,128)}, u32[]{:S(2)}) copy-start(s32[1,64]{1,0:T(1,128)} %band_ref.3) | copy-start | bytes 772
  46.6 14.2 %collective-permute-start.13 = (bf16[256,768]{1,0:T(8,128)(2,1)S(1)}, bf16[256,768]{1,0:T(8,128)(2,1)S(1)}, u32[]{:S(2)}, u32[]{:S(2)}) collective-permute-start(bf16[256,768]{1,0:T(8,128)(2,1)S(1)} %copy-done), channel_id=1, source_target_pairs={{128,0},{132,4},{136,8},{140,12},{144,16},{148,20},{152,24},{156,2... | collective-permute-start | bytes 1179656 | tf_op jit(solution)/shard_map/ppermute | solution.py:54
  49.1 18.5 %collective-permute-start.12 = (bf16[256,768]{1,0:T(8,128)(2,1)S(1)}, bf16[256,768]{1,0:T(8,128)(2,1)S(1)}, u32[]{:S(2)}, u32[]{:S(2)}) collective-permute-start(bf16[256,768]{1,0:T(8,128)(2,1)S(1)} %bitcast.2), channel_id=1, source_target_pairs={{192,0},{196,4},{200,8},{204,12},{208,16},{212,20},{216,24},{220,2... | collective-permute-start | bytes 1179656 | tf_op jit(solution)/shard_map/ppermute | solution.py:54
  67.6 1.8 %collective-permute-start.15 = (bf16[256,768]{1,0:T(8,128)(2,1)S(1)}, bf16[256,768]{1,0:T(8,128)(2,1)S(1)}, u32[]{:S(2)}, u32[]{:S(2)}) collective-permute-start(bf16[256,768]{1,0:T(8,128)(2,1)S(1)} %collective-permute-done.9.refs_4_), channel_id=1, source_target_pairs={{4,0},{0,4},{12,8},{8,12},{20,16},{16,20},{28,24},{24,28},{36,32},... | collective-permute-start | bytes 1179656 | tf_op jit(solution)/shard_map/ppermute | solution.py:54
  68.1 1.9 %collective-permute-start.6 = (bf16[256,768]{1,0:T(8,128)(2,1)S(1)}, bf16[256,768]{1,0:T(8,128)(2,1)S(1)}, u32[]{:S(2)}, u32[]{:S(2)}) collective-permute-start(bf16[256,768]{1,0:T(8,128)(2,1)S(1)} %collective-permute-done.3.refs_5_), channel_id=1, source_target_pairs={{4,0},{0,4},{12,8},{8,12},{20,16},{16,20},{28,24},{24,28},{36,32},... | collective-permute-start | bytes 1179656 | tf_op jit(solution)/shard_map/ppermute | solution.py:54
  68.1 2.5 %collective-permute-start.7 = (bf16[256,768]{1,0:T(8,128)(2,1)S(1)}, bf16[256,768]{1,0:T(8,128)(2,1)S(1)}, u32[]{:S(2)}, u32[]{:S(2)}) collective-permute-start(bf16[256,768]{1,0:T(8,128)(2,1)S(1)} %collective-permute-done.4.refs_6_), channel_id=1, source_target_pairs={{4,0},{0,4},{12,8},{8,12},{20,16},{16,20},{28,24},{24,28},{36,32},... | collective-permute-start | bytes 1179656 | tf_op jit(solution)/shard_map/ppermute | solution.py:54
  69.5 1.7 %collective-permute-start.16 = (bf16[256,768]{1,0:T(8,128)(2,1)S(1)}, bf16[256,768]{1,0:T(8,128)(2,1)S(1)}, u32[]{:S(2)}, u32[]{:S(2)}) collective-permute-start(bf16[256,768]{1,0:T(8,128)(2,1)S(1)} %collective-permute-done.11.refs_5_), channel_id=1, source_target_pairs={{4,0},{0,4},{12,8},{8,12},{20,16},{16,20},{28,24},{24,28},{36,32},... | collective-permute-start | bytes 1179656 | tf_op jit(solution)/shard_map/ppermute | solution.py:54
  74.7 0.6 copy-start.2
  75.3 5.2 %collective-permute-start.17 = (bf16[64,384]{1,0:T(8,128)(2,1)S(1)}, bf16[64,384]{1,0:T(8,128)(2,1)S(1)}, u32[]{:S(2)}, u32[]{:S(2)}) collective-permute-start(bf16[64,384]{1,0:T(8,128)(2,1)S(1)} %get-tuple-element.54), channel_id=1, source_target_pairs={{3,0},{0,1},{1,2},{2,3},{7,4},{4,5},{5,6},{6,7},{11,8},{8,9},{9,10... | collective-permute-start | bytes 147464 | tf_op jit(solution)/shard_map/ppermute | solution.py:147
  77.0 4.7 %collective-permute-start.18 = (bf16[64,384]{1,0:T(8,128)(2,1)S(1)}, bf16[64,384]{1,0:T(8,128)(2,1)S(1)}, u32[]{:S(2)}, u32[]{:S(2)}) collective-permute-start(bf16[64,384]{1,0:T(8,128)(2,1)S(1)} %get-tuple-element.55), channel_id=1, source_target_pairs={{2,0},{3,1},{0,2},{1,3},{6,4},{7,5},{4,6},{5,7},{10,8},{11,9},{8,1... | collective-permute-start | bytes 147464 | tf_op jit(solution)/shard_map/ppermute | solution.py:147
  79.4 3.2 %collective-permute-start.19 = (bf16[64,384]{1,0:T(8,128)(2,1)S(1)}, bf16[64,384]{1,0:T(8,128)(2,1)S(1)}, u32[]{:S(2)}, u32[]{:S(2)}) collective-permute-start(bf16[64,384]{1,0:T(8,128)(2,1)S(1)} %get-tuple-element.56), channel_id=1, source_target_pairs={{1,0},{2,1},{3,2},{0,3},{5,4},{6,5},{7,6},{4,7},{9,8},{10,9},{11,1... | collective-permute-start | bytes 147464 | tf_op jit(solution)/shard_map/ppermute | solution.py:147
  80.6 2.1 %copy-start.8 = (bf16[64,384]{1,0:T(8,128)(2,1)}, bf16[64,384]{1,0:T(8,128)(2,1)S(1)}, u32[]{:S(2)}) copy-start(bf16[64,384]{1,0:T(8,128)(2,1)S(1)} %collective-permute-done.17.p1) | copy-start | bytes 147460
  81.7 0.9 %copy-start.9 = (bf16[64,384]{1,0:T(8,128)(2,1)}, bf16[64,384]{1,0:T(8,128)(2,1)S(1)}, u32[]{:S(2)}) copy-start(bf16[64,384]{1,0:T(8,128)(2,1)S(1)} %collective-permute-done.18.p2) | copy-start | bytes 147460
  82.6 0.6 copy-start.10

commit v7 on v4

--- a/solution.py
+++ b/solution.py
@@ -361,7 +361,7 @@
     next2 = move(jnp.where(z < 2, xnext, own), from_z(2))
     prev2 = move(jnp.where(z >= ZS - 2, xprev, own), from_z(-2))
     z4x = move(z4, FROM_X_FOR_8)
-    sent, sent1, sent2, *_ = barrier((own, next1, prev1, z4))
+    sent, sent1, sent2, *_ = barrier((own, next1, prev1, z4_packed))
     x2 = move(sent, from_x(2))
     next1p, prev1p = move(sent1, FROM_PARTNER), move(sent2, FROM_PARTNER)
     state = step(None, own=own, xnext=xnext, xprev=xprev, z4=z4, next1=next1, prev1=prev1)

time: 82.9 us -> 83.6 us (level)
  local copies, waits for them, and re-layouts: 2.73 us -> 4.67 us
  waiting for transfers between devices: 19.7 us -> 18.6 us
    unnamed x22 -> x28, local copies, waits for them, and re-layouts: 2.73 us -> 4.67 us
    ppermute x14, waiting for transfers between devices: 17.7 us -> 16.6 us  [move(): return lax.ppermute(block, 'frame', pairs)]
where the time goes in v7:
time: 83.6 us; the launch traced here: 83.3 us
  starting transfers between devices  44.7 us (53%)
  waiting for transfers between devices  18.6 us (22%)
  Pallas kernels  14.1 us (17%)
  local copies, waits for them, and re-layouts  4.67 us (6%)
  other arithmetic  0.97 us (1%)
    ppermute x14, starting transfers between devices, move(): return lax.ppermute(block, 'frame', pairs)  30.4 us
    ppermute x14, waiting for transfers between devices, move(): return lax.ppermute(block, 'frame', pairs)  16.6 us
    ppermute x6, starting transfers between devices, over_heads(): lax.ppermute(pieces[s], 'head', y_from(s))  10.8 us
    pallas_call x4, Pallas kernels, copier(): pl.pallas_call(kernel, out_shape=out_shape, in_specs=[VMEM] * len(arrays)...  7.47 us
    pallas_call x2, Pallas kernels, attend(): pl.pallas_call(functools.partial(attend_kernel, names, kinds, first, last...  6.66 us
    unnamed x28, local copies, waits for them, and re-layouts  4.67 us
    all_to_all x1, starting transfers between devices, shards(): lax.all_to_all(z4_packed, 'head', split_axis=0, concat_axis=0, tiled=True)  3.59 us
    ppermute x6, waiting for transfers between devices, over_heads(): lax.ppermute(pieces[s], 'head', y_from(s))  2.06 us
  transfers between devices with their start and end apart: 21, of which 10 were waited for; matrix products, arithmetic and copies ran while one was open for 1% of the time, Pallas kernels for 8%

profile of v7, /device:TPU:1, one launch (start us, length us, event | category | flops | bytes accessed | tf_op | source)
XLA Modules:
  0.0 83.3 jit_solution(13255470383581606299)
XLA Ops:
  0.0 2.1 %pack.1 = (bf16[64,1152]{1,0:T(8,128)(2,1)}, bf16[64,1152]{1,0:T(8,128)(2,1)}, bf16[64,1152]{1,0:T(8,128)(2,1)}, bf16[64,1152]{1,0:T(8,128)(2,1)}, bf16[64,3072]{1,0:T(8,128)(2,1)}) custom-call(bf16[64,1536]{1,0:T(8,128)(2,1)} %k_ref.1, bf16[64,1536]{1,0:T(8,128)(2,1)} %v_ref.1, bf16[64,1536]{1,0:T(8,128)(2,1)} %q_ref.1), custom_call_target="tpu_custom_call" | custom-call | flops 1 | bytes 1 | tf_op jit(solution)/shard_map/pack/pallas_call | solution.py:63
  2.1 2.1 %collective-permute-start = (bf16[64,1152]{1,0:T(8,128)(2,1)}, bf16[64,1152]{1,0:T(8,128)(2,1)S(1)}, u32[]{:S(2)}, u32[]{:S(2)}) collective-permute-start(bf16[64,1152]{1,0:T(8,128)(2,1)} %get-tuple-element.31), channel_id=1, source_target_pairs={{3,0},{0,1},{1,2},{2,3},{7,4},{4,5},{5,6},{6,7},{11,8},{8,9},{9,10... | collective-permute-start | bytes 442376 | tf_op jit(solution)/shard_map/ppermute | solution.py:147
  4.3 2.6 %collective-permute-start.1 = (bf16[64,1152]{1,0:T(8,128)(2,1)}, bf16[64,1152]{1,0:T(8,128)(2,1)S(1)}, u32[]{:S(2)}, u32[]{:S(2)}) collective-permute-start(bf16[64,1152]{1,0:T(8,128)(2,1)} %get-tuple-element.32), channel_id=1, source_target_pairs={{2,0},{3,1},{0,2},{1,3},{6,4},{7,5},{4,6},{5,7},{10,8},{11,9},{8,1... | collective-permute-start | bytes 442376 | tf_op jit(solution)/shard_map/ppermute | solution.py:147
  6.9 1.1 %collective-permute-start.2 = (bf16[64,1152]{1,0:T(8,128)(2,1)}, bf16[64,1152]{1,0:T(8,128)(2,1)S(1)}, u32[]{:S(2)}, u32[]{:S(2)}) collective-permute-start(bf16[64,1152]{1,0:T(8,128)(2,1)} %get-tuple-element.33), channel_id=1, source_target_pairs={{1,0},{2,1},{3,2},{0,3},{5,4},{6,5},{7,6},{4,7},{9,8},{10,9},{11,1... | collective-permute-start | bytes 442376 | tf_op jit(solution)/shard_map/ppermute | solution.py:147
  8.0 6.9 %collective-permute-start.3 = (bf16[64,3072]{1,0:T(8,128)(2,1)}, bf16[64,3072]{1,0:T(8,128)(2,1)S(1)}, u32[]{:S(2)}, u32[]{:S(2)}) collective-permute-start(bf16[64,3072]{1,0:T(8,128)(2,1)} %get-tuple-element.36), channel_id=1, source_target_pairs={{32,0},{36,4},{40,8},{44,12},{48,16},{52,20},{56,24},{60,28},{0,32... | collective-permute-start | bytes 1179656 | tf_op jit(solution)/shard_map/ppermute | solution.py:54
  14.9 0.6 copy-done.8
  15.6 2.0 %join.1 = (bf16[256,768]{1,0:T(8,128)(2,1)}, bf16[256,384]{1,0:T(8,128)(2,1)}) custom-call(bf16[64,1152]{1,0:T(8,128)(2,1)} %get-tuple-element.30.p0, bf16[64,1152]{1,0:T(8,128)(2,1)} %copy-done.8, bf16[64,1152]{1,0:T(8,128)(2,1)} %copy-done.9, bf16[64,1152]{1,0:T(8,128)(2,1)} %copy-done.10), custom_call_target="tpu_custom_call" | custom-call | flops 1 | bytes 1 | tf_op jit(solution)/shard_map/join/pallas_call | solution.py:63
  17.6 1.2 %collective-permute-start.11 = (bf16[256,768]{1,0:T(8,128)(2,1)}, bf16[256,768]{1,0:T(8,128)(2,1)S(1)}, u32[]{:S(2)}, u32[]{:S(2)}) collective-permute-start(bf16[256,768]{1,0:T(8,128)(2,1)} %get-tuple-element.41.refs_0_), channel_id=1, source_target_pairs={{192,0},{196,4},{200,8},{204,12},{208,16},{212,20},{216,24},{220,2... | collective-permute-start | bytes 1179656 | tf_op jit(solution)/shard_map/ppermute | solution.py:54
  18.8 1.5 %collective-permute-start.9 = (bf16[256,768]{1,0:T(8,128)(2,1)}, bf16[256,768]{1,0:T(8,128)(2,1)S(1)}, u32[]{:S(2)}, u32[]{:S(2)}) collective-permute-start(bf16[256,768]{1,0:T(8,128)(2,1)} %get-tuple-element.41.refs_0_), channel_id=1, source_target_pairs={{64,0},{68,4},{72,8},{76,12},{80,16},{84,20},{88,24},{92,28},{96,3... | collective-permute-start | bytes 1179656 | tf_op jit(solution)/shard_map/ppermute | solution.py:54
  20.3 5.2 %collective-permute-start.5 = (bf16[256,768]{1,0:T(8,128)(2,1)}, bf16[256,768]{1,0:T(8,128)(2,1)S(1)}, u32[]{:S(2)}, u32[]{:S(2)}) collective-permute-start(bf16[256,768]{1,0:T(8,128)(2,1)} %get-tuple-element.41.refs_0_), channel_id=1, source_target_pairs={{8,0},{12,4},{16,8},{20,12},{24,16},{28,20},{32,24},{36,28},{40,32... | collective-permute-start | bytes 1179656 | tf_op jit(solution)/shard_map/ppermute | solution.py:54
  25.5 0.8 copy-done.7
  26.2 1.8 %unpack.1 = bf16[256,768]{1,0:T(8,128)(2,1)} custom-call(bf16[64,3072]{1,0:T(8,128)(2,1)} %copy-done.7), custom_call_target="tpu_custom_call" | custom-call | flops 1 | bytes 1 | tf_op jit(solution)/shard_map/unpack/pallas_call | solution.py:63
  28.0 3.6 %all-to-all-start = ((bf16[4,64,768]{2,1,0:T(8,128)(2,1)}), bf16[4,64,768]{2,1,0:T(8,128)(2,1)S(1)}, u32[]{:S(2)}, u32[]{:S(2)}) async-start(bf16[4,64,768]{2,1,0:T(8,128)(2,1)} %bitcast.4), calls=%async_computation | async-start | bytes 786432 | tf_op jit(solution)/shard_map/all_to_all | solution.py:354
  31.7 1.0 %broadcast_select_fusion = (bf16[256,768]{1,0:T(8,128)(2,1)}, bf16[256,768]{1,0:T(8,128)(2,1)}) fusion(bf16[256,768]{1,0:T(8,128)(2,1)S(1)} %collective-permute-done.11.refs_2_, bf16[256,768]{1,0:T(8,128)(2,1)S(1)} %copy-done, pred[]{:T(512)S(6)} %ge.3, bf16[256,768]{1,0:T(8,128)(2,1)S(1)} %collective-permute-done.9.refs_1_, pred[]{:T(512)S(6)} %lt.10), kind=kLoop, calls=%fused_computation | loop fusion | flops 393216 | bytes 1966082 | tf_op jit(solution)/shard_map/jit(_where)/select_n | solution.py:362
  32.6 11.0 %collective-permute-start.10 = (bf16[256,768]{1,0:T(8,128)(2,1)}, bf16[256,768]{1,0:T(8,128)(2,1)S(1)}, u32[]{:S(2)}, u32[]{:S(2)}) collective-permute-start(bf16[256,768]{1,0:T(8,128)(2,1)} %get-tuple-element.56), channel_id=1, source_target_pairs={{16,0},{20,4},{24,8},{28,12},{32,16},{36,20},{40,24},{44,28},{48,3... | collective-permute-start | bytes 1179656 | tf_op jit(solution)/shard_map/ppermute | solution.py:54
  43.7 0.8 copy-done.2
  44.4 2.3 %collective-permute-start.14 = (bf16[256,768]{1,0:T(8,128)(2,1)S(1)}, bf16[256,768]{1,0:T(8,128)(2,1)S(1)}, u32[]{:S(2)}, u32[]{:S(2)}) collective-permute-start(bf16[256,768]{1,0:T(8,128)(2,1)S(1)} %copy-done), channel_id=1, source_target_pairs={{128,0},{132,4},{136,8},{140,12},{144,16},{148,20},{152,24},{156,2... | collective-permute-start | bytes 1179656 | tf_op jit(solution)/shard_map/ppermute | solution.py:54
  47.4 1.0 %copy-done.3 = bf16[256,768]{1,0:T(8,128)(2,1)S(1)} copy-done((bf16[256,768]{1,0:T(8,128)(2,1)S(1)}, bf16[256,768]{1,0:T(8,128)(2,1)}, u32[]{:S(2)}) %copy-start.3) | copy-done | bytes 393240
  48.4 2.7 %attend6.1 = (f32[256,128]{1,0:T(8,128)S(1)}, f32[256,384]{1,0:T(8,128)S(1)}) custom-call(s32[1,64]{1,0:T(1,128)S(1)} %copy-done.6, bf16[256,384]{1,0:T(8,128)(2,1)S(1)} %copy-done.1, bf16[256,768]{1,0:T(8,128)(2,1)S(1)} %copy-done, bf16[256,768]{1,0:T(8,128)(2,1)S(1)} %collective-permute-done.9.refs_1_, ...), custom_call_target="tpu_custom_call" | custom-call | flops 1 | bytes 1 | tf_op jit(solution)/shard_map/attend6/pallas_call | solution.py:331
  51.1 8.0 %collective-permute-done.10.refs_5_ = bf16[256,768]{1,0:T(8,128)(2,1)S(1)} collective-permute-done((bf16[256,768]{1,0:T(8,128)(2,1)}, bf16[256,768]{1,0:T(8,128)(2,1)S(1)}, u32[]{:S(2)}, u32[]{:S(2)}) %collective-permute-start.10) | collective-permute-done | bytes 393248 | tf_op jit(solution)/shard_map/ppermute | solution.py:54
  59.1 1.1 %collective-permute-done.12.refs_6_ = bf16[256,768]{1,0:T(8,128)(2,1)S(1)} collective-permute-done((bf16[256,768]{1,0:T(8,128)(2,1)}, bf16[256,768]{1,0:T(8,128)(2,1)S(1)}, u32[]{:S(2)}, u32[]{:S(2)}) %collective-permute-start.12) | collective-permute-done | bytes 393248 | tf_op jit(solution)/shard_map/ppermute | solution.py:54
  60.2 4.8 %collective-permute-done.13.refs_4_ = bf16[256,768]{1,0:T(8,128)(2,1)S(1)} collective-permute-done((bf16[256,768]{1,0:T(8,128)(2,1)S(1)}, bf16[256,768]{1,0:T(8,128)(2,1)S(1)}, u32[]{:S(2)}, u32[]{:S(2)}) %collective-permute-start.13) | collective-permute-done | bytes 393248 | tf_op jit(solution)/shard_map/ppermute | solution.py:54
  64.9 1.0 %collective-permute-start.15 = (bf16[256,768]{1,0:T(8,128)(2,1)S(1)}, bf16[256,768]{1,0:T(8,128)(2,1)S(1)}, u32[]{:S(2)}, u32[]{:S(2)}) collective-permute-start(bf16[256,768]{1,0:T(8,128)(2,1)S(1)} %collective-permute-done.10.refs_5_), channel_id=1, source_target_pairs={{4,0},{0,4},{12,8},{8,12},{20,16},{16,20},{28,24},{24,28},{36,32},... | collective-permute-start | bytes 1179656 | tf_op jit(solution)/shard_map/ppermute | solution.py:54
  66.4 0.8 collective-permute-done.15.refs_8_
  69.5 4.0 %attend8.1 = (bf16[64,384]{1,0:T(8,128)(2,1)S(1)}, bf16[64,384]{1,0:T(8,128)(2,1)S(1)}, bf16[64,384]{1,0:T(8,128)(2,1)S(1)}, bf16[64,384]{1,0:T(8,128)(2,1)S(1)}) custom-call(s32[1,64]{1,0:T(1,128)S(1)} %copy-done.6, bf16[256,384]{1,0:T(8,128)(2,1)S(1)} %copy-done.1, bf16[256,768]{1,0:T(8,128)(2,1)S(1)} %collective-permute-done.4.refs_0_, ...), custom_call_target="tpu_custom_call" | custom-call | flops 1 | bytes 1 | tf_op jit(solution)/shard_map/attend8/pallas_call | solution.py:331
  73.5 0.6 copy-done.5
  74.1 1.4 %collective-permute-start.17 = (bf16[64,384]{1,0:T(8,128)(2,1)S(1)}, bf16[64,384]{1,0:T(8,128)(2,1)S(1)}, u32[]{:S(2)}, u32[]{:S(2)}) collective-permute-start(bf16[64,384]{1,0:T(8,128)(2,1)S(1)} %get-tuple-element.52), channel_id=1, source_target_pairs={{3,0},{0,1},{1,2},{2,3},{7,4},{4,5},{5,6},{6,7},{11,8},{8,9},{9,10... | collective-permute-start | bytes 147464 | tf_op jit(solution)/shard_map/ppermute | solution.py:147
  75.5 2.4 %collective-permute-start.18 = (bf16[64,384]{1,0:T(8,128)(2,1)S(1)}, bf16[64,384]{1,0:T(8,128)(2,1)S(1)}, u32[]{:S(2)}, u32[]{:S(2)}) collective-permute-start(bf16[64,384]{1,0:T(8,128)(2,1)S(1)} %get-tuple-element.53), channel_id=1, source_target_pairs={{2,0},{3,1},{0,2},{1,3},{6,4},{7,5},{4,6},{5,7},{10,8},{11,9},{8,1... | collective-permute-start | bytes 147464 | tf_op jit(solution)/shard_map/ppermute | solution.py:147
  77.9 1.2 %collective-permute-start.19 = (bf16[64,384]{1,0:T(8,128)(2,1)S(1)}, bf16[64,384]{1,0:T(8,128)(2,1)S(1)}, u32[]{:S(2)}, u32[]{:S(2)}) collective-permute-start(bf16[64,384]{1,0:T(8,128)(2,1)S(1)} %get-tuple-element.54), channel_id=1, source_target_pairs={{1,0},{2,1},{3,2},{0,3},{5,4},{6,5},{7,6},{4,7},{9,8},{10,9},{11,1... | collective-permute-start | bytes 147464 | tf_op jit(solution)/shard_map/ppermute | solution.py:147
  79.0 1.1 %collective-permute-done.18.p2 = bf16[64,384]{1,0:T(8,128)(2,1)S(1)} collective-permute-done((bf16[64,384]{1,0:T(8,128)(2,1)S(1)}, bf16[64,384]{1,0:T(8,128)(2,1)S(1)}, u32[]{:S(2)}, u32[]{:S(2)}) %collective-permute-start.18) | collective-permute-done | bytes 49184 | tf_op jit(solution)/shard_map/ppermute | solution.py:147
  80.2 0.9 %collective-permute-done.19.p3 = bf16[64,384]{1,0:T(8,128)(2,1)S(1)} collective-permute-done((bf16[64,384]{1,0:T(8,128)(2,1)S(1)}, bf16[64,384]{1,0:T(8,128)(2,1)S(1)}, u32[]{:S(2)}, u32[]{:S(2)}) %collective-permute-start.19) | collective-permute-done | bytes 49184 | tf_op jit(solution)/shard_map/ppermute | solution.py:147
  81.7 1.6 %place.1 = bf16[64,1536]{1,0:T(8,128)(2,1)} custom-call(bf16[64,384]{1,0:T(8,128)(2,1)} %copy-done.5, bf16[64,384]{1,0:T(8,128)(2,1)} %copy-done.11, bf16[64,384]{1,0:T(8,128)(2,1)} %copy-done.12, bf16[64,384]{1,0:T(8,128)(2,1)} %copy-done.13), custom_call_target="tpu_custom_call" | custom-call | flops 1 | bytes 1 | tf_op jit(solution)/shard_map/place/pallas_call | solution.py:63
  (45 shorter events, 4.2 us)
Async XLA Ops:
  2.1 12.7 %collective-permute-start = (bf16[64,1152]{1,0:T(8,128)(2,1)}, bf16[64,1152]{1,0:T(8,128)(2,1)S(1)}, u32[]{:S(2)}, u32[]{:S(2)}) collective-permute-start(bf16[64,1152]{1,0:T(8,128)(2,1)} %get-tuple-element.31), channel_id=1, source_target_pairs={{3,0},{0,1},{1,2},{2,3},{7,4},{4,5},{5,6},{6,7},{11,8},{8,9},{9,10... | collective-permute-start | bytes 442376 | tf_op jit(solution)/shard_map/ppermute | solution.py:147
  4.3 10.6 %collective-permute-start.1 = (bf16[64,1152]{1,0:T(8,128)(2,1)}, bf16[64,1152]{1,0:T(8,128)(2,1)S(1)}, u32[]{:S(2)}, u32[]{:S(2)}) collective-permute-start(bf16[64,1152]{1,0:T(8,128)(2,1)} %get-tuple-element.32), channel_id=1, source_target_pairs={{2,0},{3,1},{0,2},{1,3},{6,4},{7,5},{4,6},{5,7},{10,8},{11,9},{8,1... | collective-permute-start | bytes 442376 | tf_op jit(solution)/shard_map/ppermute | solution.py:147
  6.9 8.0 %collective-permute-start.2 = (bf16[64,1152]{1,0:T(8,128)(2,1)}, bf16[64,1152]{1,0:T(8,128)(2,1)S(1)}, u32[]{:S(2)}, u32[]{:S(2)}) collective-permute-start(bf16[64,1152]{1,0:T(8,128)(2,1)} %get-tuple-element.33), channel_id=1, source_target_pairs={{1,0},{2,1},{3,2},{0,3},{5,4},{6,5},{7,6},{4,7},{9,8},{10,9},{11,1... | collective-permute-start | bytes 442376 | tf_op jit(solution)/shard_map/ppermute | solution.py:147
  8.0 17.5 %collective-permute-start.3 = (bf16[64,3072]{1,0:T(8,128)(2,1)}, bf16[64,3072]{1,0:T(8,128)(2,1)S(1)}, u32[]{:S(2)}, u32[]{:S(2)}) collective-permute-start(bf16[64,3072]{1,0:T(8,128)(2,1)} %get-tuple-element.36), channel_id=1, source_target_pairs={{32,0},{36,4},{40,8},{44,12},{48,16},{52,20},{56,24},{60,28},{0,32... | collective-permute-start | bytes 1179656 | tf_op jit(solution)/shard_map/ppermute | solution.py:54
  14.9 0.7 copy-start.8
  14.9 0.7 copy-start.9
  14.9 0.7 copy-start.10
  17.6 14.0 %collective-permute-start.11 = (bf16[256,768]{1,0:T(8,128)(2,1)}, bf16[256,768]{1,0:T(8,128)(2,1)S(1)}, u32[]{:S(2)}, u32[]{:S(2)}) collective-permute-start(bf16[256,768]{1,0:T(8,128)(2,1)} %get-tuple-element.41.refs_0_), channel_id=1, source_target_pairs={{192,0},{196,4},{200,8},{204,12},{208,16},{212,20},{216,24},{220,2... | collective-permute-start | bytes 1179656 | tf_op jit(solution)/shard_map/ppermute | solution.py:54
  18.8 12.8 %collective-permute-start.9 = (bf16[256,768]{1,0:T(8,128)(2,1)}, bf16[256,768]{1,0:T(8,128)(2,1)S(1)}, u32[]{:S(2)}, u32[]{:S(2)}) collective-permute-start(bf16[256,768]{1,0:T(8,128)(2,1)} %get-tuple-element.41.refs_0_), channel_id=1, source_target_pairs={{64,0},{68,4},{72,8},{76,12},{80,16},{84,20},{88,24},{92,28},{96,3... | collective-permute-start | bytes 1179656 | tf_op jit(solution)/shard_map/ppermute | solution.py:54
  20.3 23.4 %collective-permute-start.5 = (bf16[256,768]{1,0:T(8,128)(2,1)}, bf16[256,768]{1,0:T(8,128)(2,1)S(1)}, u32[]{:S(2)}, u32[]{:S(2)}) collective-permute-start(bf16[256,768]{1,0:T(8,128)(2,1)} %get-tuple-element.41.refs_0_), channel_id=1, source_target_pairs={{8,0},{12,4},{16,8},{20,12},{24,16},{28,20},{32,24},{36,28},{40,32... | collective-permute-start | bytes 1179656 | tf_op jit(solution)/shard_map/ppermute | solution.py:54
  25.4 18.2 %collective-permute-start.6 = (bf16[256,768]{1,0:T(8,128)(2,1)}, bf16[256,768]{1,0:T(8,128)(2,1)S(1)}, u32[]{:S(2)}, u32[]{:S(2)}) collective-permute-start(bf16[256,768]{1,0:T(8,128)(2,1)} %get-tuple-element.41.refs_0_), channel_id=1, source_target_pairs={{248,0},{252,4},{0,8},{4,12},{8,16},{12,20},{16,24},{20,28},{24,32... | collective-permute-start | bytes 1179656 | tf_op jit(solution)/shard_map/ppermute | solution.py:54
  25.5 0.8 copy-start.7
  28.0 3.7 %copy-start = (bf16[256,768]{1,0:T(8,128)(2,1)S(1)}, bf16[256,768]{1,0:T(8,128)(2,1)}, u32[]{:S(2)}) copy-start(bf16[256,768]{1,0:T(8,128)(2,1)} %get-tuple-element.41.refs_0_) | copy-start | bytes 1179652
  28.0 18.7 %all-to-all-start = ((bf16[4,64,768]{2,1,0:T(8,128)(2,1)}), bf16[4,64,768]{2,1,0:T(8,128)(2,1)S(1)}, u32[]{:S(2)}, u32[]{:S(2)}) async-start(bf16[4,64,768]{2,1,0:T(8,128)(2,1)} %bitcast.4), calls=%async_computation | async-start | bytes 786432 | tf_op jit(solution)/shard_map/all_to_all | solution.py:354
  31.6 15.6 %copy-start.1 = (bf16[256,384]{1,0:T(8,128)(2,1)S(1)}, bf16[256,384]{1,0:T(8,128)(2,1)}, u32[]{:S(2)}) copy-start(bf16[256,384]{1,0:T(8,128)(2,1)} %get-tuple-element.34.q_ref) | copy-start | bytes 589828
  32.6 26.4 %collective-permute-start.10 = (bf16[256,768]{1,0:T(8,128)(2,1)}, bf16[256,768]{1,0:T(8,128)(2,1)S(1)}, u32[]{:S(2)}, u32[]{:S(2)}) collective-permute-start(bf16[256,768]{1,0:T(8,128)(2,1)} %get-tuple-element.56), channel_id=1, source_target_pairs={{16,0},{20,4},{24,8},{28,12},{32,16},{36,20},{40,24},{44,28},{48,3... | collective-permute-start | bytes 1179656 | tf_op jit(solution)/shard_map/ppermute | solution.py:54
  43.7 16.5 %collective-permute-start.12 = (bf16[256,768]{1,0:T(8,128)(2,1)}, bf16[256,768]{1,0:T(8,128)(2,1)S(1)}, u32[]{:S(2)}, u32[]{:S(2)}) collective-permute-start(bf16[256,768]{1,0:T(8,128)(2,1)} %get-tuple-element.55), channel_id=1, source_target_pairs={{48,0},{52,4},{56,8},{60,12},{0,16},{4,20},{8,24},{12,28},{16,32},... | collective-permute-start | bytes 1179656 | tf_op jit(solution)/shard_map/ppermute | solution.py:54
  43.7 0.8 copy-start.2
  44.4 15.7 %collective-permute-start.14 = (bf16[256,768]{1,0:T(8,128)(2,1)S(1)}, bf16[256,768]{1,0:T(8,128)(2,1)S(1)}, u32[]{:S(2)}, u32[]{:S(2)}) collective-permute-start(bf16[256,768]{1,0:T(8,128)(2,1)S(1)} %copy-done), channel_id=1, source_target_pairs={{128,0},{132,4},{136,8},{140,12},{144,16},{148,20},{152,24},{156,2... | collective-permute-start | bytes 1179656 | tf_op jit(solution)/shard_map/ppermute | solution.py:54
  46.7 18.2 %collective-permute-start.13 = (bf16[256,768]{1,0:T(8,128)(2,1)S(1)}, bf16[256,768]{1,0:T(8,128)(2,1)S(1)}, u32[]{:S(2)}, u32[]{:S(2)}) collective-permute-start(bf16[256,768]{1,0:T(8,128)(2,1)S(1)} %bitcast.2), channel_id=1, source_target_pairs={{192,0},{196,4},{200,8},{204,12},{208,16},{212,20},{216,24},{220,2... | collective-permute-start | bytes 1179656 | tf_op jit(solution)/shard_map/ppermute | solution.py:54
  47.4 1.0 %copy-start.3 = (bf16[256,768]{1,0:T(8,128)(2,1)S(1)}, bf16[256,768]{1,0:T(8,128)(2,1)}, u32[]{:S(2)}) copy-start(bf16[256,768]{1,0:T(8,128)(2,1)} %copy-done.2) | copy-start | bytes 1179652
  48.4 18.0 %copy-start.4 = (bf16[256,768]{1,0:T(8,128)(2,1)S(1)}, bf16[256,768]{1,0:T(8,128)(2,1)}, u32[]{:S(2)}) copy-start(bf16[256,768]{1,0:T(8,128)(2,1)} %copy-done.2) | copy-start | bytes 1179652
  64.9 2.3 %collective-permute-start.15 = (bf16[256,768]{1,0:T(8,128)(2,1)S(1)}, bf16[256,768]{1,0:T(8,128)(2,1)S(1)}, u32[]{:S(2)}, u32[]{:S(2)}) collective-permute-start(bf16[256,768]{1,0:T(8,128)(2,1)S(1)} %collective-permute-done.10.refs_5_), channel_id=1, source_target_pairs={{4,0},{0,4},{12,8},{8,12},{20,16},{16,20},{28,24},{24,28},{36,32},... | collective-permute-start | bytes 1179656 | tf_op jit(solution)/shard_map/ppermute | solution.py:54
  65.9 1.9 %collective-permute-start.4 = (bf16[256,768]{1,0:T(8,128)(2,1)S(1)}, bf16[256,768]{1,0:T(8,128)(2,1)S(1)}, u32[]{:S(2)}, u32[]{:S(2)}) collective-permute-start(bf16[256,768]{1,0:T(8,128)(2,1)S(1)} %copy-done), channel_id=1, source_target_pairs={{4,0},{0,4},{12,8},{8,12},{20,16},{16,20},{28,24},{24,28},{36,32},... | collective-permute-start | bytes 1179656 | tf_op jit(solution)/shard_map/ppermute | solution.py:54
  65.9 2.5 %collective-permute-start.7 = (bf16[256,768]{1,0:T(8,128)(2,1)S(1)}, bf16[256,768]{1,0:T(8,128)(2,1)S(1)}, u32[]{:S(2)}, u32[]{:S(2)}) collective-permute-start(bf16[256,768]{1,0:T(8,128)(2,1)S(1)} %collective-permute-done.5.refs_4_), channel_id=1, source_target_pairs={{4,0},{0,4},{12,8},{8,12},{20,16},{16,20},{28,24},{24,28},{36,32},... | collective-permute-start | bytes 1179656 | tf_op jit(solution)/shard_map/ppermute | solution.py:54
  66.4 2.5 %collective-permute-start.8 = (bf16[256,768]{1,0:T(8,128)(2,1)S(1)}, bf16[256,768]{1,0:T(8,128)(2,1)S(1)}, u32[]{:S(2)}, u32[]{:S(2)}) collective-permute-start(bf16[256,768]{1,0:T(8,128)(2,1)S(1)} %copy-done.4), channel_id=1, source_target_pairs={{4,0},{0,4},{12,8},{8,12},{20,16},{16,20},{28,24},{24,28},{36,32},... | collective-permute-start | bytes 1179656 | tf_op jit(solution)/shard_map/ppermute | solution.py:54
  67.2 2.2 %collective-permute-start.16 = (bf16[256,768]{1,0:T(8,128)(2,1)S(1)}, bf16[256,768]{1,0:T(8,128)(2,1)S(1)}, u32[]{:S(2)}, u32[]{:S(2)}) collective-permute-start(bf16[256,768]{1,0:T(8,128)(2,1)S(1)} %collective-permute-done.12.refs_6_), channel_id=1, source_target_pairs={{4,0},{0,4},{12,8},{8,12},{20,16},{16,20},{28,24},{24,28},{36,32},... | collective-permute-start | bytes 1179656 | tf_op jit(solution)/shard_map/ppermute | solution.py:54
  74.1 4.9 %collective-permute-start.17 = (bf16[64,384]{1,0:T(8,128)(2,1)S(1)}, bf16[64,384]{1,0:T(8,128)(2,1)S(1)}, u32[]{:S(2)}, u32[]{:S(2)}) collective-permute-start(bf16[64,384]{1,0:T(8,128)(2,1)S(1)} %get-tuple-element.52), channel_id=1, source_target_pairs={{3,0},{0,1},{1,2},{2,3},{7,4},{4,5},{5,6},{6,7},{11,8},{8,9},{9,10... | collective-permute-start | bytes 147464 | tf_op jit(solution)/shard_map/ppermute | solution.py:147
  75.5 4.7 %collective-permute-start.18 = (bf16[64,384]{1,0:T(8,128)(2,1)S(1)}, bf16[64,384]{1,0:T(8,128)(2,1)S(1)}, u32[]{:S(2)}, u32[]{:S(2)}) collective-permute-start(bf16[64,384]{1,0:T(8,128)(2,1)S(1)} %get-tuple-element.53), channel_id=1, source_target_pairs={{2,0},{3,1},{0,2},{1,3},{6,4},{7,5},{4,6},{5,7},{10,8},{11,9},{8,1... | collective-permute-start | bytes 147464 | tf_op jit(solution)/shard_map/ppermute | solution.py:147
  77.9 3.2 %collective-permute-start.19 = (bf16[64,384]{1,0:T(8,128)(2,1)S(1)}, bf16[64,384]{1,0:T(8,128)(2,1)S(1)}, u32[]{:S(2)}, u32[]{:S(2)}) collective-permute-start(bf16[64,384]{1,0:T(8,128)(2,1)S(1)} %get-tuple-element.54), channel_id=1, source_target_pairs={{1,0},{2,1},{3,2},{0,3},{5,4},{6,5},{7,6},{4,7},{9,8},{10,9},{11,1... | collective-permute-start | bytes 147464 | tf_op jit(solution)/shard_map/ppermute | solution.py:147
  79.0 2.1 %copy-start.11 = (bf16[64,384]{1,0:T(8,128)(2,1)}, bf16[64,384]{1,0:T(8,128)(2,1)S(1)}, u32[]{:S(2)}) copy-start(bf16[64,384]{1,0:T(8,128)(2,1)S(1)} %collective-permute-done.17.p1) | copy-start | bytes 147460
  80.2 0.9 %copy-start.12 = (bf16[64,384]{1,0:T(8,128)(2,1)}, bf16[64,384]{1,0:T(8,128)(2,1)S(1)}, u32[]{:S(2)}) copy-start(bf16[64,384]{1,0:T(8,128)(2,1)S(1)} %collective-permute-done.18.p2) | copy-start | bytes 147460
  (3 other events, 1.9 us)
